TPU v7x, 32 devices: a whole 2x2x4 slice. The times are simulated.
32 devices in a mesh: group: 2 (over x), tensor: 8 (over z, y), dp: 2 (over core).
Axes of the slice: x: 2, y: 2, z: 4, core: 2. Of those that a mesh axis runs over, the one named last changes fastest.
Arguments:
- features: bfloat16 [512, 8192], P(('group', 'dp'), 'tensor'), parts along dimension 0, may hold values from -64 to 64
- cotangent: bfloat16 [512, 8192], P(('group', 'dp'), 'tensor'), parts along dimension 0, may hold values from -64 to 64
- token_tenant: int32 [512], P(('group', 'dp')), parts along dimension 0, may hold values from 0 to 15
- owner_device: int32 [32], P('group'), parts along dimension 0, may hold values from 0 to 15, each once
- frozen_weight: bfloat16 [8192, 8192], P('tensor'), may hold values from -0.09375 to 0.09375
- adapter_down: bfloat16 [32, 16, 8192], P('group', None, 'tensor'), parts along dimension 0, may hold values from -0.0625 to 0.0625
- adapter_up: bfloat16 [32, 16, 8192], P('group', None, 'tensor'), parts along dimension 0, may hold values from -0.29882812 to 0.29882812
- momentum_down: float32 [32, 16, 8192], P(('group', 'tensor', 'dp')), parts along dimension 0, may hold values from -12 to 12
- momentum_up: float32 [32, 16, 8192], P(('group', 'tensor', 'dp')), parts along dimension 0, may hold values from -3 to 3
- variance_down: float32 [32, 16, 8192], P(('group', 'tensor', 'dp')), parts along dimension 0, may hold values from 0.3 to 3
- variance_up: float32 [32, 16, 8192], P(('group', 'tensor', 'dp')), parts along dimension 0, may hold values from 0.02 to 0.2
Outputs:
- projected: bfloat16 [512, 8192], P(('group', 'dp'), 'tensor'), parts along dimension 0
- updated_down: bfloat16 [32, 16, 8192], P('group', None, 'tensor'), parts along dimension 0
- updated_up: bfloat16 [32, 16, 8192], P('group', None, 'tensor'), parts along dimension 0
- mean_down: float32 [32, 16, 8192], P(('group', 'tensor', 'dp')), parts along dimension 0
- mean_up: float32 [32, 16, 8192], P(('group', 'tensor', 'dp')), parts along dimension 0
- power_down: float32 [32, 16, 8192], P(('group', 'tensor', 'dp')), parts along dimension 0
- power_up: float32 [32, 16, 8192], P(('group', 'tensor', 'dp')), parts along dimension 0
There are 2 independent parts, one for each index of `group`. A program takes and returns all parts, laid end to end along the dimension named above; an argument that names none is the same for every part. Nothing has to cross between parts.
Inputs may be any that keep to these rules, and one draw needn't show every extreme that they name: Tenant t belongs to the device whose index along tensor+dp (dp fastest) is owner_device[t]; every index appears once.
All inputs are finite; a program needn't handle non-finite values.
Results may differ from a plain program's by a relative error of at most 0.0014.
The roundings to bfloat16 on the way count: a program that leaves them out, or rounds other values in their place, can miss the bound.
Values sent between devices are 32-bit elements; how exact they have to be, the bound alone decides.
No kernel may reach another device: no remote copies, remote signals or barrier semaphores. Data moves between devices by JAX's collectives and lax.ppermute only.
A program may use at most 128 MiB of HBM per device.

v0:
```python
import jax
import jax.numpy as jnp
from jax import lax
from jax.sharding import PartitionSpec as P

adapter_scale = 2.0
clip_norm = 12000.0
learn_rate = 0.004
beta_one = 0.9
beta_two = 0.999
adam_eps = 1e-08
correct_one = 1.0 - beta_one**20
correct_two = 1.0 - beta_two**20


def tenant_mask(token_tenant, tenants, lowrank):
    columns = lax.broadcasted_iota(jnp.int32, (1, tenants * lowrank), 1) // lowrank
    return token_tenant[:, None] == columns


def rank_fold(tenants, lowrank):
    row_index = lax.broadcasted_iota(jnp.int32, (tenants * lowrank, lowrank), 0) % lowrank
    col_index = lax.broadcasted_iota(jnp.int32, (tenants * lowrank, lowrank), 1)
    return (row_index == col_index).astype(jnp.float32)


def select_rank(scores, token_mask, folding):
    picked = jnp.where(token_mask, scores, jnp.zeros_like(scores))
    return jnp.dot(
        picked, folding, precision=lax.Precision.HIGHEST, preferred_element_type=jnp.float32
    )


def spread_rank(values, token_mask, tenants):
    scaled = (adapter_scale * values).astype(jnp.bfloat16)
    tiled_rank = jnp.tile(scaled, (1, tenants))
    return jnp.where(token_mask, tiled_rank, jnp.zeros_like(tiled_rank))


def owner_order(owner_device):
    total = owner_device.shape[0]
    slot_index = lax.broadcasted_iota(jnp.int32, (total, total), 0)
    tenant_index = lax.broadcasted_iota(jnp.int32, (total, total), 1)
    return jnp.sum(jnp.where(owner_device[None, :] == slot_index, tenant_index, 0), axis=1)


def adam_step(gradient, factor, moment, square):
    clipped = gradient * factor
    moment_next = beta_one * moment + (1.0 - beta_one) * clipped
    square_next = beta_two * square + (1.0 - beta_two) * clipped * clipped
    change = (
        learn_rate * (moment_next / correct_one) / (jnp.sqrt(square_next / correct_two) + adam_eps)
    )
    return (moment_next, square_next, change)


def frozen_blocks(features, frozen_weight, width_shard, blocks):
    columns = frozen_weight
    columns = columns.reshape(frozen_weight.shape[0], blocks, width_shard)
    return jnp.einsum("ti,ibc->btc", features, columns, preferred_element_type=jnp.float32)


def on_device(
    features,
    cotangent,
    token_tenant,
    owner_device,
    frozen_weight,
    adapter_down,
    adapter_up,
    momentum_down,
    momentum_up,
    variance_down,
    variance_up,
):
    tokens = features.shape[0]
    tenants, lowrank, width_shard = adapter_down.shape
    parts_tensor = lax.axis_size("tensor")
    parts_dp = lax.axis_size("dp")
    token_mask = tenant_mask(token_tenant, tenants, lowrank)
    folding = rank_fold(tenants, lowrank)
    down_flat = adapter_down.reshape(tenants * lowrank, width_shard)
    up_flattened = adapter_up.reshape(tenants * lowrank, width_shard)
    contract = (((1,), (1,)), ((), ()))
    down_part = select_rank(
        lax.dot_general(features, down_flat, contract, preferred_element_type=jnp.float32),
        token_mask,
        folding,
    )
    up_part = select_rank(
        lax.dot_general(cotangent, up_flattened, contract, preferred_element_type=jnp.float32),
        token_mask,
        folding,
    )
    blocks = lax.axis_size("tensor") * tokens // tokens
    result = frozen_blocks(features, frozen_weight, width_shard, blocks)
    frozen_result = lax.psum_scatter(
        result.reshape(blocks * tokens, width_shard), "tensor", scatter_dimension=0, tiled=True
    )
    down_sum, up_sum = lax.psum((down_part, up_part), "tensor")
    down_scattered = spread_rank(down_sum, token_mask, tenants)
    up_scattered = spread_rank(up_sum, token_mask, tenants)
    adapter_result = jnp.dot(down_scattered, up_flattened, preferred_element_type=jnp.float32)
    projected = (frozen_result + adapter_result).astype(jnp.bfloat16)
    outer_product = (((0,), (0,)), ((), ()))
    down_gradient = lax.dot_general(
        up_scattered, features, outer_product, preferred_element_type=jnp.float32
    )
    up_gradient = lax.dot_general(
        down_scattered, cotangent, outer_product, preferred_element_type=jnp.float32
    )
    down_gradient = down_gradient.reshape(tenants, lowrank, width_shard)
    up_gradient = up_gradient.reshape(tenants, lowrank, width_shard)
    slot_tenant = owner_order(owner_device)
    half_index = lax.broadcasted_iota(jnp.int32, (tenants,), 0)
    slot_index = half_index % parts_tensor * parts_dp + half_index // parts_tensor
    half_tenant = jnp.take(slot_tenant, slot_index, axis=0)
    down_halves = jnp.take(down_gradient, half_tenant, axis=0)
    up_halves = jnp.take(up_gradient, half_tenant, axis=0)
    summed = (
        lax.psum_scatter(down_halves, "dp", scatter_dimension=0, tiled=True),
        lax.psum_scatter(up_halves, "dp", scatter_dimension=0, tiled=True),
    )
    own_down, own_up = (
        lax.all_to_all(summed[0], "tensor", split_axis=0, concat_axis=2, tiled=True),
        lax.all_to_all(summed[1], "tensor", split_axis=0, concat_axis=2, tiled=True),
    )
    squares = jnp.sum(own_down * own_down) + jnp.sum(own_up * own_up)
    factor = clip_norm / jnp.maximum(jnp.sqrt(squares), clip_norm)
    mean_down, power_down, change_down = adam_step(own_down, factor, momentum_down, variance_down)
    mean_up, power_up, change_up = adam_step(own_up, factor, momentum_up, variance_up)
    pieces = (
        lax.all_to_all(change_down, ("tensor", "dp"), split_axis=2, concat_axis=0, tiled=True),
        lax.all_to_all(change_up, ("tensor", "dp"), split_axis=2, concat_axis=0, tiled=True),
    )
    joined = (
        lax.all_gather(pieces[0], "dp", axis=2, tiled=True),
        lax.all_gather(pieces[1], "dp", axis=2, tiled=True),
    )
    back_down = jnp.take(joined[0], owner_device, axis=0)
    back_up = jnp.take(joined[1], owner_device, axis=0)
    updated_down = (adapter_down.astype(jnp.float32) - back_down).astype(jnp.bfloat16)
    updated_up = (adapter_up.astype(jnp.float32) - back_up).astype(jnp.bfloat16)
    return (projected, updated_down, updated_up, mean_down, mean_up, power_down, power_up)


def solution(mesh):
    in_specs = (
        P(("group", "dp"), "tensor"),
        P(("group", "dp"), "tensor"),
        P(("group", "dp")),
        P("group"),
        P("tensor", None),
        P("group", None, "tensor"),
        P("group", None, "tensor"),
        P(("group", "tensor", "dp"), None, None),
        P(("group", "tensor", "dp"), None, None),
        P(("group", "tensor", "dp"), None, None),
        P(("group", "tensor", "dp"), None, None),
    )
    out_specs = (
        P(("group", "dp"), "tensor"),
        P("group", None, "tensor"),
        P("group", None, "tensor"),
        P(("group", "tensor", "dp"), None, None),
        P(("group", "tensor", "dp"), None, None),
        P(("group", "tensor", "dp"), None, None),
        P(("group", "tensor", "dp"), None, None),
    )
    return jax.shard_map(
        on_device, mesh=mesh, in_specs=in_specs, out_specs=out_specs, check_vma=False
    )
```

profile of v0, /device:TPU:0, one launch (start us, length us, event | category | flops | bytes accessed | tf_op | source)
XLA Modules:
  0.0 376.7 jit_solution(10851005240872450794)
XLA Ops:
  11.8 38.8 %all-reduce = (f32[128,16]{0,1:T(8,128)S(1)}, f32[128,16]{0,1:T(8,128)S(1)}) all-reduce(f32[128,16]{0,1:T(8,128)S(1)} %fusion.15, f32[128,16]{0,1:T(8,128)S(1)} %fusion.14), channel_id=1, replica_groups=mesh['group'=2,'tensor'=8,'dp'=2] {'tensor'}, use_global_device_ids=true, to_apply=%region_1.2 | all-reduce | flops 4096 | bytes 32768 | tf_op jit(solution)/shard_map/psum | solution.py:100
  56.9 5.2 %reduce-scatter.8.cloned.1.call-done = f32[8,16,1024]{2,1,0:T(8,128)} async-done(((f32[16,16,1024]{2,1,0:T(8,128)}), f32[8,16,1024]{2,1,0:T(8,128)}) %reduce-scatter.8.cloned.1.call-update) | async-done | bytes 524304 | tf_op jit(solution)/shard_map/reduce_scatter | solution.py:122
  62.1 5.8 %all-to-all-start.1 = ((f32[8,16,1024]{2,1,0:T(8,128)}), f32[8,16,1024]{2,1,0:T(8,128)S(1)}, u32[]{:S(2)}, u32[]{:S(2)}) async-start(f32[8,16,1024]{2,1,0:T(8,128)} %reduce-scatter.8.cloned.1.call-done), calls=%async_computation.4 | async-start | bytes 1048576 | tf_op jit(solution)/shard_map/all_to_all | solution.py:126
  67.9 6.2 %reduce-scatter.6.cloned.1.call-done = f32[8,16,1024]{2,1,0:T(8,128)} async-done(((f32[16,16,1024]{2,1,0:T(8,128)}), f32[8,16,1024]{2,1,0:T(8,128)}) %reduce-scatter.6.cloned.1.call-update) | async-done | bytes 524304 | tf_op jit(solution)/shard_map/reduce_scatter | solution.py:121
  74.1 8.7 %all-to-all-done.1 = f32[8,16,1024]{2,1,0:T(8,128)S(1)} async-done(((f32[8,16,1024]{2,1,0:T(8,128)}), f32[8,16,1024]{2,1,0:T(8,128)S(1)}, u32[]{:S(2)}, u32[]{:S(2)}) %all-to-all-start.1) | async-done | bytes 524320 | tf_op jit(solution)/shard_map/all_to_all | solution.py:126
  82.9 3.6 all-to-all-start
  87.2 13.9 %all-to-all-done = f32[8,16,1024]{2,1,0:T(8,128)S(1)} async-done(((f32[8,16,1024]{2,1,0:T(8,128)}), f32[8,16,1024]{2,1,0:T(8,128)S(1)}, u32[]{:S(2)}, u32[]{:S(2)}) %all-to-all-start) | async-done | bytes 524320 | tf_op jit(solution)/shard_map/all_to_all | solution.py:125
  104.7 6.4 %copy.46 = f32[1,16,8192]{1,0,2:T(1,128)} copy(f32[1,16,8192]{2,1,0:T(8,128)S(1)} %get-tuple-element.13) | data formatting | bytes 1048576 | tf_op jit(solution)/shard_map/div | solution.py:52
  111.6 38.4 %reduce.8 = f32[8192,16]{1,0:T(8,128)} reduce(f32[8192,1,16]{2,1,0:T(1,128)} %bitcast.66, f32[]{:T(128)} %broadcast.462), dimensions={1}, to_apply=%bitcast.51.reduce_sub_computation | reduce | bytes 1048580
  150.0 4.2 %reshape.313 = f32[16,1,8192]{2,1,0:T(1,128)} reshape(f32[8192,16]{1,0:T(8,128)} %reduce.8) | data formatting | bytes 1048576
  154.2 3.7 all-to-all-start.2
  158.3 14.1 %all-to-all-done.2 = f32[16,1,8192]{2,1,0:T(1,128)S(1)} async-done(((f32[16,1,8192]{2,1,0:T(1,128)}), f32[16,1,8192]{2,1,0:T(1,128)S(1)}, u32[]{:S(2)}, u32[]{:S(2)}) %all-to-all-start.2) | async-done | bytes 524320 | tf_op jit(solution)/shard_map/all_to_all | solution.py:133
  174.4 9.3 %reshape.314 = f32[8192,1,16]{2,1,0:T(1,128)} reshape(f32[16,8192]{1,0:T(8,128)S(1)} %reduce.9) | data formatting | bytes 1048576
  183.6 3.5 copy.48
  188.5 6.4 %copy.50 = f32[1,16,8192]{1,0,2:T(1,128)} copy(f32[1,16,8192]{2,1,0:T(8,128)S(1)} %get-tuple-element.10) | data formatting | bytes 1048576 | tf_op jit(solution)/shard_map/div | solution.py:52
  194.9 38.4 %reduce.6 = f32[8192,16]{1,0:T(8,128)} reduce(f32[8192,1,16]{2,1,0:T(1,128)} %bitcast.67, f32[]{:T(128)} %broadcast.462), dimensions={1}, to_apply=%bitcast.53.reduce_sub_computation | reduce | bytes 1048580
  233.3 3.5 reshape.315
  236.8 18.5 %all_to_all.54 = f32[16,1,8192]{2,1,0:T(1,128)S(1)} all-to-all(f32[16,1,8192]{2,1,0:T(1,128)S(1)} %reshape.315), channel_id=1, replica_groups=mesh['group'=2,'tensor'=8,'dp'=2] {'tensor','dp'}, dimensions={0} | all-to-all | bytes 1048576 | tf_op jit(solution)/shard_map/all_to_all | solution.py:134
  257.2 9.3 %reshape.316 = f32[8192,1,16]{2,1,0:T(1,128)} reshape(f32[16,8192]{1,0:T(8,128)S(1)} %reduce.7) | data formatting | bytes 1048576
  266.5 3.5 copy.52
  270.1 10.2 %fusion = f32[8,1024,128]{1,2,0:T(8,128)} fusion(bf16[128,8,8,1024]{3,2,1,0:T(8,128)(2,1)} %bitcast.81, bf16[128,1024]{1,0:T(8,128)(2,1)S(1)} %copy-done), kind=kOutput, calls=%fused_computation.5 | convolution fusion | flops 2147483648 | bytes 21233664 | tf_op jit(solution)/shard_map/ti,ibc->btc/dot_general | solution.py:60
  280.4 1.9 gather_fusion.3
  285.6 81.9 %reduce-scatter.4.cloned.1.call-done = f32[128,1024]{1,0:T(8,128)} async-done(((f32[1024,1024]{1,0:T(8,128)}), f32[128,1024]{1,0:T(8,128)}) %reduce-scatter.4.cloned.1.call-update) | async-done | bytes 524304 | tf_op jit(solution)/shard_map/reduce_scatter | solution.py:97
  367.5 2.1 fusion.4
  (76 shorter events, 22.1 us)
Async XLA Ops:
  8.0 1.6 copy-start
  8.0 45.0 %copy-start.3 = (bf16[128,1024]{1,0:T(8,128)(2,1)S(1)}, bf16[128,1024]{1,0:T(8,128)(2,1)}, u32[]{:S(2)}) copy-start(bf16[128,1024]{1,0:T(8,128)(2,1)} %param.14) | copy-start | bytes 786436
  8.0 44.0 %copy-start.9 = (s32[16]{0:T(128)S(1)}, s32[16]{0:T(128)}, u32[]{:S(2)}) copy-start(s32[16]{0:T(128)} %param.16) | copy-start | bytes 196
  8.0 54.1 %reduce-scatter.8.cloned.1.call-start = ((), (), s32[]{:S(2)}) async-start(), calls=%async_computation.9 | async-start | bytes 1572864 | tf_op jit(solution)/shard_map/reduce_scatter | solution.py:122
  56.1 47.2 %copy-start.4 = (f32[1,16,8192]{2,1,0:T(8,128)S(1)}, f32[1,16,8192]{2,1,0:T(8,128)}, u32[]{:S(2)}) copy-start(f32[1,16,8192]{2,1,0:T(8,128)} %param.20) | copy-start | bytes 1572868
  56.2 47.2 %copy-start.5 = (f32[1,16,8192]{2,1,0:T(8,128)S(1)}, f32[1,16,8192]{2,1,0:T(8,128)}, u32[]{:S(2)}) copy-start(f32[1,16,8192]{2,1,0:T(8,128)} %param.22) | copy-start | bytes 1572868
  56.2 17.9 %reduce-scatter.6.cloned.1.call-start = ((), (), s32[]{:S(2)}) async-start(), calls=%async_computation.8 | async-start | bytes 1572864 | tf_op jit(solution)/shard_map/reduce_scatter | solution.py:121
  62.1 20.7 %all-to-all-start.1 = ((f32[8,16,1024]{2,1,0:T(8,128)}), f32[8,16,1024]{2,1,0:T(8,128)S(1)}, u32[]{:S(2)}, u32[]{:S(2)}) async-start(f32[8,16,1024]{2,1,0:T(8,128)} %reduce-scatter.8.cloned.1.call-done), calls=%async_computation.4 | async-start | bytes 1048576 | tf_op jit(solution)/shard_map/all_to_all | solution.py:126
  82.9 18.3 %all-to-all-start = ((f32[8,16,1024]{2,1,0:T(8,128)}), f32[8,16,1024]{2,1,0:T(8,128)S(1)}, u32[]{:S(2)}, u32[]{:S(2)}) async-start(f32[8,16,1024]{2,1,0:T(8,128)} %reduce-scatter.6.cloned.1.call-done), calls=%async_computation.2 | async-start | bytes 1048576 | tf_op jit(solution)/shard_map/all_to_all | solution.py:125
  154.2 18.2 %all-to-all-start.2 = ((f32[16,1,8192]{2,1,0:T(1,128)}), f32[16,1,8192]{2,1,0:T(1,128)S(1)}, u32[]{:S(2)}, u32[]{:S(2)}) async-start(f32[16,1,8192]{2,1,0:T(1,128)} %reshape.313), calls=%async_computation.5 | async-start | bytes 1048576 | tf_op jit(solution)/shard_map/all_to_all | solution.py:133
  158.0 122.4 %all-gather.5.cloned.1.call-start = ((), (), s32[]{:S(2)}) async-start(), calls=%async_computation.10 | async-start | bytes 1572864 | tf_op jit(solution)/shard_map/all_gather | solution.py:137
  174.3 12.9 %copy-start.6 = (f32[1,16,8192]{2,1,0:T(8,128)S(1)}, f32[1,16,8192]{2,1,0:T(8,128)}, u32[]{:S(2)}) copy-start(f32[1,16,8192]{2,1,0:T(8,128)} %param.21) | copy-start | bytes 1572868
  174.4 12.9 %copy-start.7 = (f32[1,16,8192]{2,1,0:T(8,128)S(1)}, f32[1,16,8192]{2,1,0:T(8,128)}, u32[]{:S(2)}) copy-start(f32[1,16,8192]{2,1,0:T(8,128)} %param.23) | copy-start | bytes 1572868
  187.2 95.1 %all-gather.7.cloned.1.call-start = ((), (), s32[]{:S(2)}) async-start(), calls=%async_computation.11 | async-start | bytes 1572864 | tf_op jit(solution)/shard_map/all_gather | solution.py:138
  270.0 97.5 %reduce-scatter.4.cloned.1.call-start = ((), (), s32[]{:S(2)}) async-start(), calls=%async_computation.7 | async-start | bytes 4718592 | tf_op jit(solution)/shard_map/reduce_scatter | solution.py:97
  280.2 3.9 %copy-start.1 = (bf16[16,16,1024]{2,1,0:T(8,128)(2,1)S(1)}, bf16[16,16,1024]{2,1,0:T(8,128)(2,1)}, u32[]{:S(2)}) copy-start(bf16[16,16,1024]{2,1,0:T(8,128)(2,1)} %param.19) | copy-start | bytes 1572868
  280.2 3.9 %copy-start.2 = (bf16[16,16,1024]{2,1,0:T(8,128)(2,1)S(1)}, bf16[16,16,1024]{2,1,0:T(8,128)(2,1)}, u32[]{:S(2)}) copy-start(bf16[16,16,1024]{2,1,0:T(8,128)(2,1)} %param.18) | copy-start | bytes 1572868
  280.3 87.2 %copy-start.8 = (s32[128]{0:T(128)S(1)}, s32[128]{0:T(128)}, u32[]{:S(2)}) copy-start(s32[128]{0:T(128)} %param.15) | copy-start | bytes 1540
Sparse Core Ops, SparseCore 0:
  56.3 5.7 reduce-scatter.7
  64.4 9.6 reduce-scatter.5
  187.3 8.4 all-gather.4
  270.1 8.4 all-gather.6
Sparse Core Ops, SparseCore 1:
  280.3 87.1 reduce-scatter.3
where the time goes:
time: 378 us; the launch traced here: 377 us
  waiting for transfers between devices  131 us (35%)
  other arithmetic  88.7 us (23%)
  blocking collectives  57.3 us (15%)
  local copies, waits for them, and re-layouts  52.8 us (14%)
  between operations  17 us (4%)
  matrix products  16.4 us (4%)
  starting transfers between devices  13.5 us (4%)
    reduce_scatter x1, waiting for transfers between devices, on_device(): lax.psum_scatter(result.reshape(blocks * tokens, width_shard), 'tensor',...  81.9 us
    unnamed x4, other arithmetic  76.9 us
    psum x1, blocking collectives, on_device(): down_sum, up_sum = lax.psum((down_part, up_part), 'tensor')  38.8 us
    unnamed x25, local copies, waits for them, and re-layouts  26.8 us
    all_to_all x1, blocking collectives, on_device(): lax.all_to_all(change_up, ('tensor', 'dp'), split_axis=2, concat_axis=0,...  18.5 us
    all_to_all x1, waiting for transfers between devices, on_device(): lax.all_to_all(change_down, ('tensor', 'dp'), split_axis=2, concat_axis=0...  14.1 us
    all_to_all x1, waiting for transfers between devices, on_device(): lax.all_to_all(summed[0], 'tensor', split_axis=0, concat_axis=2, tiled=True)  13.9 us
    div x2, local copies, waits for them, and re-layouts, adam_step(): learn_rate * (moment_next / correct_one)  12.8 us
  transfers between devices with their start and end apart: 8, of which 6 were waited for; matrix products, arithmetic and copies ran while one was open for 21% of the time, Pallas kernels for 0%

commit v1 on v0

v1 whole, which is shorter than its diff:
```python
import functools

import jax
import jax.numpy as jnp
from jax import lax
from jax.experimental import pallas as pl
from jax.experimental.pallas import tpu as pltpu
from jax.sharding import PartitionSpec as P

adapter_scale = 2.0
clip_norm = 12000.0
learn_rate = 0.004
beta_one = 0.9
beta_two = 0.999
adam_eps = 1e-08
correct_one = 1.0 - beta_one**20
correct_two = 1.0 - beta_two**20

f32, bf16 = jnp.float32, jnp.bfloat16
vmem = pl.BlockSpec(memory_space=pltpu.VMEM)
smem = pl.BlockSpec(memory_space=pltpu.SMEM)
NT = (((1,), (1,)), ((), ()))
NN = (((1,), (0,)), ((), ()))
TN = (((0,), (0,)), ((), ()))


def params(mib=48):
    return pltpu.CompilerParams(vmem_limit_bytes=mib << 20)


def dot(a, b, dims):
    return lax.dot_general(a, b, dims, preferred_element_type=f32)


def rank_kernel(tenants, lowrank, tenant_ref, feat_ref, cot_ref, down_ref, up_ref, out_ref):
    tokens = feat_ref.shape[0]
    row = lax.broadcasted_iota(jnp.int32, (tenants, lowrank, tokens), 0)
    mine = row == tenant_ref[...].reshape(1, 1, tokens)
    for half, (x_ref, a_ref) in enumerate(((feat_ref, down_ref), (cot_ref, up_ref))):
        scores = dot(a_ref[...], x_ref[...], NT).reshape(tenants, lowrank, tokens)
        out_ref[half * lowrank : (half + 1) * lowrank, :] = jnp.sum(
            jnp.where(mine, scores, 0.0), axis=0
        )


def frozen_kernel(feat_ref, weight_ref, out_ref):
    out_ref[0] = dot(feat_ref[...], weight_ref[...], NN)


def frozen_partials(features, weight, parts):
    tokens, depth = features.shape
    width = weight.shape[1] // parts
    return pl.pallas_call(
        frozen_kernel,
        grid=(parts,),
        in_specs=[
            pl.BlockSpec((tokens, depth), lambda j: (0, 0)),
            pl.BlockSpec((depth, width), lambda j: (0, j)),
        ],
        out_specs=pl.BlockSpec((1, tokens, width), lambda j: (j, 0, 0)),
        out_shape=jax.ShapeDtypeStruct((parts, tokens, width), f32),
        compiler_params=params(),
        cost_estimate=pl.CostEstimate(
            flops=2 * tokens * depth * width * parts,
            bytes_accessed=2 * depth * width * parts + 4 * tokens * width * parts,
            transcendentals=0,
        ),
        name="frozen_partials",
    )(features, weight)


def grad_kernel(
    parts, parts_dp, lowrank, tenants, place_ref, owner_ref, sum_own, sum_other, ten_own, ten_other,
    feat_own, feat_other, cot_own, cot_other, *outs
):
    me, core = place_ref[0], place_ref[1]
    low = jnp.concatenate([sum_own[...], sum_other[...]], axis=1) * adapter_scale
    tenant = jnp.concatenate([ten_own[...], ten_other[...]], axis=1)
    slot = jnp.zeros_like(tenant)
    for t in range(tenants):
        slot = jnp.where(tenant == t, owner_ref[t], slot)
    down, up = low[:lowrank], low[lowrank:]
    picks = [slot == (me ^ k) * parts_dp + core for k in range(parts)]
    for half, (rank, own, other) in enumerate(
        ((up, feat_own, feat_other), (down, cot_own, cot_other))
    ):
        lhs = jnp.concatenate([jnp.where(p, rank, 0.0) for p in picks], axis=0).astype(bf16)
        rhs = jnp.concatenate([own[...], other[...].astype(bf16)], axis=0)
        grad = dot(lhs, rhs, NN)
        for k in range(parts):
            outs[k][half * lowrank : (half + 1) * lowrank, :] = grad[
                k * lowrank : (k + 1) * lowrank
            ]


def adapter_kernel(tenants, lowrank, tenant_ref, sum_ref, up_ref, out_ref):
    low = sum_ref[:lowrank, :] * adapter_scale
    spread = [jnp.where(tenant_ref[...] == t, low, 0.0) for t in range(tenants)]
    lhs = jnp.concatenate(spread, axis=0).astype(bf16)
    out_ref[...] = dot(lhs, up_ref[...], TN)


def adam_kernel(parts, lowrank, width, place_ref, *refs):
    grads = refs[:parts]
    moments, squares = refs[parts : parts + 2], refs[parts + 2 : parts + 4]
    means, powers = refs[parts + 4 : parts + 6], refs[parts + 6 : parts + 8]
    changes = refs[parts + 8 :]
    me = place_ref[0]
    total = jnp.zeros((2 * lowrank, width), f32)
    for ref in grads:
        total = total + ref[...] * ref[...]
    norm = jnp.sqrt(jnp.sum(total, keepdims=True))
    factor = clip_norm / jnp.maximum(norm, clip_norm)
    for k in range(parts):
        columns = pl.ds(pl.multiple_of((me ^ k) * width, width), width)
        for half in range(2):
            rows = pl.ds(half * lowrank, lowrank)
            clipped = grads[k][rows, :] * factor
            mean = beta_one * moments[half][0, :, columns] + (1.0 - beta_one) * clipped
            power = (
                beta_two * squares[half][0, :, columns] + (1.0 - beta_two) * clipped * clipped
            )
            means[half][0, :, columns] = mean
            powers[half][0, :, columns] = power
            changes[k][rows, :] = (
                learn_rate * (mean / correct_one) / (jnp.sqrt(power / correct_two) + adam_eps)
            )


def update_kernel(parts, parts_dp, lowrank, place_ref, slot_ref, down_ref, up_ref, *refs):
    blocks, (down_out, up_out) = refs[: parts * parts_dp], refs[parts * parts_dp :]
    me, core = place_ref[0], place_ref[1]
    for j in range(parts_dp):
        for k in range(parts):
            tenant = slot_ref[(me ^ k) * parts_dp + (core ^ j)]
            block = blocks[j * parts + k]
            down_out[tenant] = (down_ref[tenant].astype(f32) - block[:lowrank]).astype(bf16)
            up_out[tenant] = (up_ref[tenant].astype(f32) - block[lowrank:]).astype(bf16)


def swap(x, axis, bits):
    size = lax.axis_size(axis)
    return lax.ppermute(x, axis, [(i, i ^ bits) for i in range(size)])


def sum_over(x, axis):
    size, low = lax.axis_size(axis), 1
    while low < size:
        reach = 2 if low == 1 else min(4, size // low)
        others = [swap(x, axis, low * j) for j in range(1, reach)]
        for other in others:
            x = x + other
        low *= reach
    return x


def on_device(
    features,
    cotangent,
    token_tenant,
    owner_device,
    frozen_weight,
    adapter_down,
    adapter_up,
    momentum_down,
    momentum_up,
    variance_down,
    variance_up,
):
    tokens = features.shape[0]
    tenants, lowrank, width = adapter_down.shape
    parts = lax.axis_size("tensor")
    parts_dp = lax.axis_size("dp")
    me, core = lax.axis_index("tensor"), lax.axis_index("dp")
    place = jnp.stack([me, core]).astype(jnp.int32)
    tenant_row = token_tenant.reshape(1, tokens)
    down_flat = adapter_down.reshape(tenants * lowrank, width)
    up_flat = adapter_up.reshape(tenants * lowrank, width)
    slot_index = lax.broadcasted_iota(jnp.int32, (tenants, tenants), 0)
    tenant_index = lax.broadcasted_iota(jnp.int32, (tenants, tenants), 1)
    slot_tenant = jnp.sum(jnp.where(owner_device[None, :] == slot_index, tenant_index, 0), axis=1)

    rank_part = pl.pallas_call(
        functools.partial(rank_kernel, tenants, lowrank),
        in_specs=[vmem] * 5,
        out_specs=vmem,
        out_shape=jax.ShapeDtypeStruct((2 * lowrank, tokens), f32),
        compiler_params=params(),
        name="rank_part",
    )(tenant_row, features, cotangent, down_flat, up_flat)
    features_next, cotangent_next, rank_part = lax.optimization_barrier(
        (features, cotangent, rank_part)
    )
    feat_other = swap(features_next.astype(f32), "dp", 1)
    cot_other = swap(cotangent_next.astype(f32), "dp", 1)
    tenant_other = swap(tenant_row, "dp", 1)

    partials = frozen_partials(features_next, frozen_weight, parts)
    frozen_result = lax.psum_scatter(
        partials.reshape(parts * tokens, width), "tensor", scatter_dimension=0, tiled=True
    )

    rank_sum = sum_over(rank_part, "tensor")
    sum_other = swap(rank_sum, "dp", 1)

    grads = pl.pallas_call(
        functools.partial(grad_kernel, parts, parts_dp, lowrank, tenants),
        in_specs=[smem, smem] + [vmem] * 8,
        out_specs=[vmem] * parts,
        out_shape=[jax.ShapeDtypeStruct((2 * lowrank, width), f32)] * parts,
        compiler_params=params(),
        name="gradients",
    )(
        place, owner_device, rank_sum, sum_other, tenant_row, tenant_other,
        features, feat_other, cotangent, cot_other,
    )
    order = sorted(range(1, parts), key=lambda k: (-(k // 2), k))
    got = {0: grads[0]}
    for k in order:
        got[k] = swap(grads[k], "tensor", k)

    adapter_result = pl.pallas_call(
        functools.partial(adapter_kernel, tenants, lowrank),
        in_specs=[vmem] * 3,
        out_specs=vmem,
        out_shape=jax.ShapeDtypeStruct((tokens, width), f32),
        compiler_params=params(),
        name="adapter_result",
    )(tenant_row, rank_sum, up_flat)

    state = jax.ShapeDtypeStruct(momentum_down.shape, f32)
    adam = pl.pallas_call(
        functools.partial(adam_kernel, parts, lowrank, width),
        in_specs=[smem] + [vmem] * (parts + 4),
        out_specs=[vmem] * (parts + 4),
        out_shape=[state] * 4 + [jax.ShapeDtypeStruct((2 * lowrank, width), f32)] * parts,
        compiler_params=params(),
        name="adam",
    )(
        place, *[got[k] for k in range(parts)],
        momentum_down, momentum_up, variance_down, variance_up,
    )
    mean_down, mean_up, power_down, power_up = adam[:4]
    change = adam[4:]
    blocks = {0: change[0]}
    for k in order:
        blocks[k] = swap(change[k], "tensor", k)
    blocks = [blocks[k] for k in range(parts)]
    for k in range(parts):
        blocks.append(swap(blocks[k], "dp", 1))
    updated_down, updated_up = pl.pallas_call(
        functools.partial(update_kernel, parts, parts_dp, lowrank),
        in_specs=[smem, smem] + [vmem] * (2 + parts * parts_dp),
        out_specs=[vmem] * 2,
        out_shape=[jax.ShapeDtypeStruct(adapter_down.shape, bf16)] * 2,
        compiler_params=params(),
        name="update",
    )(place, slot_tenant, adapter_down, adapter_up, *blocks)

    projected = (frozen_result + adapter_result).astype(bf16)
    return (projected, updated_down, updated_up, mean_down, mean_up, power_down, power_up)


def solution(mesh):
    in_specs = (
        P(("group", "dp"), "tensor"),
        P(("group", "dp"), "tensor"),
        P(("group", "dp")),
        P("group"),
        P("tensor", None),
        P("group", None, "tensor"),
        P("group", None, "tensor"),
        P(("group", "tensor", "dp"), None, None),
        P(("group", "tensor", "dp"), None, None),
        P(("group", "tensor", "dp"), None, None),
        P(("group", "tensor", "dp"), None, None),
    )
    out_specs = (
        P(("group", "dp"), "tensor"),
        P("group", None, "tensor"),
        P("group", None, "tensor"),
        P(("group", "tensor", "dp"), None, None),
        P(("group", "tensor", "dp"), None, None),
        P(("group", "tensor", "dp"), None, None),
        P(("group", "tensor", "dp"), None, None),
    )
    return jax.shard_map(
        on_device, mesh=mesh, in_specs=in_specs, out_specs=out_specs, check_vma=False
    )
```

time: 378 us -> 153 us (0.40)
  other arithmetic: 88.7 us -> 3.72 us
  waiting for transfers between devices: 131 us -> 67.2 us
  blocking collectives: 57.3 us -> 0 us
  local copies, waits for them, and re-layouts: 52.8 us -> 10.7 us
  starting transfers between devices: 13.5 us -> 41.6 us
  matrix products: 16.4 us -> 0 us
  Pallas kernels: 0 us -> 15.5 us
    unnamed x4 -> x0, other arithmetic: 76.9 us -> none
    reduce_scatter x3 -> x1, waiting for transfers between devices: 93.4 us -> 17.3 us  [on_device(): lax.psum_scatter(partials.reshape(parts * tokens, width), 'tensor', scatt...]
    ppermute x0 -> x30, waiting for transfers between devices: none -> 49.9 us  [swap(): return lax.ppermute(x, axis, [(i, i ^ bits) for i in range(size)])]
    ppermute x0 -> x30, starting transfers between devices: none -> 41.6 us  [swap(): return lax.ppermute(x, axis, [(i, i ^ bits) for i in range(size)])]
    psum x1 -> x0, blocking collectives: 38.8 us -> none  [on_device(): down_sum, up_sum = lax.psum((down_part, up_part), 'tensor')]
    all_to_all x3 -> x0, waiting for transfers between devices: 36.8 us -> none  [the longest x1 14.1 us: on_device(): lax.all_to_all(change_down, ('tensor', 'dp'), split_axis=2, concat_axis=0...]
    all_to_all x1 -> x0, blocking collectives: 18.5 us -> none  [on_device(): lax.all_to_all(change_up, ('tensor', 'dp'), split_axis=2, concat_axis=0,...]
    dot_general x8 -> x0, matrix products: 16.4 us -> none  [the longest x1 10.2 us: frozen_blocks(): jnp.einsum('ti,ibc->btc', features, columns, preferred_element_type=jnp.f...]
  transfers between devices with their start and end apart: 8 -> 31, of which waited for: 6 -> 17; matrix products, arithmetic and copies ran while one was open for 21% -> 1% of each run, Pallas kernels for 0% -> 4%
where the time goes in v1:
time: 153 us
  waiting for transfers between devices  67.2 us (44%)
  starting transfers between devices  41.6 us (27%)
  Pallas kernels  15.5 us (10%)
  between operations  14.2 us (9%)
  local copies, waits for them, and re-layouts  10.7 us (7%)
  other arithmetic  3.72 us (2%)
    ppermute x30, waiting for transfers between devices, swap(): return lax.ppermute(x, axis, [(i, i ^ bits) for i in range(size)])  49.9 us
    ppermute x30, starting transfers between devices, swap(): return lax.ppermute(x, axis, [(i, i ^ bits) for i in range(size)])  41.6 us
    reduce_scatter x1, waiting for transfers between devices, on_device(): lax.psum_scatter(partials.reshape(parts * tokens, width), 'tensor', scatt...  17.3 us
    unnamed x34, local copies, waits for them, and re-layouts  10.7 us
    pallas_call x1, Pallas kernels, frozen_partials(): pl.pallas_call(frozen_kernel, grid=(parts,), in_specs=[pl.BlockSpec((toke...  9.36 us
  transfers between devices with their start and end apart: 31, of which 17 were waited for; matrix products, arithmetic and copies ran while one was open for 1% of the time, Pallas kernels for 4%

profile of v1, /device:TPU:0, one launch (start us, length us, event | category | flops | bytes accessed | tf_op | source)
XLA Modules:
  0.0 152.9 jit_solution(9700107336697577933)
XLA Ops:
  13.3 9.4 %frozen_partials.1 = f32[8,128,1024]{2,1,0:T(8,128)S(1)} custom-call(bf16[128,1024]{1,0:T(8,128)(2,1)S(1)} %copy-done.4, bf16[1024,8192]{1,0:T(8,128)(2,1)} %weight_ref.1), custom_call_target="tpu_custom_call" | custom-call | flops 2147483648 | bytes 20971520 | tf_op jit(solution)/shard_map/frozen_partials/pallas_call | solution.py:53
  22.7 2.0 %copy-done = f32[8,128,1024]{2,1,0:T(8,128)} copy-done((f32[8,128,1024]{2,1,0:T(8,128)}, f32[8,128,1024]{2,1,0:T(8,128)S(1)}, u32[]{:S(2)}) %copy-start) | copy-done | bytes 4194328
  26.9 3.0 %collective-permute-start = (f32[32,128]{1,0:T(8,128)S(1)}, f32[32,128]{1,0:T(8,128)S(1)}, u32[]{:S(2)}, u32[]{:S(2)}) collective-permute-start(f32[32,128]{1,0:T(8,128)S(1)} %rank_part.1), channel_id=1, source_target_pairs={{0,2},{2,0},{4,6},{6,4},{8,10},{10,8},{12,14},{14,12},{1,3},{3,1},... | collective-permute-start | bytes 49160 | tf_op jit(solution)/shard_map/ppermute | solution.py:143
  29.9 1.7 %collective-permute-done = f32[32,128]{1,0:T(8,128)S(1)} collective-permute-done((f32[32,128]{1,0:T(8,128)S(1)}, f32[32,128]{1,0:T(8,128)S(1)}, u32[]{:S(2)}, u32[]{:S(2)}) %collective-permute-start) | collective-permute-done | bytes 16416 | tf_op jit(solution)/shard_map/ppermute | solution.py:143
  31.6 4.1 %collective-permute-start.3 = (f32[32,128]{1,0:T(8,128)S(1)}, f32[32,128]{1,0:T(8,128)S(1)}, u32[]{:S(2)}, u32[]{:S(2)}) collective-permute-start(f32[32,128]{1,0:T(8,128)S(1)} %add.17), channel_id=1, source_target_pairs={{0,12},{2,14},{4,8},{6,10},{8,4},{10,6},{12,0},{14,2},{1,13},{3,15... | collective-permute-start | bytes 49160 | tf_op jit(solution)/shard_map/ppermute | solution.py:143
  37.5 3.8 %collective-permute-done.2 = f32[32,128]{1,0:T(8,128)S(1)} collective-permute-done((f32[32,128]{1,0:T(8,128)S(1)}, f32[32,128]{1,0:T(8,128)S(1)}, u32[]{:S(2)}, u32[]{:S(2)}) %collective-permute-start.2) | collective-permute-done | bytes 16416 | tf_op jit(solution)/shard_map/ppermute | solution.py:143
  45.0 2.0 %collective-permute-start.10 = (f32[32,1024]{1,0:T(8,128)S(1)}, f32[32,1024]{1,0:T(8,128)S(1)}, u32[]{:S(2)}, u32[]{:S(2)}) collective-permute-start(f32[32,1024]{1,0:T(8,128)S(1)} %get-tuple-element.38), channel_id=1, source_target_pairs={{0,6},{2,4},{4,2},{6,0},{8,14},{10,12},{12,10},{14,8},{1,7},{3,5},... | collective-permute-start | bytes 393224 | tf_op jit(solution)/shard_map/ppermute | solution.py:143
  48.3 2.6 %collective-permute-start.12 = (f32[32,1024]{1,0:T(8,128)S(1)}, f32[32,1024]{1,0:T(8,128)S(1)}, u32[]{:S(2)}, u32[]{:S(2)}) collective-permute-start(f32[32,1024]{1,0:T(8,128)S(1)} %get-tuple-element.40), channel_id=1, source_target_pairs={{0,10},{2,8},{4,14},{6,12},{8,2},{10,0},{12,6},{14,4},{1,11},{3,9}... | collective-permute-start | bytes 393224 | tf_op jit(solution)/shard_map/ppermute | solution.py:143
  52.5 10.9 %collective-permute-done.9.refs_2_ = f32[32,1024]{1,0:T(8,128)S(1)} collective-permute-done((f32[32,1024]{1,0:T(8,128)S(1)}, f32[32,1024]{1,0:T(8,128)S(1)}, u32[]{:S(2)}, u32[]{:S(2)}) %collective-permute-start.9) | collective-permute-done | bytes 131104 | tf_op jit(solution)/shard_map/ppermute | solution.py:143
  63.4 1.8 %collective-permute-start.14 = (f32[32,1024]{1,0:T(8,128)S(1)}, f32[32,1024]{1,0:T(8,128)S(1)}, u32[]{:S(2)}, u32[]{:S(2)}) collective-permute-start(f32[32,1024]{1,0:T(8,128)S(1)} %get-tuple-element.42), channel_id=1, source_target_pairs={{0,14},{2,12},{4,10},{6,8},{8,6},{10,4},{12,2},{14,0},{1,15},{3,13... | collective-permute-start | bytes 393224 | tf_op jit(solution)/shard_map/ppermute | solution.py:143
  65.2 4.8 %collective-permute-done.10.refs_3_ = f32[32,1024]{1,0:T(8,128)S(1)} collective-permute-done((f32[32,1024]{1,0:T(8,128)S(1)}, f32[32,1024]{1,0:T(8,128)S(1)}, u32[]{:S(2)}, u32[]{:S(2)}) %collective-permute-start.10) | collective-permute-done | bytes 131104 | tf_op jit(solution)/shard_map/ppermute | solution.py:143
  70.1 2.0 %collective-permute-done.12.refs_5_ = f32[32,1024]{1,0:T(8,128)S(1)} collective-permute-done((f32[32,1024]{1,0:T(8,128)S(1)}, f32[32,1024]{1,0:T(8,128)S(1)}, u32[]{:S(2)}, u32[]{:S(2)}) %collective-permute-start.12) | collective-permute-done | bytes 131104 | tf_op jit(solution)/shard_map/ppermute | solution.py:143
  72.1 5.3 %collective-permute-done.13.refs_6_ = f32[32,1024]{1,0:T(8,128)S(1)} collective-permute-done((f32[32,1024]{1,0:T(8,128)S(1)}, f32[32,1024]{1,0:T(8,128)S(1)}, u32[]{:S(2)}, u32[]{:S(2)}) %collective-permute-start.13) | collective-permute-done | bytes 131104 | tf_op jit(solution)/shard_map/ppermute | solution.py:143
  77.4 5.3 %collective-permute-done.14.refs_7_ = f32[32,1024]{1,0:T(8,128)S(1)} collective-permute-done((f32[32,1024]{1,0:T(8,128)S(1)}, f32[32,1024]{1,0:T(8,128)S(1)}, u32[]{:S(2)}, u32[]{:S(2)}) %collective-permute-start.14) | collective-permute-done | bytes 131104 | tf_op jit(solution)/shard_map/ppermute | solution.py:143
  85.8 2.8 %adam.1 = (f32[1,16,8192]{2,1,0:T(8,128)}, f32[1,16,8192]{2,1,0:T(8,128)}, f32[1,16,8192]{2,1,0:T(8,128)}, f32[1,16,8192]{2,1,0:T(8,128)}, f32[32,1024]{1,0:T(8,...) custom-call(s32[2]{0:T(128)S(1)} %pad_add_fusion.place_ref, ...), custom_call_target="tpu_custom_call" | custom-call | tf_op jit(solution)/shard_map/adam/pallas_call | solution.py:232
  90.2 10.9 %collective-permute-start.16 = (f32[32,1024]{1,0:T(8,128)S(1)}, f32[32,1024]{1,0:T(8,128)S(1)}, u32[]{:S(2)}, u32[]{:S(2)}) collective-permute-start(f32[32,1024]{1,0:T(8,128)S(1)} %get-tuple-element.45), channel_id=1, source_target_pairs={{0,4},{2,6},{4,0},{6,2},{8,12},{10,14},{12,8},{14,10},{1,5},{3,7},... | collective-permute-start | bytes 393224 | tf_op jit(solution)/shard_map/ppermute | solution.py:143
  102.2 2.5 %collective-permute-start.18 = (f32[32,1024]{1,0:T(8,128)S(1)}, f32[32,1024]{1,0:T(8,128)S(1)}, u32[]{:S(2)}, u32[]{:S(2)}) collective-permute-start(f32[32,1024]{1,0:T(8,128)S(1)} %get-tuple-element.47), channel_id=1, source_target_pairs={{0,8},{2,10},{4,12},{6,14},{8,0},{10,2},{12,4},{14,6},{1,9},{3,11}... | collective-permute-start | bytes 393224 | tf_op jit(solution)/shard_map/ppermute | solution.py:143
  105.1 1.9 %collective-permute-start.20 = (f32[32,1024]{1,0:T(8,128)S(1)}, f32[32,1024]{1,0:T(8,128)S(1)}, u32[]{:S(2)}, u32[]{:S(2)}) collective-permute-start(f32[32,1024]{1,0:T(8,128)S(1)} %get-tuple-element.49), channel_id=1, source_target_pairs={{0,12},{2,14},{4,8},{6,10},{8,4},{10,6},{12,0},{14,2},{1,13},{3,15... | collective-permute-start | bytes 393224 | tf_op jit(solution)/shard_map/ppermute | solution.py:143
  107.0 2.8 %collective-permute-start.21 = (f32[32,1024]{1,0:T(8,128)S(1)}, f32[32,1024]{1,0:T(8,128)S(1)}, u32[]{:S(2)}, u32[]{:S(2)}) collective-permute-start(f32[32,1024]{1,0:T(8,128)S(1)} %get-tuple-element.50), channel_id=1, source_target_pairs={{0,14},{2,12},{4,10},{6,8},{8,6},{10,4},{12,2},{14,0},{1,15},{3,13... | collective-permute-start | bytes 393224 | tf_op jit(solution)/shard_map/ppermute | solution.py:143
  110.0 10.0 %collective-permute-done.18.refs_4_ = f32[32,1024]{1,0:T(8,128)S(1)} collective-permute-done((f32[32,1024]{1,0:T(8,128)S(1)}, f32[32,1024]{1,0:T(8,128)S(1)}, u32[]{:S(2)}, u32[]{:S(2)}) %collective-permute-start.18) | collective-permute-done | bytes 131104 | tf_op jit(solution)/shard_map/ppermute | solution.py:143
  120.0 2.5 %collective-permute-done.19.refs_5_ = f32[32,1024]{1,0:T(8,128)S(1)} collective-permute-done((f32[32,1024]{1,0:T(8,128)S(1)}, f32[32,1024]{1,0:T(8,128)S(1)}, u32[]{:S(2)}, u32[]{:S(2)}) %collective-permute-start.19) | collective-permute-done | bytes 131104 | tf_op jit(solution)/shard_map/ppermute | solution.py:143
  125.2 1.8 %update.1 = (bf16[16,16,1024]{2,1,0:T(8,128)(2,1)}, bf16[16,16,1024]{2,1,0:T(8,128)(2,1)}) custom-call(s32[2]{0:T(128)S(1)} %pad_add_fusion.place_ref, s32[16]{0:T(128)S(1)} %select_reduce_fusion.slot_ref, bf16[16,16,1024]{2,1,0:T(8,128)(2,1)S(1)} %copy-done.9, bf16[16,16,1024]{2,1,0:T(8,128)(2,1)S(1)} %copy-done.2, ...), custom_call_target="tpu_custom_call" | custom-call | tf_op jit(solution)/shard_map/update/pallas_call | solution.py:251
  127.0 17.3 %reduce-scatter.2.cloned.1.call-done = f32[128,1024]{1,0:T(8,128)} async-done(((f32[1024,1024]{1,0:T(8,128)}), f32[128,1024]{1,0:T(8,128)}) %reduce-scatter.2.cloned.1.call-update) | async-done | bytes 524304 | tf_op jit(solution)/shard_map/reduce_scatter | solution.py:199
  144.3 1.8 %add_convert_fusion = bf16[128,1024]{1,0:T(8,128)(2,1)} fusion(f32[128,1024]{1,0:T(8,128)} %reduce-scatter.2.cloned.1.call-done, f32[128,1024]{1,0:T(8,128)S(1)} %adapter_result.1), kind=kLoop, calls=%fused_computation | loop fusion | flops 262144 | bytes 1310720 | tf_op jit(solution)/shard_map/convert_element_type | solution.py:260
  (86 shorter events, 25.7 us)
Async XLA Ops:
  7.2 137.1 %reduce-scatter.2.cloned.1.call-start = ((), (), s32[]{:S(2)}) async-start(), calls=%async_computation.1 | async-start | bytes 4718592 | tf_op jit(solution)/shard_map/reduce_scatter | solution.py:199
  25.5 17.1 %collective-permute-start.6 = (f32[128,1024]{1,0:T(8,128)}, f32[128,1024]{1,0:T(8,128)S(1)}, u32[]{:S(2)}, u32[]{:S(2)}) collective-permute-start(f32[128,1024]{1,0:T(8,128)} %convert_element_type.10), channel_id=1, source_target_pairs={{0,1},{1,0},{2,3},{3,2},{4,5},{5,4},{6,7},{7,6},{8,9},{9,8},{10,11... | collective-permute-start | bytes 1572872 | tf_op jit(solution)/shard_map/ppermute | solution.py:143
  26.8 15.8 %collective-permute-start.7 = (f32[128,1024]{1,0:T(8,128)}, f32[128,1024]{1,0:T(8,128)S(1)}, u32[]{:S(2)}, u32[]{:S(2)}) collective-permute-start(f32[128,1024]{1,0:T(8,128)} %convert_element_type.11), channel_id=1, source_target_pairs={{0,1},{1,0},{2,3},{3,2},{4,5},{5,4},{6,7},{7,6},{8,9},{9,8},{10,11... | collective-permute-start | bytes 1572872 | tf_op jit(solution)/shard_map/ppermute | solution.py:143
  26.9 4.7 %collective-permute-start = (f32[32,128]{1,0:T(8,128)S(1)}, f32[32,128]{1,0:T(8,128)S(1)}, u32[]{:S(2)}, u32[]{:S(2)}) collective-permute-start(f32[32,128]{1,0:T(8,128)S(1)} %rank_part.1), channel_id=1, source_target_pairs={{0,2},{2,0},{4,6},{6,4},{8,10},{10,8},{12,14},{14,12},{1,3},{3,1},... | collective-permute-start | bytes 49160 | tf_op jit(solution)/shard_map/ppermute | solution.py:143
  31.6 5.9 %collective-permute-start.3 = (f32[32,128]{1,0:T(8,128)S(1)}, f32[32,128]{1,0:T(8,128)S(1)}, u32[]{:S(2)}, u32[]{:S(2)}) collective-permute-start(f32[32,128]{1,0:T(8,128)S(1)} %add.17), channel_id=1, source_target_pairs={{0,12},{2,14},{4,8},{6,10},{8,4},{10,6},{12,0},{14,2},{1,13},{3,15... | collective-permute-start | bytes 49160 | tf_op jit(solution)/shard_map/ppermute | solution.py:143
  35.7 5.6 %collective-permute-start.2 = (f32[32,128]{1,0:T(8,128)S(1)}, f32[32,128]{1,0:T(8,128)S(1)}, u32[]{:S(2)}, u32[]{:S(2)}) collective-permute-start(f32[32,128]{1,0:T(8,128)S(1)} %add.17), channel_id=1, source_target_pairs={{0,8},{2,10},{4,12},{6,14},{8,0},{10,2},{12,4},{14,6},{1,9},{3,11}... | collective-permute-start | bytes 49160 | tf_op jit(solution)/shard_map/ppermute | solution.py:143
  35.7 5.6 %collective-permute-start.1 = (f32[32,128]{1,0:T(8,128)S(1)}, f32[32,128]{1,0:T(8,128)S(1)}, u32[]{:S(2)}, u32[]{:S(2)}) collective-permute-start(f32[32,128]{1,0:T(8,128)S(1)} %add.17), channel_id=1, source_target_pairs={{0,4},{2,6},{4,0},{6,2},{8,12},{10,14},{12,8},{14,10},{1,5},{3,7},... | collective-permute-start | bytes 49160 | tf_op jit(solution)/shard_map/ppermute | solution.py:143
  37.5 4.0 %collective-permute-start.5 = (s32[1,128]{1,0:T(1,128)S(1)}, s32[1,128]{1,0:T(1,128)S(1)}, u32[]{:S(2)}, u32[]{:S(2)}) collective-permute-start(s32[1,128]{1,0:T(1,128)S(1)} %bitcast.11), channel_id=1, source_target_pairs={{0,1},{1,0},{2,3},{3,2},{4,5},{5,4},{6,7},{7,6},{8,9},{9,8},{10,11... | collective-permute-start | bytes 1544 | tf_op jit(solution)/shard_map/ppermute | solution.py:143
  43.5 7.4 %collective-permute-start.8 = (f32[32,1024]{1,0:T(8,128)S(1)}, f32[32,1024]{1,0:T(8,128)S(1)}, u32[]{:S(2)}, u32[]{:S(2)}) collective-permute-start(f32[32,1024]{1,0:T(8,128)S(1)} %get-tuple-element.36), channel_id=1, source_target_pairs={{0,2},{2,0},{4,6},{6,4},{8,10},{10,8},{12,14},{14,12},{1,3},{3,1},... | collective-permute-start | bytes 393224 | tf_op jit(solution)/shard_map/ppermute | solution.py:143
  45.0 18.4 %collective-permute-start.9 = (f32[32,1024]{1,0:T(8,128)S(1)}, f32[32,1024]{1,0:T(8,128)S(1)}, u32[]{:S(2)}, u32[]{:S(2)}) collective-permute-start(f32[32,1024]{1,0:T(8,128)S(1)} %get-tuple-element.37), channel_id=1, source_target_pairs={{0,4},{2,6},{4,0},{6,2},{8,12},{10,14},{12,8},{14,10},{1,5},{3,7},... | collective-permute-start | bytes 393224 | tf_op jit(solution)/shard_map/ppermute | solution.py:143
  45.0 25.0 %collective-permute-start.10 = (f32[32,1024]{1,0:T(8,128)S(1)}, f32[32,1024]{1,0:T(8,128)S(1)}, u32[]{:S(2)}, u32[]{:S(2)}) collective-permute-start(f32[32,1024]{1,0:T(8,128)S(1)} %get-tuple-element.38), channel_id=1, source_target_pairs={{0,6},{2,4},{4,2},{6,0},{8,14},{10,12},{12,10},{14,8},{1,7},{3,5},... | collective-permute-start | bytes 393224 | tf_op jit(solution)/shard_map/ppermute | solution.py:143
  47.0 23.0 %collective-permute-start.11 = (f32[32,1024]{1,0:T(8,128)S(1)}, f32[32,1024]{1,0:T(8,128)S(1)}, u32[]{:S(2)}, u32[]{:S(2)}) collective-permute-start(f32[32,1024]{1,0:T(8,128)S(1)} %get-tuple-element.39), channel_id=1, source_target_pairs={{0,8},{2,10},{4,12},{6,14},{8,0},{10,2},{12,4},{14,6},{1,9},{3,11}... | collective-permute-start | bytes 393224 | tf_op jit(solution)/shard_map/ppermute | solution.py:143
  48.3 23.8 %collective-permute-start.12 = (f32[32,1024]{1,0:T(8,128)S(1)}, f32[32,1024]{1,0:T(8,128)S(1)}, u32[]{:S(2)}, u32[]{:S(2)}) collective-permute-start(f32[32,1024]{1,0:T(8,128)S(1)} %get-tuple-element.40), channel_id=1, source_target_pairs={{0,10},{2,8},{4,14},{6,12},{8,2},{10,0},{12,6},{14,4},{1,11},{3,9}... | collective-permute-start | bytes 393224 | tf_op jit(solution)/shard_map/ppermute | solution.py:143
  50.9 26.5 %collective-permute-start.13 = (f32[32,1024]{1,0:T(8,128)S(1)}, f32[32,1024]{1,0:T(8,128)S(1)}, u32[]{:S(2)}, u32[]{:S(2)}) collective-permute-start(f32[32,1024]{1,0:T(8,128)S(1)} %get-tuple-element.41), channel_id=1, source_target_pairs={{0,12},{2,14},{4,8},{6,10},{8,4},{10,6},{12,0},{14,2},{1,13},{3,15... | collective-permute-start | bytes 393224 | tf_op jit(solution)/shard_map/ppermute | solution.py:143
  63.4 19.2 %collective-permute-start.14 = (f32[32,1024]{1,0:T(8,128)S(1)}, f32[32,1024]{1,0:T(8,128)S(1)}, u32[]{:S(2)}, u32[]{:S(2)}) collective-permute-start(f32[32,1024]{1,0:T(8,128)S(1)} %get-tuple-element.42), channel_id=1, source_target_pairs={{0,14},{2,12},{4,10},{6,8},{8,6},{10,4},{12,2},{14,0},{1,15},{3,13... | collective-permute-start | bytes 393224 | tf_op jit(solution)/shard_map/ppermute | solution.py:143
  88.6 16.5 %collective-permute-start.15 = (f32[32,1024]{1,0:T(8,128)S(1)}, f32[32,1024]{1,0:T(8,128)S(1)}, u32[]{:S(2)}, u32[]{:S(2)}) collective-permute-start(f32[32,1024]{1,0:T(8,128)S(1)} %get-tuple-element.44), channel_id=1, source_target_pairs={{0,2},{2,0},{4,6},{6,4},{8,10},{10,8},{12,14},{14,12},{1,3},{3,1},... | collective-permute-start | bytes 393224 | tf_op jit(solution)/shard_map/ppermute | solution.py:143
  90.2 16.9 %collective-permute-start.16 = (f32[32,1024]{1,0:T(8,128)S(1)}, f32[32,1024]{1,0:T(8,128)S(1)}, u32[]{:S(2)}, u32[]{:S(2)}) collective-permute-start(f32[32,1024]{1,0:T(8,128)S(1)} %get-tuple-element.45), channel_id=1, source_target_pairs={{0,4},{2,6},{4,0},{6,2},{8,12},{10,14},{12,8},{14,10},{1,5},{3,7},... | collective-permute-start | bytes 393224 | tf_op jit(solution)/shard_map/ppermute | solution.py:143
  101.1 8.9 %collective-permute-start.17 = (f32[32,1024]{1,0:T(8,128)S(1)}, f32[32,1024]{1,0:T(8,128)S(1)}, u32[]{:S(2)}, u32[]{:S(2)}) collective-permute-start(f32[32,1024]{1,0:T(8,128)S(1)} %get-tuple-element.46), channel_id=1, source_target_pairs={{0,6},{2,4},{4,2},{6,0},{8,14},{10,12},{12,10},{14,8},{1,7},{3,5},... | collective-permute-start | bytes 393224 | tf_op jit(solution)/shard_map/ppermute | solution.py:143
  102.2 17.8 %collective-permute-start.18 = (f32[32,1024]{1,0:T(8,128)S(1)}, f32[32,1024]{1,0:T(8,128)S(1)}, u32[]{:S(2)}, u32[]{:S(2)}) collective-permute-start(f32[32,1024]{1,0:T(8,128)S(1)} %get-tuple-element.47), channel_id=1, source_target_pairs={{0,8},{2,10},{4,12},{6,14},{8,0},{10,2},{12,4},{14,6},{1,9},{3,11}... | collective-permute-start | bytes 393224 | tf_op jit(solution)/shard_map/ppermute | solution.py:143
  104.7 17.9 %collective-permute-start.19 = (f32[32,1024]{1,0:T(8,128)S(1)}, f32[32,1024]{1,0:T(8,128)S(1)}, u32[]{:S(2)}, u32[]{:S(2)}) collective-permute-start(f32[32,1024]{1,0:T(8,128)S(1)} %get-tuple-element.48), channel_id=1, source_target_pairs={{0,10},{2,8},{4,14},{6,12},{8,2},{10,0},{12,6},{14,4},{1,11},{3,9}... | collective-permute-start | bytes 393224 | tf_op jit(solution)/shard_map/ppermute | solution.py:143
  105.1 17.4 %collective-permute-start.20 = (f32[32,1024]{1,0:T(8,128)S(1)}, f32[32,1024]{1,0:T(8,128)S(1)}, u32[]{:S(2)}, u32[]{:S(2)}) collective-permute-start(f32[32,1024]{1,0:T(8,128)S(1)} %get-tuple-element.49), channel_id=1, source_target_pairs={{0,12},{2,14},{4,8},{6,10},{8,4},{10,6},{12,0},{14,2},{1,13},{3,15... | collective-permute-start | bytes 393224 | tf_op jit(solution)/shard_map/ppermute | solution.py:143
  107.0 16.0 %collective-permute-start.21 = (f32[32,1024]{1,0:T(8,128)S(1)}, f32[32,1024]{1,0:T(8,128)S(1)}, u32[]{:S(2)}, u32[]{:S(2)}) collective-permute-start(f32[32,1024]{1,0:T(8,128)S(1)} %get-tuple-element.50), channel_id=1, source_target_pairs={{0,14},{2,12},{4,10},{6,8},{8,6},{10,4},{12,2},{14,0},{1,15},{3,13... | collective-permute-start | bytes 393224 | tf_op jit(solution)/shard_map/ppermute | solution.py:143
  110.0 13.1 %collective-permute-start.22 = (f32[32,1024]{1,0:T(8,128)S(1)}, f32[32,1024]{1,0:T(8,128)S(1)}, u32[]{:S(2)}, u32[]{:S(2)}) collective-permute-start(f32[32,1024]{1,0:T(8,128)S(1)} %get-tuple-element.43.refs_0_), channel_id=1, source_target_pairs={{0,1},{1,0},{2,3},{3,2},{4,5},{5,4},{6,7},{7,6},{8,9},{9,8},{10,11... | collective-permute-start | bytes 393224 | tf_op jit(solution)/shard_map/ppermute | solution.py:143
  120.0 3.5 %collective-permute-start.23 = (f32[32,1024]{1,0:T(8,128)S(1)}, f32[32,1024]{1,0:T(8,128)S(1)}, u32[]{:S(2)}, u32[]{:S(2)}) collective-permute-start(f32[32,1024]{1,0:T(8,128)S(1)} %collective-permute-done.15.refs_1_), channel_id=1, source_target_pairs={{0,1},{1,0},{2,3},{3,2},{4,5},{5,4},{6,7},{7,6},{8,9},{9,8},{10,11... | collective-permute-start | bytes 393224 | tf_op jit(solution)/shard_map/ppermute | solution.py:143
  (24 other events, 408.6 us)
Sparse Core Ops, SparseCore 0:
  24.8 119.4 reduce-scatter.1

commit v2 on v0

v2 whole, which is shorter than its diff:
```python
import functools

import jax
import jax.numpy as jnp
from jax import lax
from jax.experimental import pallas as pl
from jax.experimental.pallas import tpu as pltpu
from jax.sharding import PartitionSpec as P

adapter_scale = 2.0
clip_norm = 12000.0
learn_rate = 0.004
beta_one = 0.9
beta_two = 0.999
adam_eps = 1e-08
correct_one = 1.0 - beta_one**20
correct_two = 1.0 - beta_two**20

f32, bf16 = jnp.float32, jnp.bfloat16
vmem = pl.BlockSpec(memory_space=pltpu.VMEM)
smem = pl.BlockSpec(memory_space=pltpu.SMEM)
hbm = pl.BlockSpec(memory_space=pltpu.HBM)
anywhere = pl.BlockSpec(memory_space=pl.ANY)
NT = (((1,), (1,)), ((), ()))
NN = (((1,), (0,)), ((), ()))
TN = (((0,), (0,)), ((), ()))


def params(mib=14):
    return pltpu.CompilerParams(vmem_limit_bytes=mib << 20)


def dot(a, b, dims):
    return lax.dot_general(a, b, dims, preferred_element_type=f32)


hbm_type = type(pltpu.HBM((8,), f32))


def call(body, outs, *args, specs=None, scratch=(), name=None, after=()):
    flat, tree = jax.tree.flatten(outs)
    specs = [vmem] * len(args) if specs is None else list(specs)
    far = [i for i, x in enumerate(args) if isinstance(x, Far)]
    back = [i for i, out in enumerate(flat) if isinstance(out, hbm_type)]
    for i in far:
        specs[i] = hbm
    args = [in_hbm(x.array) if isinstance(x, Far) else x for x in args]
    staged = [pltpu.VMEM(args[i].shape, args[i].dtype) for i in far]
    staged += [pltpu.VMEM(flat[i].shape, flat[i].dtype) for i in back]
    used, extra, count, own = len(args), len(after), len(flat), len(scratch)

    def kernel(*refs):
        ins = list(refs[:used])
        results = list(refs[used + extra : used + extra + count])
        mine = refs[used + extra + count : used + extra + count + own]
        held = refs[used + extra + count + own :]
        loads = [
            pltpu.make_async_copy(ins[i], held[n], held[-1].at[n]) for n, i in enumerate(far)
        ]
        for load in loads:
            load.start()
        for n, i in enumerate(far):
            ins[i] = held[n]
        stores = []
        for n, i in enumerate(back, len(far)):
            stores.append(pltpu.make_async_copy(held[n], results[i], held[-1].at[n]))
            results[i] = held[n]
        for load in loads:
            load.wait()
        body(*ins, *results, *mine)
        for store in stores:
            store.start()
        for store in stores:
            store.wait()

    made = pl.pallas_call(
        kernel,
        in_specs=specs + [anywhere] * extra,
        out_specs=[hbm if isinstance(out, hbm_type) else vmem for out in flat],
        out_shape=flat,
        scratch_shapes=list(scratch) + staged
        + ([pltpu.SemaphoreType.DMA((len(staged),))] if staged else []),
        compiler_params=params(),
        cost_estimate=pl.CostEstimate(flops=0, bytes_accessed=0, transcendentals=0),
        name=name,
    )(*args, *after)
    return jax.tree.unflatten(tree, made)


class Far:
    def __init__(self, array):
        self.array = array


def in_hbm(x):
    return pltpu.with_memory_space_constraint(x, pltpu.HBM)


def rank_kernel(
    tenants, lowrank, tenant_hbm, owner_hbm, feat_hbm, cot_hbm, down_hbm, up_hbm,
    out_ref, rows_ref, ids_ref, tenant_ref, owner_ref, feat_ref, cot_ref, down_ref, up_ref, sems
):
    copies = [
        pltpu.make_async_copy(src, dst, sems.at[i])
        for i, (src, dst) in enumerate(
            (
                (tenant_hbm, tenant_ref), (owner_hbm, owner_ref), (feat_hbm, feat_ref),
                (down_hbm, down_ref), (cot_hbm, cot_ref), (up_hbm, up_ref),
            )
        )
    ]
    for copy in copies:
        copy.start()
    tokens = feat_ref.shape[0]
    row = lax.broadcasted_iota(jnp.int32, (tenants, lowrank, tokens), 0)
    copies[0].wait()
    copies[1].wait()
    tenant = tenant_ref[...]
    slot = jnp.zeros_like(tenant)
    for t in range(tenants):
        slot = jnp.where(tenant == t, owner_ref[:, t : t + 1], slot)
    ids_ref[...] = jnp.zeros_like(ids_ref)
    ids_ref[0:1, :] = tenant.astype(f32)
    ids_ref[1:2, :] = slot.astype(f32)
    out_ref[2 * lowrank :, :] = ids_ref[...]
    mine = row == tenant.reshape(1, 1, tokens)
    for half, (x_ref, a_ref) in enumerate(((feat_ref, down_ref), (cot_ref, up_ref))):
        copies[2 * half + 2].wait()
        copies[2 * half + 3].wait()
        x = x_ref[...]
        scores = dot(a_ref[...].reshape(tenants * lowrank, x.shape[1]), x, NT)
        scores = scores.reshape(tenants, lowrank, tokens)
        out_ref[half * lowrank : (half + 1) * lowrank, :] = jnp.sum(
            jnp.where(mine, scores, 0.0), axis=0
        )
        rows_ref[half * tokens : (half + 1) * tokens, :] = x.astype(f32)


def near_kernel(part, near, across, diagonal, out_ref, ids_ref):
    both = out_ref.shape[0] // 2
    out_ref[:both] = part[:both] + near[:both]
    out_ref[both:] = across[:both] + diagonal[:both]
    ids_ref[...] = across[both:]


def frozen_kernel(ks, first, rows_ref, weight_hbm, out_ref, weight_ref, sems):
    count, tokens, width = out_ref.shape
    whole = weight_hbm.shape[1] // lax.axis_size("tensor")
    me = lax.axis_index("tensor")
    copies = []
    for g, k in enumerate(ks):
        columns = pl.ds(pl.multiple_of((me ^ k) * whole + first, 128), width)
        copies.append(
            pltpu.make_async_copy(
                weight_hbm.at[:, columns],
                weight_ref.at[:, pl.ds(g * width, width)],
                sems.at[g],
            )
        )
        copies[g].start()
    x = rows_ref[:tokens, :].astype(bf16)
    for copy in copies:
        copy.wait()
    result = dot(x, weight_ref[...], NN)
    for g in range(count):
        out_ref[g] = result[:, g * width : (g + 1) * width]


def add_kernel(*refs):
    total = refs[0][...]
    for ref in refs[1:-1]:
        total = total + ref[...]
    refs[-1][...] = total


def merge_kernel(keep_ref, got_ref, send_ref, hold_ref):
    half = send_ref.shape[0]
    send_ref[...] = keep_ref[:half] + got_ref[:half]
    hold_ref[...] = keep_ref[half:] + got_ref[half:]


def finish_kernel(keep_ref, got_ref, out_ref):
    out_ref[...] = keep_ref[0] + got_ref[0]


class Chunk:
    def __init__(self, rows, weight, tokens, parts, first, piece):
        self.bits = [1 << i for i in range(parts.bit_length() - 1)]
        offsets = [0]
        for bit in reversed(self.bits):
            offsets = [k ^ bit for k in offsets] + offsets
        half = parts // 2
        self.merges = len(self.bits) - 1
        self.make = lambda ks, after: call(
            functools.partial(frozen_kernel, ks, first),
            pltpu.HBM((half, tokens, piece), f32), rows, weight,
            specs=[vmem, hbm], name="frozen_blocks", after=after,
            scratch=[
                pltpu.VMEM((weight.shape[0], half * piece), bf16),
                pltpu.SemaphoreType.DMA((half,)),
            ],
        )
        self.halves = offsets[:half], offsets[half:]

    def send(self, *after):
        self.out = self.make(self.halves[0], after)
        self.got = swap(self.out, "tensor", self.bits.pop(0))
        return in_hbm(self.out)

    def keep(self, *after):
        self.hold = self.make(self.halves[1], after)
        return in_hbm(self.hold)

    def merge(self, *after):
        count, tokens, piece = self.hold.shape
        shape = pltpu.HBM((count // 2, tokens, piece), f32)
        self.out, self.hold = call(
            merge_kernel, [shape, shape], Far(self.hold), self.got, after=after, name="merge"
        )
        self.got = swap(self.out, "tensor", self.bits.pop(0))
        self.merges -= 1
        return in_hbm(self.out)

    def finish(self):
        shape = pltpu.HBM(self.hold.shape[1:], f32)
        self.sum = call(finish_kernel, shape, Far(self.hold), self.got, name="finish")
        return in_hbm(self.sum)


def project_kernel(pieces, adapter_ref, *refs):
    out_ref = refs[-1]
    for c, (first, piece) in enumerate(pieces):
        columns = slice(first, first + piece)
        total = refs[c][...] + adapter_ref[:, columns]
        out_ref[:, columns] = total.astype(bf16)


def grad_kernel(parts, sum_ref, ids_own, ids_other, rows_own, rows_other, *outs):
    both, tokens = sum_ref.shape[0] // 2, ids_own.shape[1]
    lowrank = both // 2
    me, core, cores = lax.axis_index("tensor"), lax.axis_index("dp"), lax.axis_size("dp")
    low = jnp.concatenate([sum_ref[:both], sum_ref[both:]], axis=1) * adapter_scale
    slot = jnp.concatenate([ids_own[1:2], ids_other[1:2]], axis=1).astype(jnp.int32)
    picks = [slot == (me ^ k) * cores + core for k in range(parts)]
    for half, rank in enumerate((low[lowrank:], low[:lowrank])):
        these = slice(half * tokens, (half + 1) * tokens)
        lhs = jnp.concatenate([jnp.where(p, rank, 0.0) for p in picks], axis=0).astype(bf16)
        rhs = jnp.concatenate([rows_own[these], rows_other[these]], axis=0).astype(bf16)
        grad = dot(lhs, rhs, NN)
        for k in range(parts):
            outs[k][half * lowrank : (half + 1) * lowrank, :] = grad[
                k * lowrank : (k + 1) * lowrank
            ]


def adapter_kernel(tenants, lowrank, ids_ref, sum_ref, up_ref, out_ref):
    low = sum_ref[:lowrank, :] * adapter_scale
    spread = [jnp.where(ids_ref[0:1].astype(jnp.int32) == t, low, 0.0) for t in range(tenants)]
    lhs = jnp.concatenate(spread, axis=0).astype(bf16)
    out_ref[...] = dot(lhs, up_ref[...], TN)


def clip_factor(grads):
    total = grads[0][...] * grads[0][...]
    for ref in grads[1:]:
        total = total + ref[...] * ref[...]
    return clip_norm / jnp.maximum(jnp.sqrt(jnp.sum(total, keepdims=True)), clip_norm)


def moments_of(grads, state, factor, k, half):
    both, width = grads[k].shape
    lowrank = both // 2
    rows = slice(half * lowrank, (half + 1) * lowrank)
    columns = pl.ds(pl.multiple_of((lax.axis_index("tensor") ^ k) * width, width), width)
    clipped = grads[k][rows, :] * factor
    mean = beta_one * state[half][0, :, columns] + (1.0 - beta_one) * clipped
    power = beta_two * state[2 + half][0, :, columns] + (1.0 - beta_two) * clipped * clipped
    return rows, columns, mean, power


def change_kernel(parts, *refs):
    grads, state, outs = refs[:parts], refs[parts : parts + 4], refs[parts + 4 :]
    factor = clip_factor(grads)
    for k in range(parts):
        for half in range(2):
            rows, _, mean, power = moments_of(grads, state, factor, k, half)
            outs[k][rows, :] = (mean * (learn_rate / correct_one)) / (
                jnp.sqrt(power * (1.0 / correct_two)) + adam_eps
            )


def state_kernel(parts, *refs):
    grads, state = refs[:parts], refs[parts : parts + 4]
    means, powers = refs[parts + 4 : parts + 6], refs[parts + 6 : parts + 8]
    factor = clip_factor(grads)
    for k in range(parts):
        for half in range(2):
            _, columns, mean, power = moments_of(grads, state, factor, k, half)
            means[half][0, :, columns] = mean
            powers[half][0, :, columns] = power


def gate_kernel(x_ref, out_ref):
    out_ref[...] = x_ref[...]


def pack_kernel(*refs):
    for i, ref in enumerate(refs[:-1]):
        refs[-1][i] = ref[...]


def update_kernel(groups, slot_ref, down_ref, up_ref, *refs):
    down_out, up_out = refs[-2:]
    lowrank = down_ref.shape[1]
    me, core, cores = lax.axis_index("tensor"), lax.axis_index("dp"), lax.axis_size("dp")
    for i, ks in enumerate(groups):
        for j in range(2):
            for n, k in enumerate(ks):
                tenant = slot_ref[(me ^ k) * cores + (core ^ j)]
                block = refs[2 * i + j][n]
                down_out[tenant] = (down_ref[tenant].astype(f32) - block[:lowrank]).astype(bf16)
                up_out[tenant] = (up_ref[tenant].astype(f32) - block[lowrank:]).astype(bf16)


def swap(x, axis, bits):
    size = lax.axis_size(axis)
    return lax.ppermute(x, axis, [(i, i ^ bits) for i in range(size)])


def on_device(
    features,
    cotangent,
    token_tenant,
    owner_device,
    frozen_weight,
    adapter_down,
    adapter_up,
    momentum_down,
    momentum_up,
    variance_down,
    variance_up,
):
    tokens = features.shape[0]
    tenants, lowrank, width = adapter_down.shape
    parts = lax.axis_size("tensor")
    parts_dp = lax.axis_size("dp")
    slot_index = lax.broadcasted_iota(jnp.int32, (tenants, tenants), 0)
    tenant_index = lax.broadcasted_iota(jnp.int32, (tenants, tenants), 1)
    slot_tenant = jnp.sum(jnp.where(owner_device[None, :] == slot_index, tenant_index, 0), axis=1)
    bits = [1 << i for i in range(parts.bit_length() - 1)]
    block = jax.ShapeDtypeStruct((2 * lowrank, width), f32)
    low_both = jax.ShapeDtypeStruct((4 * lowrank, tokens), f32)
    id_rows = jax.ShapeDtypeStruct((8, tokens), f32)
    features, cotangent = in_hbm(features), in_hbm(cotangent)
    frozen_weight = in_hbm(frozen_weight)
    state = [Far(x) for x in (momentum_down, momentum_up, variance_down, variance_up)]

    rank_part, rows, ids = call(
        functools.partial(rank_kernel, tenants, lowrank),
        [
            jax.ShapeDtypeStruct((2 * lowrank + 8, tokens), f32),
            jax.ShapeDtypeStruct((2 * tokens, width), f32),
            id_rows,
        ],
        in_hbm(token_tenant.reshape(1, tokens)), in_hbm(owner_device.reshape(1, tenants)),
        features, cotangent, in_hbm(adapter_down), in_hbm(adapter_up),
        specs=[hbm] * 6,
        scratch=[pltpu.VMEM((1, tokens), jnp.int32), pltpu.VMEM((1, tenants), jnp.int32)]
        + [pltpu.VMEM((tokens, width), bf16)] * 2
        + [pltpu.VMEM(adapter_down.shape, bf16)] * 2
        + [pltpu.SemaphoreType.DMA((6,))],
        name="rank_part",
    )
    cores = [(i, i ^ 1) for i in range(parts_dp)]
    diagonal = [
        (t * parts_dp + i, (t ^ 1) * parts_dp + j) for t in range(parts) for i, j in cores
    ]
    rank_sum, ids_other = call(
        near_kernel, [low_both, id_rows], rank_part, swap(rank_part, "tensor", 1),
        swap(rank_part, "dp", 1), lax.ppermute(rank_part, ("tensor", "dp"), diagonal),
        name="rank_near",
    )
    rows_other = swap(rows, "dp", 1)

    units = width // 128
    cuts = sorted({0, (units + 1) // 4 or 1, (5 * units + 4) // 8, units})
    pieces = [(128 * a, 128 * (b - a)) for a, b in zip(cuts, cuts[1:])]
    frozen = [
        Chunk(rows, frozen_weight, tokens, parts, first, piece) for first, piece in pieces
    ]

    sent = frozen[0].send(rank_sum)

    done = 1
    while done < len(bits):
        two = bits[done : done + 2]
        steps = two if len(two) == 1 else [two[0], two[1], two[0] ^ two[1]]
        rank_sum = call(
            add_kernel, low_both, rank_sum, *[swap(rank_sum, "tensor", k) for k in steps],
            name="rank_far", after=[sent],
        )
        done += len(two)

    grads = call(
        functools.partial(grad_kernel, parts), [block] * parts,
        rank_sum, ids, ids_other, rows, rows_other, name="gradients",
    )

    order = sorted(range(2, parts), key=lambda k: (-(k // 2), k))
    order.insert(2, 1)
    flight = 3

    def exchange(made, beside):
        arrived = {0: made[0]}
        for n, k in enumerate(order):
            x = made[k]
            if n >= flight:
                ready = [arrived[j] for j in order[: n - flight + 1]]
                x = call(
                    gate_kernel, block, x, name="gate",
                    after=ready[-1:] + beside(n - flight, ready),
                )
            arrived[k] = swap(x, "tensor", k)
        return arrived

    early, late = frozen[:-1], frozen[-1]
    extra = {}

    def beside_gradients(n, ready):
        if n == 0:
            return [early[0].keep(*ready)]
        if n == 2:
            return [chunk.send(*ready) for chunk in early[1:]]
        if n == 3:
            return [early[0].merge(*ready)] + [chunk.keep(*ready) for chunk in early[1:]]
        return []

    got = exchange(grads, beside_gradients)
    own_grads = [got[k] for k in range(parts)]
    change = call(
        functools.partial(change_kernel, parts), [block] * parts, *own_grads, *state,
        name="change",
    )

    def beside_changes(n, ready):
        if n == 0:
            mine = []
            while early[0].merges:
                mine.append(early[0].merge(*ready))
            return mine
        if n == 1:
            extra["state"] = call(
                functools.partial(state_kernel, parts),
                [pltpu.HBM(momentum_down.shape, f32)] * 4,
                *own_grads, *state, after=ready, name="state",
            )
            return [in_hbm(extra["state"][0])]
        if n == 2:
            return [chunk.merge(*ready) for chunk in early[1:]]
        if n == 3:
            extra["adapter"] = call(
                functools.partial(adapter_kernel, tenants, lowrank),
                jax.ShapeDtypeStruct((tokens, width), f32),
                ids, rank_sum, Far(adapter_up.reshape(tenants * lowrank, width)),
                after=ready, name="adapter_result",
            )
            return [late.send(*ready), late.keep(*ready), extra["adapter"]]
        return []

    back = exchange(change, beside_changes)
    mean_down, mean_up, power_down, power_up = extra["state"]
    adapter_result = extra["adapter"]
    beside = [early[0].finish()]
    for chunk in early[1:]:
        while chunk.merges:
            beside.append(chunk.merge())
    arrive = [0] + order
    groups = [arrive[: parts // 2], arrive[parts // 2 :]]
    sides = []
    for i, ks in enumerate(groups):
        packed = call(
            pack_kernel, jax.ShapeDtypeStruct((len(ks), 2 * lowrank, width), f32),
            *[back[k] for k in ks], name="pack", after=beside if i else [],
        )
        sides += [packed, swap(packed, "dp", 1)]
    updated_down, updated_up = call(
        functools.partial(update_kernel, groups),
        [pltpu.HBM(adapter_down.shape, bf16)] * 2,
        slot_tenant, Far(adapter_down), Far(adapter_up), *sides,
        specs=[smem] + [vmem] * 6,
        name="update",
    )
    for chunk in early[1:]:
        chunk.finish()
    while late.merges:
        late.merge()
    late.finish()
    projected = call(
        functools.partial(project_kernel, pieces),
        pltpu.HBM((tokens, width), bf16),
        Far(adapter_result), *[Far(chunk.sum) for chunk in frozen],
        name="project",
    )
    return (projected, updated_down, updated_up, mean_down, mean_up, power_down, power_up)


def solution(mesh):
    in_specs = (
        P(("group", "dp"), "tensor"),
        P(("group", "dp"), "tensor"),
        P(("group", "dp")),
        P("group"),
        P("tensor", None),
        P("group", None, "tensor"),
        P("group", None, "tensor"),
        P(("group", "tensor", "dp"), None, None),
        P(("group", "tensor", "dp"), None, None),
        P(("group", "tensor", "dp"), None, None),
        P(("group", "tensor", "dp"), None, None),
    )
    out_specs = (
        P(("group", "dp"), "tensor"),
        P("group", None, "tensor"),
        P("group", None, "tensor"),
        P(("group", "tensor", "dp"), None, None),
        P(("group", "tensor", "dp"), None, None),
        P(("group", "tensor", "dp"), None, None),
        P(("group", "tensor", "dp"), None, None),
    )
    return jax.shard_map(
        on_device, mesh=mesh, in_specs=in_specs, out_specs=out_specs, check_vma=False
    )
```

time: 378 us -> 138 us (0.37)
  other arithmetic: 88.7 us -> 0.11 us
  waiting for transfers between devices: 131 us -> 45.6 us
  blocking collectives: 57.3 us -> 0 us
  local copies, waits for them, and re-layouts: 52.8 us -> 0.02 us
  Pallas kernels: 0 us -> 50.4 us
  starting transfers between devices: 13.5 us -> 39.6 us
  matrix products: 16.4 us -> 0 us
  between operations: 17 us -> 1.04 us
    reduce_scatter x3 -> x0, waiting for transfers between devices: 93.4 us -> none  [the longest x1 81.9 us: on_device(): lax.psum_scatter(result.reshape(blocks * tokens, width_shard), 'tensor',...]
    unnamed x4 -> x0, other arithmetic: 76.9 us -> none
    pallas_call x0 -> x34, Pallas kernels: none -> 50.4 us  [call(): pl.pallas_call(kernel, in_specs=specs + [anywhere] * extra, out_specs=[hb...]
    ppermute x0 -> x32, waiting for transfers between devices: none -> 45.6 us  [the longest x31 44.5 us: swap(): return lax.ppermute(x, axis, [(i, i ^ bits) for i in range(size)])]
    ppermute x0 -> x32, starting transfers between devices: none -> 39.6 us  [the longest x31 37 us: swap(): return lax.ppermute(x, axis, [(i, i ^ bits) for i in range(size)])]
    psum x1 -> x0, blocking collectives: 38.8 us -> none  [on_device(): down_sum, up_sum = lax.psum((down_part, up_part), 'tensor')]
    all_to_all x3 -> x0, waiting for transfers between devices: 36.8 us -> none  [the longest x1 14.1 us: on_device(): lax.all_to_all(change_down, ('tensor', 'dp'), split_axis=2, concat_axis=0...]
    unnamed x25 -> x8, local copies, waits for them, and re-layouts: 26.8 us -> 0.02 us
  transfers between devices with their start and end apart: 8 -> 32, of which waited for: 6 -> 13; matrix products, arithmetic and copies ran while one was open for 21% -> 0% of each run, Pallas kernels for 0% -> 33%
where the time goes in v2:
time: 138 us; the launch traced here: 137 us
  Pallas kernels  50.4 us (37%)
  waiting for transfers between devices  45.6 us (33%)
  starting transfers between devices  39.6 us (29%)
    pallas_call x34, Pallas kernels, call(): pl.pallas_call(kernel, in_specs=specs + [anywhere] * extra, out_specs=[hb...  50.4 us
    ppermute x31, waiting for transfers between devices, swap(): return lax.ppermute(x, axis, [(i, i ^ bits) for i in range(size)])  44.5 us
    ppermute x31, starting transfers between devices, swap(): return lax.ppermute(x, axis, [(i, i ^ bits) for i in range(size)])  37 us
  transfers between devices with their start and end apart: 32, of which 13 were waited for; matrix products, arithmetic and copies ran while one was open for 0% of the time, Pallas kernels for 33%

profile of v2, /device:TPU:0, one launch (start us, length us, event | category | flops | bytes accessed | tf_op | source)
XLA Modules:
  0.0 136.8 jit_solution(7975603552138564705)
XLA Ops:
  3.2 2.6 %collective-permute-start.2 = (f32[40,128]{1,0:T(8,128)S(1)}, f32[40,128]{1,0:T(8,128)S(1)}, u32[]{:S(2)}, u32[]{:S(2)}) collective-permute-start(f32[40,128]{1,0:T(8,128)S(1)} %get-tuple-element.47.refs_0_), channel_id=1, source_target_pairs={{0,3},{1,2},{2,1},{3,0},{4,7},{5,6},{6,5},{7,4},{8,11},{9,10},{10,... | collective-permute-start | bytes 61448 | tf_op jit(solution)/shard_map/ppermute | solution.py:380
  7.3 2.4 %collective-permute-done.refs_1_ = f32[40,128]{1,0:T(8,128)S(1)} collective-permute-done((f32[40,128]{1,0:T(8,128)S(1)}, f32[40,128]{1,0:T(8,128)S(1)}, u32[]{:S(2)}, u32[]{:S(2)}) %collective-permute-start) | collective-permute-done | bytes 20512 | tf_op jit(solution)/shard_map/ppermute | solution.py:327
  9.7 2.8 %frozen_blocks.6.refs_4_ = f32[4,128,256]{2,1,0:T(8,128)} custom-call(f32[256,1024]{1,0:T(8,128)S(1)} %get-tuple-element.49.refs_0_.refs_3_, bf16[1024,8192]{1,0:T(8,128)(2,1)} %refs_1_.12, f32[64,128]{1,0:T(8,128)S(1)} %get-tuple-element.48.refs_2_.refs_0_), custom_call_target="tpu_custom_call" | custom-call | tf_op jit(solution)/shard_map/frozen_blocks/pallas_call | solution.py:76
  12.9 3.8 %collective-permute-start.5 = (f32[64,128]{1,0:T(8,128)S(1)}, f32[64,128]{1,0:T(8,128)S(1)}, u32[]{:S(2)}, u32[]{:S(2)}) collective-permute-start(f32[64,128]{1,0:T(8,128)S(1)} %get-tuple-element.48.refs_2_.refs_0_), channel_id=1, source_target_pairs={{0,12},{2,14},{4,8},{6,10},{8,4},{10,6},{12,0},{14,2},{1,13},{3,15... | collective-permute-start | bytes 98312 | tf_op jit(solution)/shard_map/ppermute | solution.py:327
  18.9 2.6 %collective-permute-done.4.refs_2_ = f32[64,128]{1,0:T(8,128)S(1)} collective-permute-done((f32[64,128]{1,0:T(8,128)S(1)}, f32[64,128]{1,0:T(8,128)S(1)}, u32[]{:S(2)}, u32[]{:S(2)}) %collective-permute-start.4) | collective-permute-done | bytes 32800 | tf_op jit(solution)/shard_map/ppermute | solution.py:327
  23.4 3.3 %collective-permute-start.9 = (f32[32,1024]{1,0:T(8,128)S(1)}, f32[32,1024]{1,0:T(8,128)S(1)}, u32[]{:S(2)}, u32[]{:S(2)}) collective-permute-start(f32[32,1024]{1,0:T(8,128)S(1)} %get-tuple-element.55), channel_id=1, source_target_pairs={{0,14},{2,12},{4,10},{6,8},{8,6},{10,4},{12,2},{14,0},{1,15},{3,13... | collective-permute-start | bytes 393224 | tf_op jit(solution)/shard_map/ppermute | solution.py:327
  27.2 2.1 %collective-permute-done.8.refs_2_.refs_1_.refs_6_ = f32[32,1024]{1,0:T(8,128)S(1)} collective-permute-done((f32[32,1024]{1,0:T(8,128)S(1)}, f32[32,1024]{1,0:T(8,128)S(1)}, u32[]{:S(2)}, u32[]{:S(2)}) %collective-permute-start.8) | collective-permute-done | bytes 131104 | tf_op jit(solution)/shard_map/ppermute | solution.py:327
  29.4 2.8 %frozen_blocks.8.refs_2_.refs_0_ = f32[4,128,256]{2,1,0:T(8,128)} custom-call(f32[256,1024]{1,0:T(8,128)S(1)} %get-tuple-element.49.refs_0_.refs_3_, bf16[1024,8192]{1,0:T(8,128)(2,1)} %refs_1_.12, f32[32,1024]{1,0:T(8,128)S(1)} %collective-permute-done.8.refs_2_.refs_1_.refs_6_), custom_call_target="tpu_custom_call" | custom-call | tf_op jit(solution)/shard_map/frozen_blocks/pallas_call | solution.py:76
  32.2 6.7 %collective-permute-start.11 = (f32[32,1024]{1,0:T(8,128)S(1)}, f32[32,1024]{1,0:T(8,128)S(1)}, u32[]{:S(2)}, u32[]{:S(2)}) collective-permute-start(f32[32,1024]{1,0:T(8,128)S(1)} %gate.9), channel_id=1, source_target_pairs={{0,8},{2,10},{4,12},{6,14},{8,0},{10,2},{12,4},{14,6},{1,9},{3,11}... | collective-permute-start | bytes 393224 | tf_op jit(solution)/shard_map/ppermute | solution.py:327
  39.8 3.4 %frozen_blocks.7.refs_2_ = f32[4,128,384]{2,1,0:T(8,128)} custom-call(f32[256,1024]{1,0:T(8,128)S(1)} %get-tuple-element.49.refs_0_.refs_3_, bf16[1024,8192]{1,0:T(8,128)(2,1)} %refs_1_.12, f32[32,1024]{1,0:T(8,128)S(1)} %collective-permute-done.8.refs_2_.refs_1_.refs_6_, f32[32,1024]{1,0:T(8,128)S(1)} %collective-permute-done.9.refs_3_.refs_1_.refs_7_, ...), custom_call_target="tpu_custom_call" | custom-call | tf_op jit(solution)/shard_map/frozen_blocks/pallas_call | solution.py:76
  45.3 3.4 %frozen_blocks.9.refs_3_.refs_0_ = f32[4,128,384]{2,1,0:T(8,128)} custom-call(f32[256,1024]{1,0:T(8,128)S(1)} %get-tuple-element.49.refs_0_.refs_3_, bf16[1024,8192]{1,0:T(8,128)(2,1)} %refs_1_.12, f32[32,1024]{1,0:T(8,128)S(1)} %collective-permute-done.8.refs_2_.refs_1_.refs_6_, f32[32,1024]{1,0:T(8,128)S(1)} %collective-permute-done.9.refs_3_.refs_1_.refs_7_, ...), custom_call_target="tpu_custom_call" | custom-call | tf_op jit(solution)/shard_map/frozen_blocks/pallas_call | solution.py:76
  52.4 4.2 %collective-permute-done.13.refs_3_ = f32[32,1024]{1,0:T(8,128)S(1)} collective-permute-done((f32[32,1024]{1,0:T(8,128)S(1)}, f32[32,1024]{1,0:T(8,128)S(1)}, u32[]{:S(2)}, u32[]{:S(2)}) %collective-permute-start.13) | collective-permute-done | bytes 131104 | tf_op jit(solution)/shard_map/ppermute | solution.py:327
  56.6 2.7 %change.1 = (f32[32,1024]{1,0:T(8,128)S(1)}, f32[32,1024]{1,0:T(8,128)S(1)}, f32[32,1024]{1,0:T(8,128)S(1)}, f32[32,1024]{1,0:T(8,128)S(1)}, f32[32,1024]{1,0:T(...) custom-call(f32[32,1024]{1,0:T(8,128)S(1)} %get-tuple-element.51.refs_0_, ...), custom_call_target="tpu_custom_call" | custom-call | tf_op jit(solution)/shard_map/change/pallas_call | solution.py:76
  62.4 2.2 %collective-permute-start.16 = (f32[32,1024]{1,0:T(8,128)S(1)}, f32[32,1024]{1,0:T(8,128)S(1)}, u32[]{:S(2)}, u32[]{:S(2)}) collective-permute-start(f32[32,1024]{1,0:T(8,128)S(1)} %get-tuple-element.61), channel_id=1, source_target_pairs={{0,14},{2,12},{4,10},{6,8},{8,6},{10,4},{12,2},{14,0},{1,15},{3,13... | collective-permute-start | bytes 393224 | tf_op jit(solution)/shard_map/ppermute | solution.py:327
  64.8 2.6 %collective-permute-done.15.refs_2_.refs_1_.refs_3_.refs_12_ = f32[32,1024]{1,0:T(8,128)S(1)} collective-permute-done((f32[32,1024]{1,0:T(8,128)S(1)}, f32[32,1024]{1,0:T(8,128)S(1)}, u32[]{:S(2)}, u32[]{:S(2)}) %collective-permute-start.15) | collective-permute-done | bytes 131104 | tf_op jit(solution)/shard_map/ppermute | solution.py:327
  70.2 10.6 %collective-permute-done.17.refs_5_.refs_4_.refs_3_.refs_1_ = f32[32,1024]{1,0:T(8,128)S(1)} collective-permute-done((f32[32,1024]{1,0:T(8,128)S(1)}, f32[32,1024]{1,0:T(8,128)S(1)}, u32[]{:S(2)}, u32[]{:S(2)}) %collective-permute-start.17) | collective-permute-done | bytes 131104 | tf_op jit(solution)/shard_map/ppermute | solution.py:327
  80.8 3.4 %frozen_blocks.11.refs_2_ = f32[4,128,384]{2,1,0:T(8,128)} custom-call(f32[256,1024]{1,0:T(8,128)S(1)} %get-tuple-element.49.refs_0_.refs_3_, bf16[1024,8192]{1,0:T(8,128)(2,1)} %refs_1_.12, f32[32,1024]{1,0:T(8,128)S(1)} %collective-permute-done.15.refs_2_.refs_1_.refs_3_.refs_12_, ...), custom_call_target="tpu_custom_call" | custom-call | tf_op jit(solution)/shard_map/frozen_blocks/pallas_call | solution.py:76
  84.5 2.1 %merge.8 = (f32[2,128,384]{2,1,0:T(8,128)}, f32[2,128,384]{2,1,0:T(8,128)}) custom-call(f32[4,128,384]{2,1,0:T(8,128)} %frozen_blocks.9.refs_3_.refs_0_, f32[4,128,384]{2,1,0:T(8,128)S(1)} %collective-permute-done.21.refs_1_, f32[32,1024]{1,0:T(8,128)S(1)} %collective-permute-done.15.refs_2_.refs_1_.refs_3_.refs_12_, ...), custom_call_target="tpu_custom_call" | custom-call | tf_op jit(solution)/shard_map/merge/pallas_call | solution.py:76
  88.5 3.4 %state.1 = (f32[1,16,8192]{2,1,0:T(8,128)}, f32[1,16,8192]{2,1,0:T(8,128)}, f32[1,16,8192]{2,1,0:T(8,128)}, f32[1,16,8192]{2,1,0:T(8,128)}) custom-call(f32[32,1024]{1,0:T(8,128)S(1)} %get-tuple-element.51.refs_0_, f32[32,1024]{1,0:T(8,128)S(1)} %collective-permute-done.7.refs_4_.refs_1_, f32[32,1024]{1,0:T(8,128)S(1)} %collective-permute-done.10.refs_2_, ...), custom_call_target="tpu_custom_call" | custom-call | tf_op jit(solution)/shard_map/state/pallas_call | solution.py:76
  91.9 2.5 %collective-permute-start.28 = (f32[32,1024]{1,0:T(8,128)S(1)}, f32[32,1024]{1,0:T(8,128)S(1)}, u32[]{:S(2)}, u32[]{:S(2)}) collective-permute-start(f32[32,1024]{1,0:T(8,128)S(1)} %gate.13), channel_id=1, source_target_pairs={{0,10},{2,8},{4,14},{6,12},{8,2},{10,0},{12,6},{14,4},{1,11},{3,9}... | collective-permute-start | bytes 393224 | tf_op jit(solution)/shard_map/ppermute | solution.py:327
  94.4 3.4 %frozen_blocks.10.refs_0_.refs_3_ = f32[4,128,384]{2,1,0:T(8,128)} custom-call(f32[256,1024]{1,0:T(8,128)S(1)} %get-tuple-element.49.refs_0_.refs_3_, bf16[1024,8192]{1,0:T(8,128)(2,1)} %refs_1_.12, f32[32,1024]{1,0:T(8,128)S(1)} %collective-permute-done.15.refs_2_.refs_1_.refs_3_.refs_12_, ...), custom_call_target="tpu_custom_call" | custom-call | tf_op jit(solution)/shard_map/frozen_blocks/pallas_call | solution.py:76
  100.9 3.2 %collective-permute-done.24.refs_1_ = f32[4,128,384]{2,1,0:T(8,128)S(1)} collective-permute-done((f32[4,128,384]{2,1,0:T(8,128)}, f32[4,128,384]{2,1,0:T(8,128)S(1)}, u32[]{:S(2)}, u32[]{:S(2)}) %collective-permute-start.24) | collective-permute-done | bytes 786464 | tf_op jit(solution)/shard_map/ppermute | solution.py:327
  117.4 11.0 %collective-permute-done.23.refs_1_ = f32[1,128,384]{2,1,0:T(8,128)S(1)} collective-permute-done((f32[1,128,384]{2,1,0:T(8,128)}, f32[1,128,384]{2,1,0:T(8,128)S(1)}, u32[]{:S(2)}, u32[]{:S(2)}) %collective-permute-start.23) | collective-permute-done | bytes 196640 | tf_op jit(solution)/shard_map/ppermute | solution.py:327
  130.1 3.0 %update.1 = (bf16[16,16,1024]{2,1,0:T(8,128)(2,1)}, bf16[16,16,1024]{2,1,0:T(8,128)(2,1)}) custom-call(s32[16]{0:T(128)S(1)} %select_reduce_fusion.refs_0_, bf16[16,16,1024]{2,1,0:T(8,128)(2,1)} %refs_1_.13, bf16[16,16,1024]{2,1,0:T(8,128)(2,1)} %refs_2_.3, f32[4,32,1024]{2,1,0:T(8,128)S(1)} %pack.2.refs_3_, ...), custom_call_target="tpu_custom_call" | custom-call | tf_op jit(solution)/shard_map/update/pallas_call | solution.py:76
  (83 shorter events, 45.5 us)
Async XLA Ops:
  2.7 18.9 %collective-permute-start.6 = (f32[256,1024]{1,0:T(8,128)S(1)}, f32[256,1024]{1,0:T(8,128)S(1)}, u32[]{:S(2)}, u32[]{:S(2)}) collective-permute-start(f32[256,1024]{1,0:T(8,128)S(1)} %get-tuple-element.49.refs_0_.refs_3_), channel_id=1, source_target_pairs={{0,1},{1,0},{2,3},{3,2},{4,5},{5,4},{6,7},{7,6},{8,9},{9,8},{10,11... | collective-permute-start | bytes 3145736 | tf_op jit(solution)/shard_map/ppermute | solution.py:327
  12.5 36.2 %collective-permute-start.12 = (f32[4,128,256]{2,1,0:T(8,128)}, f32[4,128,256]{2,1,0:T(8,128)S(1)}, u32[]{:S(2)}, u32[]{:S(2)}) collective-permute-start(f32[4,128,256]{2,1,0:T(8,128)} %frozen_blocks.6.refs_4_), channel_id=1, source_target_pairs={{0,2},{2,0},{4,6},{6,4},{8,10},{10,8},{12,14},{14,12},{1,3},{3,1},... | collective-permute-start | bytes 1572872 | tf_op jit(solution)/shard_map/ppermute | solution.py:327
  23.4 15.5 %collective-permute-start.9 = (f32[32,1024]{1,0:T(8,128)S(1)}, f32[32,1024]{1,0:T(8,128)S(1)}, u32[]{:S(2)}, u32[]{:S(2)}) collective-permute-start(f32[32,1024]{1,0:T(8,128)S(1)} %get-tuple-element.55), channel_id=1, source_target_pairs={{0,14},{2,12},{4,10},{6,8},{8,6},{10,4},{12,2},{14,0},{1,15},{3,13... | collective-permute-start | bytes 393224 | tf_op jit(solution)/shard_map/ppermute | solution.py:327
  26.7 13.1 %collective-permute-start.7 = (f32[32,1024]{1,0:T(8,128)S(1)}, f32[32,1024]{1,0:T(8,128)S(1)}, u32[]{:S(2)}, u32[]{:S(2)}) collective-permute-start(f32[32,1024]{1,0:T(8,128)S(1)} %get-tuple-element.52), channel_id=1, source_target_pairs={{0,2},{2,0},{4,6},{6,4},{8,10},{10,8},{12,14},{14,12},{1,3},{3,1},... | collective-permute-start | bytes 393224 | tf_op jit(solution)/shard_map/ppermute | solution.py:327
  32.2 13.1 %collective-permute-start.11 = (f32[32,1024]{1,0:T(8,128)S(1)}, f32[32,1024]{1,0:T(8,128)S(1)}, u32[]{:S(2)}, u32[]{:S(2)}) collective-permute-start(f32[32,1024]{1,0:T(8,128)S(1)} %gate.9), channel_id=1, source_target_pairs={{0,8},{2,10},{4,12},{6,14},{8,0},{10,2},{12,4},{14,6},{1,9},{3,11}... | collective-permute-start | bytes 393224 | tf_op jit(solution)/shard_map/ppermute | solution.py:327
  39.0 13.5 %collective-permute-start.14 = (f32[32,1024]{1,0:T(8,128)S(1)}, f32[32,1024]{1,0:T(8,128)S(1)}, u32[]{:S(2)}, u32[]{:S(2)}) collective-permute-start(f32[32,1024]{1,0:T(8,128)S(1)} %gate.11), channel_id=1, source_target_pairs={{0,10},{2,8},{4,14},{6,12},{8,2},{10,0},{12,6},{14,4},{1,11},{3,9}... | collective-permute-start | bytes 393224 | tf_op jit(solution)/shard_map/ppermute | solution.py:327
  43.2 9.2 %collective-permute-start.10 = (f32[32,1024]{1,0:T(8,128)S(1)}, f32[32,1024]{1,0:T(8,128)S(1)}, u32[]{:S(2)}, u32[]{:S(2)}) collective-permute-start(f32[32,1024]{1,0:T(8,128)S(1)} %gate.8), channel_id=1, source_target_pairs={{0,4},{2,6},{4,0},{6,2},{8,12},{10,14},{12,8},{14,10},{1,5},{3,7},... | collective-permute-start | bytes 393224 | tf_op jit(solution)/shard_map/ppermute | solution.py:327
  50.9 16.6 %collective-permute-start.18 = (f32[2,128,256]{2,1,0:T(8,128)}, f32[2,128,256]{2,1,0:T(8,128)S(1)}, u32[]{:S(2)}, u32[]{:S(2)}) collective-permute-start(f32[2,128,256]{2,1,0:T(8,128)} %get-tuple-element.58.refs_2_), channel_id=1, source_target_pairs={{0,4},{2,6},{4,0},{6,2},{8,12},{10,14},{12,8},{14,10},{1,5},{3,7},... | collective-permute-start | bytes 786440 | tf_op jit(solution)/shard_map/ppermute | solution.py:327
  59.3 8.2 %collective-permute-start.15 = (f32[32,1024]{1,0:T(8,128)S(1)}, f32[32,1024]{1,0:T(8,128)S(1)}, u32[]{:S(2)}, u32[]{:S(2)}) collective-permute-start(f32[32,1024]{1,0:T(8,128)S(1)} %get-tuple-element.60), channel_id=1, source_target_pairs={{0,12},{2,14},{4,8},{6,10},{8,4},{10,6},{12,0},{14,2},{1,13},{3,15... | collective-permute-start | bytes 393224 | tf_op jit(solution)/shard_map/ppermute | solution.py:327
  60.4 24.1 %collective-permute-start.21 = (f32[4,128,384]{2,1,0:T(8,128)S(1)}, f32[4,128,384]{2,1,0:T(8,128)S(1)}, u32[]{:S(2)}, u32[]{:S(2)}) collective-permute-start(f32[4,128,384]{2,1,0:T(8,128)S(1)} %copy-done.1), channel_id=1, source_target_pairs={{0,2},{2,0},{4,6},{6,4},{8,10},{10,8},{12,14},{14,12},{1,3},{3,1},... | collective-permute-start | bytes 2359304 | tf_op jit(solution)/shard_map/ppermute | solution.py:327
  62.4 7.8 %collective-permute-start.16 = (f32[32,1024]{1,0:T(8,128)S(1)}, f32[32,1024]{1,0:T(8,128)S(1)}, u32[]{:S(2)}, u32[]{:S(2)}) collective-permute-start(f32[32,1024]{1,0:T(8,128)S(1)} %get-tuple-element.61), channel_id=1, source_target_pairs={{0,14},{2,12},{4,10},{6,8},{8,6},{10,4},{12,2},{14,0},{1,15},{3,13... | collective-permute-start | bytes 393224 | tf_op jit(solution)/shard_map/ppermute | solution.py:327
  64.6 16.2 %collective-permute-start.17 = (f32[32,1024]{1,0:T(8,128)S(1)}, f32[32,1024]{1,0:T(8,128)S(1)}, u32[]{:S(2)}, u32[]{:S(2)}) collective-permute-start(f32[32,1024]{1,0:T(8,128)S(1)} %get-tuple-element.62), channel_id=1, source_target_pairs={{0,2},{2,0},{4,6},{6,4},{8,10},{10,8},{12,14},{14,12},{1,3},{3,1},... | collective-permute-start | bytes 393224 | tf_op jit(solution)/shard_map/ppermute | solution.py:327
  69.2 11.6 %collective-permute-start.19 = (f32[32,1024]{1,0:T(8,128)S(1)}, f32[32,1024]{1,0:T(8,128)S(1)}, u32[]{:S(2)}, u32[]{:S(2)}) collective-permute-start(f32[32,1024]{1,0:T(8,128)S(1)} %gate.12), channel_id=1, source_target_pairs={{0,8},{2,10},{4,12},{6,14},{8,0},{10,2},{12,4},{14,6},{1,9},{3,11}... | collective-permute-start | bytes 393224 | tf_op jit(solution)/shard_map/ppermute | solution.py:327
  84.2 19.9 %collective-permute-start.24 = (f32[4,128,384]{2,1,0:T(8,128)}, f32[4,128,384]{2,1,0:T(8,128)S(1)}, u32[]{:S(2)}, u32[]{:S(2)}) collective-permute-start(f32[4,128,384]{2,1,0:T(8,128)} %frozen_blocks.11.refs_2_), channel_id=1, source_target_pairs={{0,2},{2,0},{4,6},{6,4},{8,10},{10,8},{12,14},{14,12},{1,3},{3,1},... | collective-permute-start | bytes 2359304 | tf_op jit(solution)/shard_map/ppermute | solution.py:327
  86.7 23.3 %collective-permute-start.22 = (f32[2,128,384]{2,1,0:T(8,128)}, f32[2,128,384]{2,1,0:T(8,128)S(1)}, u32[]{:S(2)}, u32[]{:S(2)}) collective-permute-start(f32[2,128,384]{2,1,0:T(8,128)} %get-tuple-element.68.refs_2_), channel_id=1, source_target_pairs={{0,4},{2,6},{4,0},{6,2},{8,12},{10,14},{12,8},{14,10},{1,5},{3,7},... | collective-permute-start | bytes 1179656 | tf_op jit(solution)/shard_map/ppermute | solution.py:327
  86.7 19.5 %collective-permute-start.20 = (f32[1,128,256]{2,1,0:T(8,128)S(1)}, f32[1,128,256]{2,1,0:T(8,128)S(1)}, u32[]{:S(2)}, u32[]{:S(2)}) collective-permute-start(f32[1,128,256]{2,1,0:T(8,128)S(1)} %copy-done.2), channel_id=1, source_target_pairs={{0,8},{2,10},{4,12},{6,14},{8,0},{10,2},{12,4},{14,6},{1,9},{3,11}... | collective-permute-start | bytes 393224 | tf_op jit(solution)/shard_map/ppermute | solution.py:327
  91.9 19.9 %collective-permute-start.28 = (f32[32,1024]{1,0:T(8,128)S(1)}, f32[32,1024]{1,0:T(8,128)S(1)}, u32[]{:S(2)}, u32[]{:S(2)}) collective-permute-start(f32[32,1024]{1,0:T(8,128)S(1)} %gate.13), channel_id=1, source_target_pairs={{0,10},{2,8},{4,14},{6,12},{8,2},{10,0},{12,6},{14,4},{1,11},{3,9}... | collective-permute-start | bytes 393224 | tf_op jit(solution)/shard_map/ppermute | solution.py:327
  99.2 12.7 %collective-permute-start.30 = (f32[32,1024]{1,0:T(8,128)S(1)}, f32[32,1024]{1,0:T(8,128)S(1)}, u32[]{:S(2)}, u32[]{:S(2)}) collective-permute-start(f32[32,1024]{1,0:T(8,128)S(1)} %gate.15), channel_id=1, source_target_pairs={{0,6},{2,4},{4,2},{6,0},{8,14},{10,12},{12,10},{14,8},{1,7},{3,5},... | collective-permute-start | bytes 393224 | tf_op jit(solution)/shard_map/ppermute | solution.py:327
  104.1 7.8 %collective-permute-start.29 = (f32[32,1024]{1,0:T(8,128)S(1)}, f32[32,1024]{1,0:T(8,128)S(1)}, u32[]{:S(2)}, u32[]{:S(2)}) collective-permute-start(f32[32,1024]{1,0:T(8,128)S(1)} %gate.14), channel_id=1, source_target_pairs={{0,4},{2,6},{4,0},{6,2},{8,12},{10,14},{12,8},{14,10},{1,5},{3,7},... | collective-permute-start | bytes 393224 | tf_op jit(solution)/shard_map/ppermute | solution.py:327
  106.2 8.3 %collective-permute-start.25 = (f32[2,128,384]{2,1,0:T(8,128)}, f32[2,128,384]{2,1,0:T(8,128)S(1)}, u32[]{:S(2)}, u32[]{:S(2)}) collective-permute-start(f32[2,128,384]{2,1,0:T(8,128)} %get-tuple-element.72), channel_id=1, source_target_pairs={{0,4},{2,6},{4,0},{6,2},{8,12},{10,14},{12,8},{14,10},{1,5},{3,7},... | collective-permute-start | bytes 1179656 | tf_op jit(solution)/shard_map/ppermute | solution.py:327
  109.9 20.2 %collective-permute-start.27 = (f32[4,32,1024]{2,1,0:T(8,128)S(1)}, f32[4,32,1024]{2,1,0:T(8,128)S(1)}, u32[]{:S(2)}, u32[]{:S(2)}) collective-permute-start(f32[4,32,1024]{2,1,0:T(8,128)S(1)} %pack.2.refs_3_), channel_id=1, source_target_pairs={{0,1},{1,0},{2,3},{3,2},{4,5},{5,4},{6,7},{7,6},{8,9},{9,8},{10,11... | collective-permute-start | bytes 1572872 | tf_op jit(solution)/shard_map/ppermute | solution.py:327
  111.9 18.2 %collective-permute-start.31 = (f32[4,32,1024]{2,1,0:T(8,128)S(1)}, f32[4,32,1024]{2,1,0:T(8,128)S(1)}, u32[]{:S(2)}, u32[]{:S(2)}) collective-permute-start(f32[4,32,1024]{2,1,0:T(8,128)S(1)} %pack.3.refs_5_), channel_id=1, source_target_pairs={{0,1},{1,0},{2,3},{3,2},{4,5},{5,4},{6,7},{7,6},{8,9},{9,8},{10,11... | collective-permute-start | bytes 1572872 | tf_op jit(solution)/shard_map/ppermute | solution.py:327
  112.5 16.0 %collective-permute-start.23 = (f32[1,128,384]{2,1,0:T(8,128)}, f32[1,128,384]{2,1,0:T(8,128)S(1)}, u32[]{:S(2)}, u32[]{:S(2)}) collective-permute-start(f32[1,128,384]{2,1,0:T(8,128)} %get-tuple-element.70.refs_5_), channel_id=1, source_target_pairs={{0,8},{2,10},{4,12},{6,14},{8,0},{10,2},{12,4},{14,6},{1,9},{3,11}... | collective-permute-start | bytes 589832 | tf_op jit(solution)/shard_map/ppermute | solution.py:327
  116.3 16.8 %collective-permute-start.26 = (f32[1,128,384]{2,1,0:T(8,128)}, f32[1,128,384]{2,1,0:T(8,128)S(1)}, u32[]{:S(2)}, u32[]{:S(2)}) collective-permute-start(f32[1,128,384]{2,1,0:T(8,128)} %get-tuple-element.74), channel_id=1, source_target_pairs={{0,8},{2,10},{4,12},{6,14},{8,0},{10,2},{12,4},{14,6},{1,9},{3,11}... | collective-permute-start | bytes 589832 | tf_op jit(solution)/shard_map/ppermute | solution.py:327
  (12 other events, 139.5 us)

commit v3 on v2

--- a/solution.py
+++ b/solution.py
@@ -37,11 +37,11 @@
 hbm_type = type(pltpu.HBM((8,), f32))
 
 
-def call(body, outs, *args, specs=None, scratch=(), name=None, after=()):
+def call(body, outs, *args, specs=None, scratch=(), name=None, after=(), stage=True):
     flat, tree = jax.tree.flatten(outs)
     specs = [vmem] * len(args) if specs is None else list(specs)
     far = [i for i, x in enumerate(args) if isinstance(x, Far)]
-    back = [i for i, out in enumerate(flat) if isinstance(out, hbm_type)]
+    back = [i for i, out in enumerate(flat) if stage and isinstance(out, hbm_type)]
     for i in far:
         specs[i] = hbm
     args = [in_hbm(x.array) if isinstance(x, Far) else x for x in args]
@@ -85,6 +85,19 @@
         name=name,
     )(*args, *after)
     return jax.tree.unflatten(tree, made)
+
+
+def release(x, after):
+    return pl.pallas_call(
+        lambda *refs: None,
+        in_specs=[anywhere] * (1 + len(after)),
+        out_specs=anywhere,
+        out_shape=jax.ShapeDtypeStruct(x.shape, x.dtype),
+        input_output_aliases={0: 0},
+        compiler_params=params(),
+        cost_estimate=pl.CostEstimate(flops=0, bytes_accessed=0, transcendentals=0),
+        name="release",
+    )(x, *after)
 
 
 class Far:
@@ -143,11 +156,11 @@
     ids_ref[...] = across[both:]
 
 
-def frozen_kernel(ks, first, rows_ref, weight_hbm, out_ref, weight_ref, sems):
+def frozen_kernel(ks, first, rows_ref, weight_hbm, out_hbm, weight_ref, out_ref, sems):
     count, tokens, width = out_ref.shape
     whole = weight_hbm.shape[1] // lax.axis_size("tensor")
     me = lax.axis_index("tensor")
-    copies = []
+    copies, stores = [], []
     for g, k in enumerate(ks):
         columns = pl.ds(pl.multiple_of((me ^ k) * whole + first, 128), width)
         copies.append(
@@ -159,11 +172,17 @@
         )
         copies[g].start()
     x = rows_ref[:tokens, :].astype(bf16)
-    for copy in copies:
-        copy.wait()
-    result = dot(x, weight_ref[...], NN)
-    for g in range(count):
-        out_ref[g] = result[:, g * width : (g + 1) * width]
+    step = max(count // 2, 1)
+    for start in range(0, count, step):
+        for g in range(start, start + step):
+            copies[g].wait()
+        result = dot(x, weight_ref[:, start * width : (start + step) * width], NN)
+        for g in range(start, start + step):
+            out_ref[g] = result[:, (g - start) * width : (g - start + 1) * width]
+            stores.append(pltpu.make_async_copy(out_ref.at[g], out_hbm.at[g], sems.at[count + g]))
+            stores[g].start()
+    for store in stores:
+        store.wait()
 
 
 def add_kernel(*refs):
@@ -177,10 +196,6 @@
     half = send_ref.shape[0]
     send_ref[...] = keep_ref[:half] + got_ref[:half]
     hold_ref[...] = keep_ref[half:] + got_ref[half:]
-
-
-def finish_kernel(keep_ref, got_ref, out_ref):
-    out_ref[...] = keep_ref[0] + got_ref[0]
 
 
 class Chunk:
@@ -194,18 +209,22 @@
         self.make = lambda ks, after: call(
             functools.partial(frozen_kernel, ks, first),
             pltpu.HBM((half, tokens, piece), f32), rows, weight,
-            specs=[vmem, hbm], name="frozen_blocks", after=after,
+            specs=[vmem, hbm], name="frozen_blocks", after=after, stage=False,
             scratch=[
                 pltpu.VMEM((weight.shape[0], half * piece), bf16),
-                pltpu.SemaphoreType.DMA((half,)),
+                pltpu.VMEM((half, tokens, piece), f32),
+                pltpu.SemaphoreType.DMA((2 * half,)),
             ],
         )
         self.halves = offsets[:half], offsets[half:]
 
     def send(self, *after):
         self.out = self.make(self.halves[0], after)
-        self.got = swap(self.out, "tensor", self.bits.pop(0))
         return in_hbm(self.out)
+
+    def go(self, *after):
+        out = release(self.out, after) if after else self.out
+        self.got = swap(out, "tensor", self.bits.pop(0))
 
     def keep(self, *after):
         self.hold = self.make(self.halves[1], after)
@@ -221,17 +240,17 @@
         self.merges -= 1
         return in_hbm(self.out)
 
-    def finish(self):
-        shape = pltpu.HBM(self.hold.shape[1:], f32)
-        self.sum = call(finish_kernel, shape, Far(self.hold), self.got, name="finish")
-        return in_hbm(self.sum)
-
-
-def project_kernel(pieces, adapter_ref, *refs):
+
+def project_kernel(pieces, tenants, ids_ref, sum_ref, up_ref, *refs):
     out_ref = refs[-1]
+    lowrank = sum_ref.shape[0] // 4
+    low = sum_ref[:lowrank, :] * adapter_scale
+    spread = [jnp.where(ids_ref[0:1].astype(jnp.int32) == t, low, 0.0) for t in range(tenants)]
+    lhs = jnp.concatenate(spread, axis=0).astype(bf16)
+    adapted = dot(lhs, up_ref[...].reshape(tenants * lowrank, up_ref.shape[2]), TN)
     for c, (first, piece) in enumerate(pieces):
         columns = slice(first, first + piece)
-        total = refs[c][...] + adapter_ref[:, columns]
+        total = refs[2 * c][0] + refs[2 * c + 1][0] + adapted[:, columns]
         out_ref[:, columns] = total.astype(bf16)
 
 
@@ -253,13 +272,6 @@
             ]
 
 
-def adapter_kernel(tenants, lowrank, ids_ref, sum_ref, up_ref, out_ref):
-    low = sum_ref[:lowrank, :] * adapter_scale
-    spread = [jnp.where(ids_ref[0:1].astype(jnp.int32) == t, low, 0.0) for t in range(tenants)]
-    lhs = jnp.concatenate(spread, axis=0).astype(bf16)
-    out_ref[...] = dot(lhs, up_ref[...], TN)
-
-
 def clip_factor(grads):
     total = grads[0][...] * grads[0][...]
     for ref in grads[1:]:
@@ -267,41 +279,34 @@
     return clip_norm / jnp.maximum(jnp.sqrt(jnp.sum(total, keepdims=True)), clip_norm)
 
 
-def moments_of(grads, state, factor, k, half):
-    both, width = grads[k].shape
+def change_kernel(parts, *refs):
+    grads, state, outs = refs[:parts], refs[parts : parts + 4], refs[parts + 4 : 2 * parts + 4]
+    state_hbm, sems = refs[2 * parts + 4 : 2 * parts + 8], refs[-1]
+    both, width = grads[0].shape
     lowrank = both // 2
-    rows = slice(half * lowrank, (half + 1) * lowrank)
-    columns = pl.ds(pl.multiple_of((lax.axis_index("tensor") ^ k) * width, width), width)
-    clipped = grads[k][rows, :] * factor
-    mean = beta_one * state[half][0, :, columns] + (1.0 - beta_one) * clipped
-    power = beta_two * state[2 + half][0, :, columns] + (1.0 - beta_two) * clipped * clipped
-    return rows, columns, mean, power
-
-
-def change_kernel(parts, *refs):
-    grads, state, outs = refs[:parts], refs[parts : parts + 4], refs[parts + 4 :]
     factor = clip_factor(grads)
+    places = []
     for k in range(parts):
+        columns = pl.ds(pl.multiple_of((lax.axis_index("tensor") ^ k) * width, width), width)
         for half in range(2):
-            rows, _, mean, power = moments_of(grads, state, factor, k, half)
-            outs[k][rows, :] = (mean * (learn_rate / correct_one)) / (
-                jnp.sqrt(power * (1.0 / correct_two)) + adam_eps
+            rows = slice(half * lowrank, (half + 1) * lowrank)
+            places.append((k, half, rows, columns))
+            clipped = grads[k][rows, :] * factor
+            state[half][0, :, columns] = (
+                beta_one * state[half][0, :, columns] + (1.0 - beta_one) * clipped
             )
-
-
-def state_kernel(parts, *refs):
-    grads, state = refs[:parts], refs[parts : parts + 4]
-    means, powers = refs[parts + 4 : parts + 6], refs[parts + 6 : parts + 8]
-    factor = clip_factor(grads)
-    for k in range(parts):
-        for half in range(2):
-            _, columns, mean, power = moments_of(grads, state, factor, k, half)
-            means[half][0, :, columns] = mean
-            powers[half][0, :, columns] = power
-
-
-def gate_kernel(x_ref, out_ref):
-    out_ref[...] = x_ref[...]
+            state[2 + half][0, :, columns] = (
+                beta_two * state[2 + half][0, :, columns] + (1.0 - beta_two) * clipped * clipped
+            )
+    stores = [pltpu.make_async_copy(state[i], state_hbm[i], sems.at[i]) for i in range(4)]
+    for store in stores:
+        store.start()
+    for k, half, rows, columns in places:
+        outs[k][rows, :] = (state[half][0, :, columns] * (learn_rate / correct_one)) / (
+            jnp.sqrt(state[2 + half][0, :, columns] * (1.0 / correct_two)) + adam_eps
+        )
+    for store in stores:
+        store.wait()
 
 
 def pack_kernel(*refs):
@@ -383,13 +388,14 @@
     rows_other = swap(rows, "dp", 1)
 
     units = width // 128
-    cuts = sorted({0, (units + 1) // 4 or 1, (5 * units + 4) // 8, units})
+    cuts = sorted({0, (3 * units + 4) // 8 or 1, (6 * units + 4) // 8, units})
     pieces = [(128 * a, 128 * (b - a)) for a, b in zip(cuts, cuts[1:])]
     frozen = [
         Chunk(rows, frozen_weight, tokens, parts, first, piece) for first, piece in pieces
     ]
 
     sent = frozen[0].send(rank_sum)
+    frozen[0].go()
 
     done = 1
     while done < len(bits):
@@ -408,98 +414,79 @@
 
     order = sorted(range(2, parts), key=lambda k: (-(k // 2), k))
     order.insert(2, 1)
-    flight = 3
-
-    def exchange(made, beside):
-        arrived = {0: made[0]}
+
+    def exchange(made, beside, arrived, flight):
         for n, k in enumerate(order):
             x = made[k]
             if n >= flight:
                 ready = [arrived[j] for j in order[: n - flight + 1]]
-                x = call(
-                    gate_kernel, block, x, name="gate",
-                    after=ready[-1:] + beside(n - flight, ready),
-                )
+                x = release(x, ready[-1:] + beside(n - flight, ready))
             arrived[k] = swap(x, "tensor", k)
-        return arrived
 
     early, late = frozen[:-1], frozen[-1]
-    extra = {}
+    second = early[1:]
 
     def beside_gradients(n, ready):
         if n == 0:
+            return [chunk.send(*ready) for chunk in second]
+        if n == 1:
             return [early[0].keep(*ready)]
         if n == 2:
-            return [chunk.send(*ready) for chunk in early[1:]]
-        if n == 3:
-            return [early[0].merge(*ready)] + [chunk.keep(*ready) for chunk in early[1:]]
+            sent = early[0].merge(*ready)
+            for chunk in second:
+                chunk.go(sent, got[1])
+            return [sent]
         return []
 
-    got = exchange(grads, beside_gradients)
+    got = {0: grads[0]}
+    exchange(grads, beside_gradients, got, 4)
     own_grads = [got[k] for k in range(parts)]
-    change = call(
-        functools.partial(change_kernel, parts), [block] * parts, *own_grads, *state,
-        name="change",
-    )
+    made = call(
+        functools.partial(change_kernel, parts),
+        [block] * parts + [pltpu.HBM(momentum_down.shape, f32)] * 4, *own_grads, *state,
+        name="change", stage=False, scratch=[pltpu.SemaphoreType.DMA((4,))],
+    )
+    change, (mean_down, mean_up, power_down, power_up) = made[:parts], made[parts:]
 
     def beside_changes(n, ready):
         if n == 0:
+            return [chunk.keep(*ready) for chunk in second] + [late.send(*ready)]
+        if n == 1:
+            late.go(back[1], *[chunk.got for chunk in second])
             mine = []
             while early[0].merges:
                 mine.append(early[0].merge(*ready))
             return mine
-        if n == 1:
-            extra["state"] = call(
-                functools.partial(state_kernel, parts),
-                [pltpu.HBM(momentum_down.shape, f32)] * 4,
-                *own_grads, *state, after=ready, name="state",
-            )
-            return [in_hbm(extra["state"][0])]
         if n == 2:
-            return [chunk.merge(*ready) for chunk in early[1:]]
-        if n == 3:
-            extra["adapter"] = call(
-                functools.partial(adapter_kernel, tenants, lowrank),
-                jax.ShapeDtypeStruct((tokens, width), f32),
-                ids, rank_sum, Far(adapter_up.reshape(tenants * lowrank, width)),
-                after=ready, name="adapter_result",
-            )
-            return [late.send(*ready), late.keep(*ready), extra["adapter"]]
+            return [chunk.merge(*ready) for chunk in second] + [late.keep(*ready)]
         return []
 
-    back = exchange(change, beside_changes)
-    mean_down, mean_up, power_down, power_up = extra["state"]
-    adapter_result = extra["adapter"]
-    beside = [early[0].finish()]
-    for chunk in early[1:]:
+    back = {0: change[0]}
+    exchange(change, beside_changes, back, 4)
+    last = back[order[-2]]
+    for chunk in second:
         while chunk.merges:
-            beside.append(chunk.merge())
-    arrive = [0] + order
-    groups = [arrive[: parts // 2], arrive[parts // 2 :]]
-    sides = []
-    for i, ks in enumerate(groups):
-        packed = call(
-            pack_kernel, jax.ShapeDtypeStruct((len(ks), 2 * lowrank, width), f32),
-            *[back[k] for k in ks], name="pack", after=beside if i else [],
-        )
-        sides += [packed, swap(packed, "dp", 1)]
+            last = chunk.merge(last)
+    late.merge(last, early[0].got, *[back[k] for k in order[3:]])
+    while late.merges:
+        late.merge(*[chunk.got for chunk in second])
+    packed = call(
+        pack_kernel, jax.ShapeDtypeStruct((parts, 2 * lowrank, width), f32),
+        *[back[k] for k in range(parts)], name="pack", after=[in_hbm(late.out)],
+    )
+    sides = [packed, swap(packed, "dp", 1)]
     updated_down, updated_up = call(
-        functools.partial(update_kernel, groups),
+        functools.partial(update_kernel, [range(parts)]),
         [pltpu.HBM(adapter_down.shape, bf16)] * 2,
         slot_tenant, Far(adapter_down), Far(adapter_up), *sides,
-        specs=[smem] + [vmem] * 6,
+        specs=[smem] + [vmem] * 4,
         name="update",
     )
-    for chunk in early[1:]:
-        chunk.finish()
-    while late.merges:
-        late.merge()
-    late.finish()
     projected = call(
-        functools.partial(project_kernel, pieces),
+        functools.partial(project_kernel, pieces, tenants),
         pltpu.HBM((tokens, width), bf16),
-        Far(adapter_result), *[Far(chunk.sum) for chunk in frozen],
-        name="project",
+        ids, rank_sum, Far(adapter_up), *[x for chunk in frozen for x in (Far(chunk.hold), chunk.got)],
+        name="project", after=[in_hbm(updated_down)],
     )
     return (projected, updated_down, updated_up, mean_down, mean_up, power_down, power_up)
 

time: 138 us -> 132 us (0.957)
  Pallas kernels: 50.4 us -> 40.2 us
  waiting for transfers between devices: 45.6 us -> 51.9 us
  starting transfers between devices: 39.6 us -> 38.2 us
    pallas_call x34 -> x20, Pallas kernels: 50.4 us -> 40.2 us  [call(): pl.pallas_call(kernel, in_specs=specs + [anywhere] * extra, out_specs=[hb...]
    ppermute x31 -> x30, waiting for transfers between devices: 44.5 us -> 50.8 us  [swap(): return lax.ppermute(x, axis, [(i, i ^ bits) for i in range(size)])]
    ppermute x31 -> x30, starting transfers between devices: 37 us -> 35.5 us  [swap(): return lax.ppermute(x, axis, [(i, i ^ bits) for i in range(size)])]
  transfers between devices with their start and end apart: 32 -> 31, of which waited for: 13 -> 20; matrix products, arithmetic and copies ran while one was open for 0% -> 0% of each run, Pallas kernels for 33% -> 23%
where the time goes in v3:
time: 132 us; the launch traced here: 131 us
  waiting for transfers between devices  51.9 us (39%)
  Pallas kernels  40.2 us (30%)
  starting transfers between devices  38.2 us (29%)
    ppermute x30, waiting for transfers between devices, swap(): return lax.ppermute(x, axis, [(i, i ^ bits) for i in range(size)])  50.8 us
    pallas_call x20, Pallas kernels, call(): pl.pallas_call(kernel, in_specs=specs + [anywhere] * extra, out_specs=[hb...  40.2 us
    ppermute x30, starting transfers between devices, swap(): return lax.ppermute(x, axis, [(i, i ^ bits) for i in range(size)])  35.5 us
    ppermute x1, starting transfers between devices, on_device(): lax.ppermute(rank_part, ('tensor', 'dp'), diagonal)  2.64 us
  transfers between devices with their start and end apart: 31, of which 20 were waited for; matrix products, arithmetic and copies ran while one was open for 0% of the time, Pallas kernels for 23%

profile of v3, /device:TPU:0, one launch (start us, length us, event | category | flops | bytes accessed | tf_op | source)
XLA Modules:
  0.0 131.4 jit_solution(7817594218885112905)
XLA Ops:
  3.2 2.6 %collective-permute-start.2 = (f32[40,128]{1,0:T(8,128)S(1)}, f32[40,128]{1,0:T(8,128)S(1)}, u32[]{:S(2)}, u32[]{:S(2)}) collective-permute-start(f32[40,128]{1,0:T(8,128)S(1)} %get-tuple-element.47.refs_0_), channel_id=1, source_target_pairs={{0,3},{1,2},{2,1},{3,0},{4,7},{5,6},{6,5},{7,4},{8,11},{9,10},{10,... | collective-permute-start | bytes 61448 | tf_op jit(solution)/shard_map/ppermute | solution.py:385
  7.3 2.4 %collective-permute-done.refs_1_ = f32[40,128]{1,0:T(8,128)S(1)} collective-permute-done((f32[40,128]{1,0:T(8,128)S(1)}, f32[40,128]{1,0:T(8,128)S(1)}, u32[]{:S(2)}, u32[]{:S(2)}) %collective-permute-start) | collective-permute-done | bytes 20512 | tf_op jit(solution)/shard_map/ppermute | solution.py:332
  9.7 3.1 %frozen_blocks.6.refs_4_ = f32[4,128,384]{2,1,0:T(8,128)} custom-call(f32[256,1024]{1,0:T(8,128)S(1)} %get-tuple-element.49.refs_0_.refs_3_, bf16[1024,8192]{1,0:T(8,128)(2,1)} %refs_1_.12, f32[64,128]{1,0:T(8,128)S(1)} %get-tuple-element.48.refs_2_.refs_0_), custom_call_target="tpu_custom_call" | custom-call | tf_op jit(solution)/shard_map/frozen_blocks/pallas_call | solution.py:76
  13.2 3.8 %collective-permute-start.5 = (f32[64,128]{1,0:T(8,128)S(1)}, f32[64,128]{1,0:T(8,128)S(1)}, u32[]{:S(2)}, u32[]{:S(2)}) collective-permute-start(f32[64,128]{1,0:T(8,128)S(1)} %get-tuple-element.48.refs_2_.refs_0_), channel_id=1, source_target_pairs={{0,12},{2,14},{4,8},{6,10},{8,4},{10,6},{12,0},{14,2},{1,13},{3,15... | collective-permute-start | bytes 98312 | tf_op jit(solution)/shard_map/ppermute | solution.py:332
  19.2 2.6 %collective-permute-done.4.refs_2_ = f32[64,128]{1,0:T(8,128)S(1)} collective-permute-done((f32[64,128]{1,0:T(8,128)S(1)}, f32[64,128]{1,0:T(8,128)S(1)}, u32[]{:S(2)}, u32[]{:S(2)}) %collective-permute-start.4) | collective-permute-done | bytes 32800 | tf_op jit(solution)/shard_map/ppermute | solution.py:332
  23.6 3.3 %collective-permute-start.8 = (f32[32,1024]{1,0:T(8,128)S(1)}, f32[32,1024]{1,0:T(8,128)S(1)}, u32[]{:S(2)}, u32[]{:S(2)}) collective-permute-start(f32[32,1024]{1,0:T(8,128)S(1)} %get-tuple-element.52), channel_id=1, source_target_pairs={{0,14},{2,12},{4,10},{6,8},{8,6},{10,4},{12,2},{14,0},{1,15},{3,13... | collective-permute-start | bytes 393224 | tf_op jit(solution)/shard_map/ppermute | solution.py:332
  29.6 3.1 %frozen_blocks.8.refs_2_.refs_0_ = f32[4,128,384]{2,1,0:T(8,128)} custom-call(f32[256,1024]{1,0:T(8,128)S(1)} %get-tuple-element.49.refs_0_.refs_3_, bf16[1024,8192]{1,0:T(8,128)(2,1)} %refs_1_.12, f32[32,1024]{1,0:T(8,128)S(1)} %collective-permute-done.7.refs_2_.refs_1_.refs_6_), custom_call_target="tpu_custom_call" | custom-call | tf_op jit(solution)/shard_map/frozen_blocks/pallas_call | solution.py:76
  32.7 3.2 %frozen_blocks.7.refs_0_.refs_2_ = f32[4,128,384]{2,1,0:T(8,128)} custom-call(f32[256,1024]{1,0:T(8,128)S(1)} %get-tuple-element.49.refs_0_.refs_3_, bf16[1024,8192]{1,0:T(8,128)(2,1)} %refs_1_.12, f32[32,1024]{1,0:T(8,128)S(1)} %collective-permute-done.7.refs_2_.refs_1_.refs_6_, f32[32,1024]{1,0:T(8,128)S(1)} %collective-permute-done.8.refs_3_.refs_1_.refs_7_), custom_call_target="tpu_custom_call" | custom-call | tf_op jit(solution)/shard_map/frozen_blocks/pallas_call | solution.py:76
  40.1 4.0 %collective-permute-start.14 = (f32[32,1024]{1,0:T(8,128)S(1)}, f32[32,1024]{1,0:T(8,128)S(1)}, u32[]{:S(2)}, u32[]{:S(2)}) collective-permute-start(f32[32,1024]{1,0:T(8,128)S(1)} %get-tuple-element.59), channel_id=1, source_target_pairs={{0,8},{2,10},{4,12},{6,14},{8,0},{10,2},{12,4},{14,6},{1,9},{3,11}... | collective-permute-start | bytes 393224 | tf_op jit(solution)/shard_map/ppermute | solution.py:332
  48.1 6.0 %collective-permute-done.13.refs_3_ = f32[32,1024]{1,0:T(8,128)S(1)} collective-permute-done((f32[32,1024]{1,0:T(8,128)S(1)}, f32[32,1024]{1,0:T(8,128)S(1)}, u32[]{:S(2)}, u32[]{:S(2)}) %collective-permute-start.13) | collective-permute-done | bytes 131104 | tf_op jit(solution)/shard_map/ppermute | solution.py:332
  55.6 3.4 %change.1 = (f32[32,1024]{1,0:T(8,128)S(1)}, f32[32,1024]{1,0:T(8,128)S(1)}, f32[32,1024]{1,0:T(8,128)S(1)}, f32[32,1024]{1,0:T(8,128)S(1)}, f32[32,1024]{1,0:T(...) custom-call(f32[32,1024]{1,0:T(8,128)S(1)} %get-tuple-element.56.ref, ...), custom_call_target="tpu_custom_call" | custom-call | tf_op jit(solution)/shard_map/change/pallas_call | solution.py:76
  64.4 2.9 %collective-permute-done.16.refs_2_.refs_1_.refs_6_ = f32[32,1024]{1,0:T(8,128)S(1)} collective-permute-done((f32[32,1024]{1,0:T(8,128)S(1)}, f32[32,1024]{1,0:T(8,128)S(1)}, u32[]{:S(2)}, u32[]{:S(2)}) %collective-permute-start.16) | collective-permute-done | bytes 131104 | tf_op jit(solution)/shard_map/ppermute | solution.py:332
  67.4 2.6 %frozen_blocks.11.refs_0_.refs_3_ = f32[4,128,256]{2,1,0:T(8,128)} custom-call(f32[256,1024]{1,0:T(8,128)S(1)} %get-tuple-element.49.refs_0_.refs_3_, bf16[1024,8192]{1,0:T(8,128)(2,1)} %refs_1_.12, f32[32,1024]{1,0:T(8,128)S(1)} %collective-permute-done.16.refs_2_.refs_1_.refs_6_), custom_call_target="tpu_custom_call" | custom-call | tf_op jit(solution)/shard_map/frozen_blocks/pallas_call | solution.py:76
  70.0 3.1 %frozen_blocks.9.refs_0_.refs_2_ = f32[4,128,384]{2,1,0:T(8,128)} custom-call(f32[256,1024]{1,0:T(8,128)S(1)} %get-tuple-element.49.refs_0_.refs_3_, bf16[1024,8192]{1,0:T(8,128)(2,1)} %refs_1_.12, f32[32,1024]{1,0:T(8,128)S(1)} %collective-permute-done.16.refs_2_.refs_1_.refs_6_), custom_call_target="tpu_custom_call" | custom-call | tf_op jit(solution)/shard_map/frozen_blocks/pallas_call | solution.py:76
  73.2 4.3 %collective-permute-done.17.refs_3_.refs_1_.refs_7_ = f32[32,1024]{1,0:T(8,128)S(1)} collective-permute-done((f32[32,1024]{1,0:T(8,128)S(1)}, f32[32,1024]{1,0:T(8,128)S(1)}, u32[]{:S(2)}, u32[]{:S(2)}) %collective-permute-start.17) | collective-permute-done | bytes 131104 | tf_op jit(solution)/shard_map/ppermute | solution.py:332
  84.3 2.9 %collective-permute-start.25 = (f32[32,1024]{1,0:T(8,128)S(1)}, f32[32,1024]{1,0:T(8,128)S(1)}, u32[]{:S(2)}, u32[]{:S(2)}) collective-permute-start(f32[32,1024]{1,0:T(8,128)S(1)} %get-tuple-element.71), channel_id=1, source_target_pairs={{0,8},{2,10},{4,12},{6,14},{8,0},{10,2},{12,4},{14,6},{1,9},{3,11}... | collective-permute-start | bytes 393224 | tf_op jit(solution)/shard_map/ppermute | solution.py:332
  87.2 2.6 %frozen_blocks.10.refs_3_.refs_0_ = f32[4,128,256]{2,1,0:T(8,128)} custom-call(f32[256,1024]{1,0:T(8,128)S(1)} %get-tuple-element.49.refs_0_.refs_3_, bf16[1024,8192]{1,0:T(8,128)(2,1)} %refs_1_.12, f32[32,1024]{1,0:T(8,128)S(1)} %collective-permute-done.16.refs_2_.refs_1_.refs_6_, f32[32,1024]{1,0:T(8,128)S(1)} %collective-permute-done.17.refs_3_.refs_1_.refs_7_, ...), custom_call_target="tpu_custom_call" | custom-call | tf_op jit(solution)/shard_map/frozen_blocks/pallas_call | solution.py:76
  89.8 7.2 %collective-permute-done.22.refs_2_.refs_6_ = f32[32,1024]{1,0:T(8,128)S(1)} collective-permute-done((f32[32,1024]{1,0:T(8,128)S(1)}, f32[32,1024]{1,0:T(8,128)S(1)}, u32[]{:S(2)}, u32[]{:S(2)}) %collective-permute-start.22) | collective-permute-done | bytes 131104 | tf_op jit(solution)/shard_map/ppermute | solution.py:332
  97.0 3.0 %collective-permute-start.27 = (f32[32,1024]{1,0:T(8,128)S(1)}, f32[32,1024]{1,0:T(8,128)S(1)}, u32[]{:S(2)}, u32[]{:S(2)}) collective-permute-start(f32[32,1024]{1,0:T(8,128)S(1)} %release.15), channel_id=1, source_target_pairs={{0,6},{2,4},{4,2},{6,0},{8,14},{10,12},{12,10},{14,8},{1,7},{3,5},... | collective-permute-start | bytes 393224 | tf_op jit(solution)/shard_map/ppermute | solution.py:332
  103.4 2.4 %collective-permute-done.26.refs_5_ = f32[32,1024]{1,0:T(8,128)S(1)} collective-permute-done((f32[32,1024]{1,0:T(8,128)S(1)}, f32[32,1024]{1,0:T(8,128)S(1)}, u32[]{:S(2)}, u32[]{:S(2)}) %collective-permute-start.26) | collective-permute-done | bytes 131104 | tf_op jit(solution)/shard_map/ppermute | solution.py:332
  109.3 8.5 %collective-permute-done.23.refs_2_.refs_6_ = f32[1,128,384]{2,1,0:T(8,128)S(1)} collective-permute-done((f32[1,128,384]{2,1,0:T(8,128)}, f32[1,128,384]{2,1,0:T(8,128)S(1)}, u32[]{:S(2)}, u32[]{:S(2)}) %collective-permute-start.23) | collective-permute-done | bytes 196640 | tf_op jit(solution)/shard_map/ppermute | solution.py:332
  122.6 3.0 %update.1 = (bf16[16,16,1024]{2,1,0:T(8,128)(2,1)}, bf16[16,16,1024]{2,1,0:T(8,128)(2,1)}) custom-call(s32[16]{0:T(128)S(1)} %select_reduce_fusion.refs_0_, bf16[16,16,1024]{2,1,0:T(8,128)(2,1)} %refs_1_.13, bf16[16,16,1024]{2,1,0:T(8,128)(2,1)} %refs_2_.5, f32[8,32,1024]{2,1,0:T(8,128)S(1)} %pack.1.refs_3_, f32[8,32,1024]{2,1,0:T(8,128)S(1)} %collective-permute-done.30.refs_4_), custom_call_target="tpu_custom_call" | custom-call | tf_op jit(solution)/shard_map/update/pallas_call | solution.py:76
  125.6 3.6 %collective-permute-done.29.refs_8_ = f32[1,128,256]{2,1,0:T(8,128)S(1)} collective-permute-done((f32[1,128,256]{2,1,0:T(8,128)}, f32[1,128,256]{2,1,0:T(8,128)S(1)}, u32[]{:S(2)}, u32[]{:S(2)}) %collective-permute-start.29) | collective-permute-done | bytes 131104 | tf_op jit(solution)/shard_map/ppermute | solution.py:332
  129.2 2.2 %project.1 = bf16[128,1024]{1,0:T(8,128)(2,1)} custom-call(f32[8,128]{1,0:T(8,128)S(1)} %get-tuple-element.46.refs_1_.refs_0_, f32[64,128]{1,0:T(8,128)S(1)} %rank_far.1.refs_0_.refs_1_, bf16[16,16,1024]{2,1,0:T(8,128)(2,1)} %refs_2_.5, f32[1,128,384]{2,1,0:T(8,128)} %get-tuple-element.63.refs_3_, ...), custom_call_target="tpu_custom_call" | custom-call | tf_op jit(solution)/shard_map/project/pallas_call | solution.py:76
  (73 shorter events, 44.4 us)
Async XLA Ops:
  2.7 19.1 %collective-permute-start.6 = (f32[256,1024]{1,0:T(8,128)S(1)}, f32[256,1024]{1,0:T(8,128)S(1)}, u32[]{:S(2)}, u32[]{:S(2)}) collective-permute-start(f32[256,1024]{1,0:T(8,128)S(1)} %get-tuple-element.49.refs_0_.refs_3_), channel_id=1, source_target_pairs={{0,1},{1,0},{2,3},{3,2},{4,5},{5,4},{6,7},{7,6},{8,9},{9,8},{10,11... | collective-permute-start | bytes 3145736 | tf_op jit(solution)/shard_map/ppermute | solution.py:332
  12.8 23.2 %collective-permute-start.9 = (f32[4,128,384]{2,1,0:T(8,128)}, f32[4,128,384]{2,1,0:T(8,128)S(1)}, u32[]{:S(2)}, u32[]{:S(2)}) collective-permute-start(f32[4,128,384]{2,1,0:T(8,128)} %frozen_blocks.6.refs_4_), channel_id=1, source_target_pairs={{0,2},{2,0},{4,6},{6,4},{8,10},{10,8},{12,14},{14,12},{1,3},{3,1},... | collective-permute-start | bytes 2359304 | tf_op jit(solution)/shard_map/ppermute | solution.py:332
  22.1 7.5 %collective-permute-start.7 = (f32[32,1024]{1,0:T(8,128)S(1)}, f32[32,1024]{1,0:T(8,128)S(1)}, u32[]{:S(2)}, u32[]{:S(2)}) collective-permute-start(f32[32,1024]{1,0:T(8,128)S(1)} %get-tuple-element.51), channel_id=1, source_target_pairs={{0,12},{2,14},{4,8},{6,10},{8,4},{10,6},{12,0},{14,2},{1,13},{3,15... | collective-permute-start | bytes 393224 | tf_op jit(solution)/shard_map/ppermute | solution.py:332
  23.6 9.1 %collective-permute-start.8 = (f32[32,1024]{1,0:T(8,128)S(1)}, f32[32,1024]{1,0:T(8,128)S(1)}, u32[]{:S(2)}, u32[]{:S(2)}) collective-permute-start(f32[32,1024]{1,0:T(8,128)S(1)} %get-tuple-element.52), channel_id=1, source_target_pairs={{0,14},{2,12},{4,10},{6,8},{8,6},{10,4},{12,2},{14,0},{1,15},{3,13... | collective-permute-start | bytes 393224 | tf_op jit(solution)/shard_map/ppermute | solution.py:332
  27.0 10.5 %collective-permute-start.10 = (f32[32,1024]{1,0:T(8,128)S(1)}, f32[32,1024]{1,0:T(8,128)S(1)}, u32[]{:S(2)}, u32[]{:S(2)}) collective-permute-start(f32[32,1024]{1,0:T(8,128)S(1)} %get-tuple-element.53), channel_id=1, source_target_pairs={{0,2},{2,0},{4,6},{6,4},{8,10},{10,8},{12,14},{14,12},{1,3},{3,1},... | collective-permute-start | bytes 393224 | tf_op jit(solution)/shard_map/ppermute | solution.py:332
  39.6 37.9 %collective-permute-start.19 = (f32[4,128,384]{2,1,0:T(8,128)S(1)}, f32[4,128,384]{2,1,0:T(8,128)S(1)}, u32[]{:S(2)}, u32[]{:S(2)}) collective-permute-start(f32[4,128,384]{2,1,0:T(8,128)S(1)} %release.11), channel_id=1, source_target_pairs={{0,2},{2,0},{4,6},{6,4},{8,10},{10,8},{12,14},{14,12},{1,3},{3,1},... | collective-permute-start | bytes 2359304 | tf_op jit(solution)/shard_map/ppermute | solution.py:332
  40.1 7.9 %collective-permute-start.14 = (f32[32,1024]{1,0:T(8,128)S(1)}, f32[32,1024]{1,0:T(8,128)S(1)}, u32[]{:S(2)}, u32[]{:S(2)}) collective-permute-start(f32[32,1024]{1,0:T(8,128)S(1)} %get-tuple-element.59), channel_id=1, source_target_pairs={{0,8},{2,10},{4,12},{6,14},{8,0},{10,2},{12,4},{14,6},{1,9},{3,11}... | collective-permute-start | bytes 393224 | tf_op jit(solution)/shard_map/ppermute | solution.py:332
  44.1 10.0 %collective-permute-start.13 = (f32[32,1024]{1,0:T(8,128)S(1)}, f32[32,1024]{1,0:T(8,128)S(1)}, u32[]{:S(2)}, u32[]{:S(2)}) collective-permute-start(f32[32,1024]{1,0:T(8,128)S(1)} %release.9), channel_id=1, source_target_pairs={{0,6},{2,4},{4,2},{6,0},{8,14},{10,12},{12,10},{14,8},{1,7},{3,5},... | collective-permute-start | bytes 393224 | tf_op jit(solution)/shard_map/ppermute | solution.py:332
  45.3 10.4 %collective-permute-start.12 = (f32[32,1024]{1,0:T(8,128)S(1)}, f32[32,1024]{1,0:T(8,128)S(1)}, u32[]{:S(2)}, u32[]{:S(2)}) collective-permute-start(f32[32,1024]{1,0:T(8,128)S(1)} %release.8), channel_id=1, source_target_pairs={{0,4},{2,6},{4,0},{6,2},{8,12},{10,14},{12,8},{14,10},{1,5},{3,7},... | collective-permute-start | bytes 393224 | tf_op jit(solution)/shard_map/ppermute | solution.py:332
  46.6 9.0 %collective-permute-start.15 = (f32[32,1024]{1,0:T(8,128)S(1)}, f32[32,1024]{1,0:T(8,128)S(1)}, u32[]{:S(2)}, u32[]{:S(2)}) collective-permute-start(f32[32,1024]{1,0:T(8,128)S(1)} %release.10), channel_id=1, source_target_pairs={{0,10},{2,8},{4,14},{6,12},{8,2},{10,0},{12,6},{14,4},{1,11},{3,9}... | collective-permute-start | bytes 393224 | tf_op jit(solution)/shard_map/ppermute | solution.py:332
  59.0 8.3 %collective-permute-start.16 = (f32[32,1024]{1,0:T(8,128)S(1)}, f32[32,1024]{1,0:T(8,128)S(1)}, u32[]{:S(2)}, u32[]{:S(2)}) collective-permute-start(f32[32,1024]{1,0:T(8,128)S(1)} %get-tuple-element.61), channel_id=1, source_target_pairs={{0,12},{2,14},{4,8},{6,10},{8,4},{10,6},{12,0},{14,2},{1,13},{3,15... | collective-permute-start | bytes 393224 | tf_op jit(solution)/shard_map/ppermute | solution.py:332
  60.2 20.2 %collective-permute-start.11 = (f32[2,128,384]{2,1,0:T(8,128)}, f32[2,128,384]{2,1,0:T(8,128)S(1)}, u32[]{:S(2)}, u32[]{:S(2)}) collective-permute-start(f32[2,128,384]{2,1,0:T(8,128)} %get-tuple-element.55.refs_2_.refs_1_), channel_id=1, source_target_pairs={{0,4},{2,6},{4,0},{6,2},{8,12},{10,14},{12,8},{14,10},{1,5},{3,7},... | collective-permute-start | bytes 1179656 | tf_op jit(solution)/shard_map/ppermute | solution.py:332
  61.6 15.9 %collective-permute-start.17 = (f32[32,1024]{1,0:T(8,128)S(1)}, f32[32,1024]{1,0:T(8,128)S(1)}, u32[]{:S(2)}, u32[]{:S(2)}) collective-permute-start(f32[32,1024]{1,0:T(8,128)S(1)} %get-tuple-element.62), channel_id=1, source_target_pairs={{0,14},{2,12},{4,10},{6,8},{8,6},{10,4},{12,2},{14,0},{1,15},{3,13... | collective-permute-start | bytes 393224 | tf_op jit(solution)/shard_map/ppermute | solution.py:332
  63.5 14.0 %collective-permute-start.20 = (f32[32,1024]{1,0:T(8,128)S(1)}, f32[32,1024]{1,0:T(8,128)S(1)}, u32[]{:S(2)}, u32[]{:S(2)}) collective-permute-start(f32[32,1024]{1,0:T(8,128)S(1)} %get-tuple-element.65), channel_id=1, source_target_pairs={{0,2},{2,0},{4,6},{6,4},{8,10},{10,8},{12,14},{14,12},{1,3},{3,1},... | collective-permute-start | bytes 393224 | tf_op jit(solution)/shard_map/ppermute | solution.py:332
  79.6 17.4 %collective-permute-start.21 = (f32[2,128,384]{2,1,0:T(8,128)}, f32[2,128,384]{2,1,0:T(8,128)S(1)}, u32[]{:S(2)}, u32[]{:S(2)}) collective-permute-start(f32[2,128,384]{2,1,0:T(8,128)} %get-tuple-element.67.refs_2_), channel_id=1, source_target_pairs={{0,4},{2,6},{4,0},{6,2},{8,12},{10,14},{12,8},{14,10},{1,5},{3,7},... | collective-permute-start | bytes 1179656 | tf_op jit(solution)/shard_map/ppermute | solution.py:332
  79.7 26.3 %collective-permute-start.24 = (f32[4,128,256]{2,1,0:T(8,128)S(1)}, f32[4,128,256]{2,1,0:T(8,128)S(1)}, u32[]{:S(2)}, u32[]{:S(2)}) collective-permute-start(f32[4,128,256]{2,1,0:T(8,128)S(1)} %release.13), channel_id=1, source_target_pairs={{0,2},{2,0},{4,6},{6,4},{8,10},{10,8},{12,14},{14,12},{1,3},{3,1},... | collective-permute-start | bytes 1572872 | tf_op jit(solution)/shard_map/ppermute | solution.py:332
  82.3 14.8 %collective-permute-start.22 = (f32[32,1024]{1,0:T(8,128)S(1)}, f32[32,1024]{1,0:T(8,128)S(1)}, u32[]{:S(2)}, u32[]{:S(2)}) collective-permute-start(f32[32,1024]{1,0:T(8,128)S(1)} %release.12), channel_id=1, source_target_pairs={{0,4},{2,6},{4,0},{6,2},{8,12},{10,14},{12,8},{14,10},{1,5},{3,7},... | collective-permute-start | bytes 393224 | tf_op jit(solution)/shard_map/ppermute | solution.py:332
  84.3 21.6 %collective-permute-start.18 = (f32[1,128,384]{2,1,0:T(8,128)}, f32[1,128,384]{2,1,0:T(8,128)S(1)}, u32[]{:S(2)}, u32[]{:S(2)}) collective-permute-start(f32[1,128,384]{2,1,0:T(8,128)} %get-tuple-element.64.refs_2_), channel_id=1, source_target_pairs={{0,8},{2,10},{4,12},{6,14},{8,0},{10,2},{12,4},{14,6},{1,9},{3,11}... | collective-permute-start | bytes 589832 | tf_op jit(solution)/shard_map/ppermute | solution.py:332
  84.3 19.2 %collective-permute-start.25 = (f32[32,1024]{1,0:T(8,128)S(1)}, f32[32,1024]{1,0:T(8,128)S(1)}, u32[]{:S(2)}, u32[]{:S(2)}) collective-permute-start(f32[32,1024]{1,0:T(8,128)S(1)} %get-tuple-element.71), channel_id=1, source_target_pairs={{0,8},{2,10},{4,12},{6,14},{8,0},{10,2},{12,4},{14,6},{1,9},{3,11}... | collective-permute-start | bytes 393224 | tf_op jit(solution)/shard_map/ppermute | solution.py:332
  97.0 8.8 %collective-permute-start.26 = (f32[32,1024]{1,0:T(8,128)S(1)}, f32[32,1024]{1,0:T(8,128)S(1)}, u32[]{:S(2)}, u32[]{:S(2)}) collective-permute-start(f32[32,1024]{1,0:T(8,128)S(1)} %release.14), channel_id=1, source_target_pairs={{0,10},{2,8},{4,14},{6,12},{8,2},{10,0},{12,6},{14,4},{1,11},{3,9}... | collective-permute-start | bytes 393224 | tf_op jit(solution)/shard_map/ppermute | solution.py:332
  97.0 9.0 %collective-permute-start.27 = (f32[32,1024]{1,0:T(8,128)S(1)}, f32[32,1024]{1,0:T(8,128)S(1)}, u32[]{:S(2)}, u32[]{:S(2)}) collective-permute-start(f32[32,1024]{1,0:T(8,128)S(1)} %release.15), channel_id=1, source_target_pairs={{0,6},{2,4},{4,2},{6,0},{8,14},{10,12},{12,10},{14,8},{1,7},{3,5},... | collective-permute-start | bytes 393224 | tf_op jit(solution)/shard_map/ppermute | solution.py:332
  107.9 10.2 %collective-permute-start.28 = (f32[2,128,256]{2,1,0:T(8,128)}, f32[2,128,256]{2,1,0:T(8,128)S(1)}, u32[]{:S(2)}, u32[]{:S(2)}) collective-permute-start(f32[2,128,256]{2,1,0:T(8,128)} %get-tuple-element.75), channel_id=1, source_target_pairs={{0,4},{2,6},{4,0},{6,2},{8,12},{10,14},{12,8},{14,10},{1,5},{3,7},... | collective-permute-start | bytes 786440 | tf_op jit(solution)/shard_map/ppermute | solution.py:332
  108.0 9.8 %collective-permute-start.23 = (f32[1,128,384]{2,1,0:T(8,128)}, f32[1,128,384]{2,1,0:T(8,128)S(1)}, u32[]{:S(2)}, u32[]{:S(2)}) collective-permute-start(f32[1,128,384]{2,1,0:T(8,128)} %get-tuple-element.70.refs_2_), channel_id=1, source_target_pairs={{0,8},{2,10},{4,12},{6,14},{8,0},{10,2},{12,4},{14,6},{1,9},{3,11}... | collective-permute-start | bytes 589832 | tf_op jit(solution)/shard_map/ppermute | solution.py:332
  119.9 9.2 %collective-permute-start.29 = (f32[1,128,256]{2,1,0:T(8,128)}, f32[1,128,256]{2,1,0:T(8,128)S(1)}, u32[]{:S(2)}, u32[]{:S(2)}) collective-permute-start(f32[1,128,256]{2,1,0:T(8,128)} %get-tuple-element.77.refs_8_), channel_id=1, source_target_pairs={{0,8},{2,10},{4,12},{6,14},{8,0},{10,2},{12,4},{14,6},{1,9},{3,11}... | collective-permute-start | bytes 393224 | tf_op jit(solution)/shard_map/ppermute | solution.py:332
  (10 other events, 92.3 us)

commit v4 on v3

--- a/solution.py
+++ b/solution.py
@@ -428,9 +428,9 @@
 
     def beside_gradients(n, ready):
         if n == 0:
+            return [early[0].keep(*ready)]
+        if n == 1:
             return [chunk.send(*ready) for chunk in second]
-        if n == 1:
-            return [early[0].keep(*ready)]
         if n == 2:
             sent = early[0].merge(*ready)
             for chunk in second:
@@ -453,12 +453,12 @@
             return [chunk.keep(*ready) for chunk in second] + [late.send(*ready)]
         if n == 1:
             late.go(back[1], *[chunk.got for chunk in second])
-            mine = []
+            return []
+        if n == 2:
+            mine = [chunk.merge(*ready) for chunk in second]
             while early[0].merges:
-                mine.append(early[0].merge(*ready))
-            return mine
-        if n == 2:
-            return [chunk.merge(*ready) for chunk in second] + [late.keep(*ready)]
+                mine.append(early[0].merge(*mine))
+            return mine + [late.keep(*mine)]
         return []
 
     back = {0: change[0]}

time: 132 us -> 128 us (0.970)
  waiting for transfers between devices: 51.9 us -> 47.5 us
    ppermute x30, waiting for transfers between devices: 50.8 us -> 46.5 us  [swap(): return lax.ppermute(x, axis, [(i, i ^ bits) for i in range(size)])]
  transfers between devices with their start and end apart: 31 -> 31, of which waited for: 20 -> 17; matrix products, arithmetic and copies ran while one was open for 0% -> 0% of each run, Pallas kernels for 23% -> 24%
where the time goes in v4:
time: 128 us
  waiting for transfers between devices  47.5 us (37%)
  Pallas kernels  40.1 us (31%)
  starting transfers between devices  38.9 us (30%)
    ppermute x30, waiting for transfers between devices, swap(): return lax.ppermute(x, axis, [(i, i ^ bits) for i in range(size)])  46.5 us
    pallas_call x20, Pallas kernels, call(): pl.pallas_call(kernel, in_specs=specs + [anywhere] * extra, out_specs=[hb...  40.1 us
    ppermute x30, starting transfers between devices, swap(): return lax.ppermute(x, axis, [(i, i ^ bits) for i in range(size)])  36.2 us
    ppermute x1, starting transfers between devices, on_device(): lax.ppermute(rank_part, ('tensor', 'dp'), diagonal)  2.64 us
  transfers between devices with their start and end apart: 31, of which 17 were waited for; matrix products, arithmetic and copies ran while one was open for 0% of the time, Pallas kernels for 24%

profile of v4, /device:TPU:0, one launch (start us, length us, event | category | flops | bytes accessed | tf_op | source)
XLA Modules:
  0.0 127.5 jit_solution(3923576076639983362)
XLA Ops:
  3.2 2.6 %collective-permute-start.2 = (f32[40,128]{1,0:T(8,128)S(1)}, f32[40,128]{1,0:T(8,128)S(1)}, u32[]{:S(2)}, u32[]{:S(2)}) collective-permute-start(f32[40,128]{1,0:T(8,128)S(1)} %get-tuple-element.47.refs_0_), channel_id=1, source_target_pairs={{0,3},{1,2},{2,1},{3,0},{4,7},{5,6},{6,5},{7,4},{8,11},{9,10},{10,... | collective-permute-start | bytes 61448 | tf_op jit(solution)/shard_map/ppermute | solution.py:385
  7.3 2.4 %collective-permute-done.refs_1_ = f32[40,128]{1,0:T(8,128)S(1)} collective-permute-done((f32[40,128]{1,0:T(8,128)S(1)}, f32[40,128]{1,0:T(8,128)S(1)}, u32[]{:S(2)}, u32[]{:S(2)}) %collective-permute-start) | collective-permute-done | bytes 20512 | tf_op jit(solution)/shard_map/ppermute | solution.py:332
  9.7 3.1 %frozen_blocks.6.refs_4_ = f32[4,128,384]{2,1,0:T(8,128)} custom-call(f32[256,1024]{1,0:T(8,128)S(1)} %get-tuple-element.49.refs_0_.refs_3_, bf16[1024,8192]{1,0:T(8,128)(2,1)} %refs_1_.12, f32[64,128]{1,0:T(8,128)S(1)} %get-tuple-element.48.refs_2_.refs_0_), custom_call_target="tpu_custom_call" | custom-call | tf_op jit(solution)/shard_map/frozen_blocks/pallas_call | solution.py:76
  13.2 3.8 %collective-permute-start.5 = (f32[64,128]{1,0:T(8,128)S(1)}, f32[64,128]{1,0:T(8,128)S(1)}, u32[]{:S(2)}, u32[]{:S(2)}) collective-permute-start(f32[64,128]{1,0:T(8,128)S(1)} %get-tuple-element.48.refs_2_.refs_0_), channel_id=1, source_target_pairs={{0,12},{2,14},{4,8},{6,10},{8,4},{10,6},{12,0},{14,2},{1,13},{3,15... | collective-permute-start | bytes 98312 | tf_op jit(solution)/shard_map/ppermute | solution.py:332
  19.2 2.6 %collective-permute-done.4.refs_2_ = f32[64,128]{1,0:T(8,128)S(1)} collective-permute-done((f32[64,128]{1,0:T(8,128)S(1)}, f32[64,128]{1,0:T(8,128)S(1)}, u32[]{:S(2)}, u32[]{:S(2)}) %collective-permute-start.4) | collective-permute-done | bytes 32800 | tf_op jit(solution)/shard_map/ppermute | solution.py:332
  23.6 3.3 %collective-permute-start.9 = (f32[32,1024]{1,0:T(8,128)S(1)}, f32[32,1024]{1,0:T(8,128)S(1)}, u32[]{:S(2)}, u32[]{:S(2)}) collective-permute-start(f32[32,1024]{1,0:T(8,128)S(1)} %get-tuple-element.52), channel_id=1, source_target_pairs={{0,14},{2,12},{4,10},{6,8},{8,6},{10,4},{12,2},{14,0},{1,15},{3,13... | collective-permute-start | bytes 393224 | tf_op jit(solution)/shard_map/ppermute | solution.py:332
  29.6 3.1 %frozen_blocks.7.refs_0_.refs_2_ = f32[4,128,384]{2,1,0:T(8,128)} custom-call(f32[256,1024]{1,0:T(8,128)S(1)} %get-tuple-element.49.refs_0_.refs_3_, bf16[1024,8192]{1,0:T(8,128)(2,1)} %refs_1_.12, f32[32,1024]{1,0:T(8,128)S(1)} %collective-permute-done.7.refs_2_.refs_1_.refs_6_), custom_call_target="tpu_custom_call" | custom-call | tf_op jit(solution)/shard_map/frozen_blocks/pallas_call | solution.py:76
  32.7 3.1 %frozen_blocks.8.refs_2_.refs_0_ = f32[4,128,384]{2,1,0:T(8,128)} custom-call(f32[256,1024]{1,0:T(8,128)S(1)} %get-tuple-element.49.refs_0_.refs_3_, bf16[1024,8192]{1,0:T(8,128)(2,1)} %refs_1_.12, f32[32,1024]{1,0:T(8,128)S(1)} %collective-permute-done.7.refs_2_.refs_1_.refs_6_, f32[32,1024]{1,0:T(8,128)S(1)} %collective-permute-done.9.refs_3_.refs_1_.refs_7_), custom_call_target="tpu_custom_call" | custom-call | tf_op jit(solution)/shard_map/frozen_blocks/pallas_call | solution.py:76
  40.1 3.9 %collective-permute-start.14 = (f32[32,1024]{1,0:T(8,128)S(1)}, f32[32,1024]{1,0:T(8,128)S(1)}, u32[]{:S(2)}, u32[]{:S(2)}) collective-permute-start(f32[32,1024]{1,0:T(8,128)S(1)} %get-tuple-element.59), channel_id=1, source_target_pairs={{0,8},{2,10},{4,12},{6,14},{8,0},{10,2},{12,4},{14,6},{1,9},{3,11}... | collective-permute-start | bytes 393224 | tf_op jit(solution)/shard_map/ppermute | solution.py:332
  47.9 5.3 %collective-permute-done.12.refs_2_ = f32[32,1024]{1,0:T(8,128)S(1)} collective-permute-done((f32[32,1024]{1,0:T(8,128)S(1)}, f32[32,1024]{1,0:T(8,128)S(1)}, u32[]{:S(2)}, u32[]{:S(2)}) %collective-permute-start.12) | collective-permute-done | bytes 131104 | tf_op jit(solution)/shard_map/ppermute | solution.py:332
  53.2 2.6 %collective-permute-done.13.refs_3_ = f32[32,1024]{1,0:T(8,128)S(1)} collective-permute-done((f32[32,1024]{1,0:T(8,128)S(1)}, f32[32,1024]{1,0:T(8,128)S(1)}, u32[]{:S(2)}, u32[]{:S(2)}) %collective-permute-start.13) | collective-permute-done | bytes 131104 | tf_op jit(solution)/shard_map/ppermute | solution.py:332
  55.9 3.4 %change.1 = (f32[32,1024]{1,0:T(8,128)S(1)}, f32[32,1024]{1,0:T(8,128)S(1)}, f32[32,1024]{1,0:T(8,128)S(1)}, f32[32,1024]{1,0:T(8,128)S(1)}, f32[32,1024]{1,0:T(...) custom-call(f32[32,1024]{1,0:T(8,128)S(1)} %get-tuple-element.56.ref, ...), custom_call_target="tpu_custom_call" | custom-call | tf_op jit(solution)/shard_map/change/pallas_call | solution.py:76
  60.2 3.3 %collective-permute-start.18 = (f32[32,1024]{1,0:T(8,128)S(1)}, f32[32,1024]{1,0:T(8,128)S(1)}, u32[]{:S(2)}, u32[]{:S(2)}) collective-permute-start(f32[32,1024]{1,0:T(8,128)S(1)} %get-tuple-element.62), channel_id=1, source_target_pairs={{0,14},{2,12},{4,10},{6,8},{8,6},{10,4},{12,2},{14,0},{1,15},{3,13... | collective-permute-start | bytes 393224 | tf_op jit(solution)/shard_map/ppermute | solution.py:332
  64.6 3.0 %collective-permute-done.16.refs_2_.refs_1_.refs_6_ = f32[32,1024]{1,0:T(8,128)S(1)} collective-permute-done((f32[32,1024]{1,0:T(8,128)S(1)}, f32[32,1024]{1,0:T(8,128)S(1)}, u32[]{:S(2)}, u32[]{:S(2)}) %collective-permute-start.16) | collective-permute-done | bytes 131104 | tf_op jit(solution)/shard_map/ppermute | solution.py:332
  67.6 2.6 %frozen_blocks.11.refs_0_.refs_3_ = f32[4,128,256]{2,1,0:T(8,128)} custom-call(f32[256,1024]{1,0:T(8,128)S(1)} %get-tuple-element.49.refs_0_.refs_3_, bf16[1024,8192]{1,0:T(8,128)(2,1)} %refs_1_.12, f32[32,1024]{1,0:T(8,128)S(1)} %collective-permute-done.16.refs_2_.refs_1_.refs_6_), custom_call_target="tpu_custom_call" | custom-call | tf_op jit(solution)/shard_map/frozen_blocks/pallas_call | solution.py:76
  70.3 3.1 %frozen_blocks.9.refs_0_.refs_2_ = f32[4,128,384]{2,1,0:T(8,128)} custom-call(f32[256,1024]{1,0:T(8,128)S(1)} %get-tuple-element.49.refs_0_.refs_3_, bf16[1024,8192]{1,0:T(8,128)(2,1)} %refs_1_.12, f32[32,1024]{1,0:T(8,128)S(1)} %collective-permute-done.16.refs_2_.refs_1_.refs_6_), custom_call_target="tpu_custom_call" | custom-call | tf_op jit(solution)/shard_map/frozen_blocks/pallas_call | solution.py:76
  75.6 2.7 %collective-permute-start.21 = (f32[2,128,384]{2,1,0:T(8,128)}, f32[2,128,384]{2,1,0:T(8,128)S(1)}, u32[]{:S(2)}, u32[]{:S(2)}) collective-permute-start(f32[2,128,384]{2,1,0:T(8,128)} %get-tuple-element.64.refs_2_), channel_id=1, source_target_pairs={{0,4},{2,6},{4,0},{6,2},{8,12},{10,14},{12,8},{14,10},{1,5},{3,7},... | collective-permute-start | bytes 1179656 | tf_op jit(solution)/shard_map/ppermute | solution.py:332
  80.9 2.2 %collective-permute-start.20 = (f32[1,128,384]{2,1,0:T(8,128)}, f32[1,128,384]{2,1,0:T(8,128)S(1)}, u32[]{:S(2)}, u32[]{:S(2)}) collective-permute-start(f32[1,128,384]{2,1,0:T(8,128)} %get-tuple-element.66.refs_3_), channel_id=1, source_target_pairs={{0,8},{2,10},{4,12},{6,14},{8,0},{10,2},{12,4},{14,6},{1,9},{3,11}... | collective-permute-start | bytes 589832 | tf_op jit(solution)/shard_map/ppermute | solution.py:332
  83.8 2.6 %frozen_blocks.10.refs_4_.refs_0_ = f32[4,128,256]{2,1,0:T(8,128)} custom-call(f32[256,1024]{1,0:T(8,128)S(1)} %get-tuple-element.49.refs_0_.refs_3_, bf16[1024,8192]{1,0:T(8,128)(2,1)} %refs_1_.12, f32[2,128,384]{2,1,0:T(8,128)} %get-tuple-element.64.refs_2_, f32[1,128,384]{2,1,0:T(8,128)} %get-tuple-element.66.refs_3_), custom_call_target="tpu_custom_call" | custom-call | tf_op jit(solution)/shard_map/frozen_blocks/pallas_call | solution.py:76
  86.5 9.2 %collective-permute-done.22.refs_2_.refs_6_ = f32[32,1024]{1,0:T(8,128)S(1)} collective-permute-done((f32[32,1024]{1,0:T(8,128)S(1)}, f32[32,1024]{1,0:T(8,128)S(1)}, u32[]{:S(2)}, u32[]{:S(2)}) %collective-permute-start.22) | collective-permute-done | bytes 131104 | tf_op jit(solution)/shard_map/ppermute | solution.py:332
  99.1 3.8 %collective-permute-done.26.refs_5_ = f32[32,1024]{1,0:T(8,128)S(1)} collective-permute-done((f32[32,1024]{1,0:T(8,128)S(1)}, f32[32,1024]{1,0:T(8,128)S(1)}, u32[]{:S(2)}, u32[]{:S(2)}) %collective-permute-start.26) | collective-permute-done | bytes 131104 | tf_op jit(solution)/shard_map/ppermute | solution.py:332
  107.6 4.7 %collective-permute-done.23.refs_2_.refs_6_ = f32[1,128,384]{2,1,0:T(8,128)S(1)} collective-permute-done((f32[1,128,384]{2,1,0:T(8,128)}, f32[1,128,384]{2,1,0:T(8,128)S(1)}, u32[]{:S(2)}, u32[]{:S(2)}) %collective-permute-start.23) | collective-permute-done | bytes 196640 | tf_op jit(solution)/shard_map/ppermute | solution.py:332
  118.2 3.0 %update.1 = (bf16[16,16,1024]{2,1,0:T(8,128)(2,1)}, bf16[16,16,1024]{2,1,0:T(8,128)(2,1)}) custom-call(s32[16]{0:T(128)S(1)} %select_reduce_fusion.refs_0_, bf16[16,16,1024]{2,1,0:T(8,128)(2,1)} %refs_1_.13, bf16[16,16,1024]{2,1,0:T(8,128)(2,1)} %refs_2_.5, f32[8,32,1024]{2,1,0:T(8,128)S(1)} %pack.1.refs_3_, f32[8,32,1024]{2,1,0:T(8,128)S(1)} %collective-permute-done.30.refs_4_), custom_call_target="tpu_custom_call" | custom-call | tf_op jit(solution)/shard_map/update/pallas_call | solution.py:76
  121.2 4.2 %collective-permute-done.29.refs_8_ = f32[1,128,256]{2,1,0:T(8,128)S(1)} collective-permute-done((f32[1,128,256]{2,1,0:T(8,128)}, f32[1,128,256]{2,1,0:T(8,128)S(1)}, u32[]{:S(2)}, u32[]{:S(2)}) %collective-permute-start.29) | collective-permute-done | bytes 131104 | tf_op jit(solution)/shard_map/ppermute | solution.py:332
  (71 shorter events, 43.1 us)
Async XLA Ops:
  2.7 19.1 %collective-permute-start.6 = (f32[256,1024]{1,0:T(8,128)S(1)}, f32[256,1024]{1,0:T(8,128)S(1)}, u32[]{:S(2)}, u32[]{:S(2)}) collective-permute-start(f32[256,1024]{1,0:T(8,128)S(1)} %get-tuple-element.49.refs_0_.refs_3_), channel_id=1, source_target_pairs={{0,1},{1,0},{2,3},{3,2},{4,5},{5,4},{6,7},{7,6},{8,9},{9,8},{10,11... | collective-permute-start | bytes 3145736 | tf_op jit(solution)/shard_map/ppermute | solution.py:332
  12.8 23.2 %collective-permute-start.8 = (f32[4,128,384]{2,1,0:T(8,128)}, f32[4,128,384]{2,1,0:T(8,128)S(1)}, u32[]{:S(2)}, u32[]{:S(2)}) collective-permute-start(f32[4,128,384]{2,1,0:T(8,128)} %frozen_blocks.6.refs_4_), channel_id=1, source_target_pairs={{0,2},{2,0},{4,6},{6,4},{8,10},{10,8},{12,14},{14,12},{1,3},{3,1},... | collective-permute-start | bytes 2359304 | tf_op jit(solution)/shard_map/ppermute | solution.py:332
  22.1 7.5 %collective-permute-start.7 = (f32[32,1024]{1,0:T(8,128)S(1)}, f32[32,1024]{1,0:T(8,128)S(1)}, u32[]{:S(2)}, u32[]{:S(2)}) collective-permute-start(f32[32,1024]{1,0:T(8,128)S(1)} %get-tuple-element.51), channel_id=1, source_target_pairs={{0,12},{2,14},{4,8},{6,10},{8,4},{10,6},{12,0},{14,2},{1,13},{3,15... | collective-permute-start | bytes 393224 | tf_op jit(solution)/shard_map/ppermute | solution.py:332
  23.6 9.0 %collective-permute-start.9 = (f32[32,1024]{1,0:T(8,128)S(1)}, f32[32,1024]{1,0:T(8,128)S(1)}, u32[]{:S(2)}, u32[]{:S(2)}) collective-permute-start(f32[32,1024]{1,0:T(8,128)S(1)} %get-tuple-element.52), channel_id=1, source_target_pairs={{0,14},{2,12},{4,10},{6,8},{8,6},{10,4},{12,2},{14,0},{1,15},{3,13... | collective-permute-start | bytes 393224 | tf_op jit(solution)/shard_map/ppermute | solution.py:332
  27.0 10.5 %collective-permute-start.10 = (f32[32,1024]{1,0:T(8,128)S(1)}, f32[32,1024]{1,0:T(8,128)S(1)}, u32[]{:S(2)}, u32[]{:S(2)}) collective-permute-start(f32[32,1024]{1,0:T(8,128)S(1)} %get-tuple-element.53), channel_id=1, source_target_pairs={{0,2},{2,0},{4,6},{6,4},{8,10},{10,8},{12,14},{14,12},{1,3},{3,1},... | collective-permute-start | bytes 393224 | tf_op jit(solution)/shard_map/ppermute | solution.py:332
  39.5 33.9 %collective-permute-start.17 = (f32[4,128,384]{2,1,0:T(8,128)}, f32[4,128,384]{2,1,0:T(8,128)S(1)}, u32[]{:S(2)}, u32[]{:S(2)}) collective-permute-start(f32[4,128,384]{2,1,0:T(8,128)} %release.11), channel_id=1, source_target_pairs={{0,2},{2,0},{4,6},{6,4},{8,10},{10,8},{12,14},{14,12},{1,3},{3,1},... | collective-permute-start | bytes 2359304 | tf_op jit(solution)/shard_map/ppermute | solution.py:332
  40.1 7.8 %collective-permute-start.14 = (f32[32,1024]{1,0:T(8,128)S(1)}, f32[32,1024]{1,0:T(8,128)S(1)}, u32[]{:S(2)}, u32[]{:S(2)}) collective-permute-start(f32[32,1024]{1,0:T(8,128)S(1)} %get-tuple-element.59), channel_id=1, source_target_pairs={{0,8},{2,10},{4,12},{6,14},{8,0},{10,2},{12,4},{14,6},{1,9},{3,11}... | collective-permute-start | bytes 393224 | tf_op jit(solution)/shard_map/ppermute | solution.py:332
  44.0 9.2 %collective-permute-start.12 = (f32[32,1024]{1,0:T(8,128)S(1)}, f32[32,1024]{1,0:T(8,128)S(1)}, u32[]{:S(2)}, u32[]{:S(2)}) collective-permute-start(f32[32,1024]{1,0:T(8,128)S(1)} %release.8), channel_id=1, source_target_pairs={{0,4},{2,6},{4,0},{6,2},{8,12},{10,14},{12,8},{14,10},{1,5},{3,7},... | collective-permute-start | bytes 393224 | tf_op jit(solution)/shard_map/ppermute | solution.py:332
  44.5 11.4 %collective-permute-start.13 = (f32[32,1024]{1,0:T(8,128)S(1)}, f32[32,1024]{1,0:T(8,128)S(1)}, u32[]{:S(2)}, u32[]{:S(2)}) collective-permute-start(f32[32,1024]{1,0:T(8,128)S(1)} %release.9), channel_id=1, source_target_pairs={{0,6},{2,4},{4,2},{6,0},{8,14},{10,12},{12,10},{14,8},{1,7},{3,5},... | collective-permute-start | bytes 393224 | tf_op jit(solution)/shard_map/ppermute | solution.py:332
  46.5 9.3 %collective-permute-start.15 = (f32[32,1024]{1,0:T(8,128)S(1)}, f32[32,1024]{1,0:T(8,128)S(1)}, u32[]{:S(2)}, u32[]{:S(2)}) collective-permute-start(f32[32,1024]{1,0:T(8,128)S(1)} %release.10), channel_id=1, source_target_pairs={{0,10},{2,8},{4,14},{6,12},{8,2},{10,0},{12,6},{14,4},{1,11},{3,9}... | collective-permute-start | bytes 393224 | tf_op jit(solution)/shard_map/ppermute | solution.py:332
  59.3 8.3 %collective-permute-start.16 = (f32[32,1024]{1,0:T(8,128)S(1)}, f32[32,1024]{1,0:T(8,128)S(1)}, u32[]{:S(2)}, u32[]{:S(2)}) collective-permute-start(f32[32,1024]{1,0:T(8,128)S(1)} %get-tuple-element.61), channel_id=1, source_target_pairs={{0,12},{2,14},{4,8},{6,10},{8,4},{10,6},{12,0},{14,2},{1,13},{3,15... | collective-permute-start | bytes 393224 | tf_op jit(solution)/shard_map/ppermute | solution.py:332
  60.2 13.2 %collective-permute-start.18 = (f32[32,1024]{1,0:T(8,128)S(1)}, f32[32,1024]{1,0:T(8,128)S(1)}, u32[]{:S(2)}, u32[]{:S(2)}) collective-permute-start(f32[32,1024]{1,0:T(8,128)S(1)} %get-tuple-element.62), channel_id=1, source_target_pairs={{0,14},{2,12},{4,10},{6,8},{8,6},{10,4},{12,2},{14,0},{1,15},{3,13... | collective-permute-start | bytes 393224 | tf_op jit(solution)/shard_map/ppermute | solution.py:332
  63.5 10.0 %collective-permute-start.19 = (f32[32,1024]{1,0:T(8,128)S(1)}, f32[32,1024]{1,0:T(8,128)S(1)}, u32[]{:S(2)}, u32[]{:S(2)}) collective-permute-start(f32[32,1024]{1,0:T(8,128)S(1)} %get-tuple-element.63), channel_id=1, source_target_pairs={{0,2},{2,0},{4,6},{6,4},{8,10},{10,8},{12,14},{14,12},{1,3},{3,1},... | collective-permute-start | bytes 393224 | tf_op jit(solution)/shard_map/ppermute | solution.py:332
  64.6 14.4 %collective-permute-start.11 = (f32[2,128,384]{2,1,0:T(8,128)}, f32[2,128,384]{2,1,0:T(8,128)S(1)}, u32[]{:S(2)}, u32[]{:S(2)}) collective-permute-start(f32[2,128,384]{2,1,0:T(8,128)} %get-tuple-element.55.refs_2_.refs_1_), channel_id=1, source_target_pairs={{0,4},{2,6},{4,0},{6,2},{8,12},{10,14},{12,8},{14,10},{1,5},{3,7},... | collective-permute-start | bytes 1179656 | tf_op jit(solution)/shard_map/ppermute | solution.py:332
  75.6 20.1 %collective-permute-start.21 = (f32[2,128,384]{2,1,0:T(8,128)}, f32[2,128,384]{2,1,0:T(8,128)S(1)}, u32[]{:S(2)}, u32[]{:S(2)}) collective-permute-start(f32[2,128,384]{2,1,0:T(8,128)} %get-tuple-element.64.refs_2_), channel_id=1, source_target_pairs={{0,4},{2,6},{4,0},{6,2},{8,12},{10,14},{12,8},{14,10},{1,5},{3,7},... | collective-permute-start | bytes 1179656 | tf_op jit(solution)/shard_map/ppermute | solution.py:332
  78.3 24.7 %collective-permute-start.24 = (f32[4,128,256]{2,1,0:T(8,128)S(1)}, f32[4,128,256]{2,1,0:T(8,128)S(1)}, u32[]{:S(2)}, u32[]{:S(2)}) collective-permute-start(f32[4,128,256]{2,1,0:T(8,128)S(1)} %release.13), channel_id=1, source_target_pairs={{0,2},{2,0},{4,6},{6,4},{8,10},{10,8},{12,14},{14,12},{1,3},{3,1},... | collective-permute-start | bytes 1572872 | tf_op jit(solution)/shard_map/ppermute | solution.py:332
  78.9 16.7 %collective-permute-start.22 = (f32[32,1024]{1,0:T(8,128)S(1)}, f32[32,1024]{1,0:T(8,128)S(1)}, u32[]{:S(2)}, u32[]{:S(2)}) collective-permute-start(f32[32,1024]{1,0:T(8,128)S(1)} %release.12), channel_id=1, source_target_pairs={{0,4},{2,6},{4,0},{6,2},{8,12},{10,14},{12,8},{14,10},{1,5},{3,7},... | collective-permute-start | bytes 393224 | tf_op jit(solution)/shard_map/ppermute | solution.py:332
  80.9 22.1 %collective-permute-start.20 = (f32[1,128,384]{2,1,0:T(8,128)}, f32[1,128,384]{2,1,0:T(8,128)S(1)}, u32[]{:S(2)}, u32[]{:S(2)}) collective-permute-start(f32[1,128,384]{2,1,0:T(8,128)} %get-tuple-element.66.refs_3_), channel_id=1, source_target_pairs={{0,8},{2,10},{4,12},{6,14},{8,0},{10,2},{12,4},{14,6},{1,9},{3,11}... | collective-permute-start | bytes 589832 | tf_op jit(solution)/shard_map/ppermute | solution.py:332
  83.1 16.0 %collective-permute-start.25 = (f32[32,1024]{1,0:T(8,128)S(1)}, f32[32,1024]{1,0:T(8,128)S(1)}, u32[]{:S(2)}, u32[]{:S(2)}) collective-permute-start(f32[32,1024]{1,0:T(8,128)S(1)} %get-tuple-element.71), channel_id=1, source_target_pairs={{0,8},{2,10},{4,12},{6,14},{8,0},{10,2},{12,4},{14,6},{1,9},{3,11}... | collective-permute-start | bytes 393224 | tf_op jit(solution)/shard_map/ppermute | solution.py:332
  95.7 7.3 %collective-permute-start.26 = (f32[32,1024]{1,0:T(8,128)S(1)}, f32[32,1024]{1,0:T(8,128)S(1)}, u32[]{:S(2)}, u32[]{:S(2)}) collective-permute-start(f32[32,1024]{1,0:T(8,128)S(1)} %release.14), channel_id=1, source_target_pairs={{0,10},{2,8},{4,14},{6,12},{8,2},{10,0},{12,6},{14,4},{1,11},{3,9}... | collective-permute-start | bytes 393224 | tf_op jit(solution)/shard_map/ppermute | solution.py:332
  95.7 7.3 %collective-permute-start.27 = (f32[32,1024]{1,0:T(8,128)S(1)}, f32[32,1024]{1,0:T(8,128)S(1)}, u32[]{:S(2)}, u32[]{:S(2)}) collective-permute-start(f32[32,1024]{1,0:T(8,128)S(1)} %release.15), channel_id=1, source_target_pairs={{0,6},{2,4},{4,2},{6,0},{8,14},{10,12},{12,10},{14,8},{1,7},{3,5},... | collective-permute-start | bytes 393224 | tf_op jit(solution)/shard_map/ppermute | solution.py:332
  104.9 8.8 %collective-permute-start.28 = (f32[2,128,256]{2,1,0:T(8,128)}, f32[2,128,256]{2,1,0:T(8,128)S(1)}, u32[]{:S(2)}, u32[]{:S(2)}) collective-permute-start(f32[2,128,256]{2,1,0:T(8,128)} %get-tuple-element.75), channel_id=1, source_target_pairs={{0,4},{2,6},{4,0},{6,2},{8,12},{10,14},{12,8},{14,10},{1,5},{3,7},... | collective-permute-start | bytes 786440 | tf_op jit(solution)/shard_map/ppermute | solution.py:332
  105.4 6.9 %collective-permute-start.23 = (f32[1,128,384]{2,1,0:T(8,128)}, f32[1,128,384]{2,1,0:T(8,128)S(1)}, u32[]{:S(2)}, u32[]{:S(2)}) collective-permute-start(f32[1,128,384]{2,1,0:T(8,128)} %get-tuple-element.70.refs_2_), channel_id=1, source_target_pairs={{0,8},{2,10},{4,12},{6,14},{8,0},{10,2},{12,4},{14,6},{1,9},{3,11}... | collective-permute-start | bytes 589832 | tf_op jit(solution)/shard_map/ppermute | solution.py:332
  115.5 9.8 %collective-permute-start.29 = (f32[1,128,256]{2,1,0:T(8,128)}, f32[1,128,256]{2,1,0:T(8,128)S(1)}, u32[]{:S(2)}, u32[]{:S(2)}) collective-permute-start(f32[1,128,256]{2,1,0:T(8,128)} %get-tuple-element.77.refs_8_), channel_id=1, source_target_pairs={{0,8},{2,10},{4,12},{6,14},{8,0},{10,2},{12,4},{14,6},{1,9},{3,11}... | collective-permute-start | bytes 393224 | tf_op jit(solution)/shard_map/ppermute | solution.py:332
  (9 other events, 79.4 us)

commit v5 on v4

--- a/solution.py
+++ b/solution.py
@@ -280,31 +280,33 @@
 
 
 def change_kernel(parts, *refs):
-    grads, state, outs = refs[:parts], refs[parts : parts + 4], refs[parts + 4 : 2 * parts + 4]
-    state_hbm, sems = refs[2 * parts + 4 : 2 * parts + 8], refs[-1]
+    grads, state_in, outs = refs[:parts], refs[parts : parts + 4], refs[parts + 4 : 2 * parts + 4]
+    state_out, state, sems = refs[2 * parts + 4 : 2 * parts + 8], refs[-5:-1], refs[-1]
+    loads = [pltpu.make_async_copy(state_in[i], state[i], sems.at[4 + i]) for i in range(4)]
+    stores = [pltpu.make_async_copy(state[i], state_out[i], sems.at[i]) for i in range(4)]
+    for i in (0, 2, 1, 3):
+        loads[i].start()
     both, width = grads[0].shape
     lowrank = both // 2
     factor = clip_factor(grads)
-    places = []
-    for k in range(parts):
-        columns = pl.ds(pl.multiple_of((lax.axis_index("tensor") ^ k) * width, width), width)
-        for half in range(2):
-            rows = slice(half * lowrank, (half + 1) * lowrank)
-            places.append((k, half, rows, columns))
+    me = lax.axis_index("tensor")
+    for half in range(2):
+        mean_ref, power_ref = state[half], state[2 + half]
+        rows = slice(half * lowrank, (half + 1) * lowrank)
+        loads[half].wait()
+        loads[2 + half].wait()
+        for k in range(parts):
+            columns = pl.ds(pl.multiple_of((me ^ k) * width, width), width)
             clipped = grads[k][rows, :] * factor
-            state[half][0, :, columns] = (
-                beta_one * state[half][0, :, columns] + (1.0 - beta_one) * clipped
+            mean = beta_one * mean_ref[0, :, columns] + (1.0 - beta_one) * clipped
+            power = beta_two * power_ref[0, :, columns] + (1.0 - beta_two) * clipped * clipped
+            mean_ref[0, :, columns] = mean
+            power_ref[0, :, columns] = power
+            outs[k][rows, :] = (mean * (learn_rate / correct_one)) / (
+                jnp.sqrt(power * (1.0 / correct_two)) + adam_eps
             )
-            state[2 + half][0, :, columns] = (
-                beta_two * state[2 + half][0, :, columns] + (1.0 - beta_two) * clipped * clipped
-            )
-    stores = [pltpu.make_async_copy(state[i], state_hbm[i], sems.at[i]) for i in range(4)]
-    for store in stores:
-        store.start()
-    for k, half, rows, columns in places:
-        outs[k][rows, :] = (state[half][0, :, columns] * (learn_rate / correct_one)) / (
-            jnp.sqrt(state[2 + half][0, :, columns] * (1.0 / correct_two)) + adam_eps
-        )
+        stores[half].start()
+        stores[2 + half].start()
     for store in stores:
         store.wait()
 
@@ -443,8 +445,10 @@
     own_grads = [got[k] for k in range(parts)]
     made = call(
         functools.partial(change_kernel, parts),
-        [block] * parts + [pltpu.HBM(momentum_down.shape, f32)] * 4, *own_grads, *state,
-        name="change", stage=False, scratch=[pltpu.SemaphoreType.DMA((4,))],
+        [block] * parts + [pltpu.HBM(momentum_down.shape, f32)] * 4, *own_grads,
+        *[in_hbm(x.array) for x in state],
+        specs=[vmem] * parts + [hbm] * 4, name="change", stage=False,
+        scratch=[pltpu.VMEM(momentum_down.shape, f32)] * 4 + [pltpu.SemaphoreType.DMA((8,))],
     )
     change, (mean_down, mean_up, power_down, power_up) = made[:parts], made[parts:]
 

time: 128 us -> 128 us (level)
  transfers between devices with their start and end apart: 31 -> 31, of which waited for: 17 -> 17; matrix products, arithmetic and copies ran while one was open for 0% -> 0% of each run, Pallas kernels for 24% -> 23%
where the time goes in v5:
time: 128 us; the launch traced here: 127 us
  waiting for transfers between devices  47.5 us (37%)
  Pallas kernels  39.9 us (31%)
  starting transfers between devices  38.9 us (30%)
    ppermute x30, waiting for transfers between devices, swap(): return lax.ppermute(x, axis, [(i, i ^ bits) for i in range(size)])  46.5 us
    pallas_call x20, Pallas kernels, call(): pl.pallas_call(kernel, in_specs=specs + [anywhere] * extra, out_specs=[hb...  39.8 us
    ppermute x30, starting transfers between devices, swap(): return lax.ppermute(x, axis, [(i, i ^ bits) for i in range(size)])  36.2 us
    ppermute x1, starting transfers between devices, on_device(): lax.ppermute(rank_part, ('tensor', 'dp'), diagonal)  2.64 us
  transfers between devices with their start and end apart: 31, of which 17 were waited for; matrix products, arithmetic and copies ran while one was open for 0% of the time, Pallas kernels for 23%

profile of v5, /device:TPU:0, one launch (start us, length us, event | category | flops | bytes accessed | tf_op | source)
XLA Modules:
  0.0 127.3 jit_solution(8662809666295053183)
XLA Ops:
  3.2 2.6 %collective-permute-start.2 = (f32[40,128]{1,0:T(8,128)S(1)}, f32[40,128]{1,0:T(8,128)S(1)}, u32[]{:S(2)}, u32[]{:S(2)}) collective-permute-start(f32[40,128]{1,0:T(8,128)S(1)} %get-tuple-element.47.refs_0_), channel_id=1, source_target_pairs={{0,3},{1,2},{2,1},{3,0},{4,7},{5,6},{6,5},{7,4},{8,11},{9,10},{10,... | collective-permute-start | bytes 61448 | tf_op jit(solution)/shard_map/ppermute | solution.py:387
  7.3 2.4 %collective-permute-done.refs_1_ = f32[40,128]{1,0:T(8,128)S(1)} collective-permute-done((f32[40,128]{1,0:T(8,128)S(1)}, f32[40,128]{1,0:T(8,128)S(1)}, u32[]{:S(2)}, u32[]{:S(2)}) %collective-permute-start) | collective-permute-done | bytes 20512 | tf_op jit(solution)/shard_map/ppermute | solution.py:334
  9.7 3.1 %frozen_blocks.6.refs_4_ = f32[4,128,384]{2,1,0:T(8,128)} custom-call(f32[256,1024]{1,0:T(8,128)S(1)} %get-tuple-element.49.refs_0_.refs_3_, bf16[1024,8192]{1,0:T(8,128)(2,1)} %refs_1_.12, f32[64,128]{1,0:T(8,128)S(1)} %get-tuple-element.48.refs_2_.refs_0_), custom_call_target="tpu_custom_call" | custom-call | tf_op jit(solution)/shard_map/frozen_blocks/pallas_call | solution.py:76
  13.2 3.8 %collective-permute-start.5 = (f32[64,128]{1,0:T(8,128)S(1)}, f32[64,128]{1,0:T(8,128)S(1)}, u32[]{:S(2)}, u32[]{:S(2)}) collective-permute-start(f32[64,128]{1,0:T(8,128)S(1)} %get-tuple-element.48.refs_2_.refs_0_), channel_id=1, source_target_pairs={{0,12},{2,14},{4,8},{6,10},{8,4},{10,6},{12,0},{14,2},{1,13},{3,15... | collective-permute-start | bytes 98312 | tf_op jit(solution)/shard_map/ppermute | solution.py:334
  19.2 2.6 %collective-permute-done.4.refs_2_ = f32[64,128]{1,0:T(8,128)S(1)} collective-permute-done((f32[64,128]{1,0:T(8,128)S(1)}, f32[64,128]{1,0:T(8,128)S(1)}, u32[]{:S(2)}, u32[]{:S(2)}) %collective-permute-start.4) | collective-permute-done | bytes 32800 | tf_op jit(solution)/shard_map/ppermute | solution.py:334
  23.6 3.3 %collective-permute-start.9 = (f32[32,1024]{1,0:T(8,128)S(1)}, f32[32,1024]{1,0:T(8,128)S(1)}, u32[]{:S(2)}, u32[]{:S(2)}) collective-permute-start(f32[32,1024]{1,0:T(8,128)S(1)} %get-tuple-element.52), channel_id=1, source_target_pairs={{0,14},{2,12},{4,10},{6,8},{8,6},{10,4},{12,2},{14,0},{1,15},{3,13... | collective-permute-start | bytes 393224 | tf_op jit(solution)/shard_map/ppermute | solution.py:334
  29.6 3.1 %frozen_blocks.7.refs_0_.refs_2_ = f32[4,128,384]{2,1,0:T(8,128)} custom-call(f32[256,1024]{1,0:T(8,128)S(1)} %get-tuple-element.49.refs_0_.refs_3_, bf16[1024,8192]{1,0:T(8,128)(2,1)} %refs_1_.12, f32[32,1024]{1,0:T(8,128)S(1)} %collective-permute-done.7.refs_2_.refs_1_.refs_6_), custom_call_target="tpu_custom_call" | custom-call | tf_op jit(solution)/shard_map/frozen_blocks/pallas_call | solution.py:76
  32.7 3.1 %frozen_blocks.8.refs_2_.refs_0_ = f32[4,128,384]{2,1,0:T(8,128)} custom-call(f32[256,1024]{1,0:T(8,128)S(1)} %get-tuple-element.49.refs_0_.refs_3_, bf16[1024,8192]{1,0:T(8,128)(2,1)} %refs_1_.12, f32[32,1024]{1,0:T(8,128)S(1)} %collective-permute-done.7.refs_2_.refs_1_.refs_6_, f32[32,1024]{1,0:T(8,128)S(1)} %collective-permute-done.9.refs_3_.refs_1_.refs_7_), custom_call_target="tpu_custom_call" | custom-call | tf_op jit(solution)/shard_map/frozen_blocks/pallas_call | solution.py:76
  40.1 3.9 %collective-permute-start.14 = (f32[32,1024]{1,0:T(8,128)S(1)}, f32[32,1024]{1,0:T(8,128)S(1)}, u32[]{:S(2)}, u32[]{:S(2)}) collective-permute-start(f32[32,1024]{1,0:T(8,128)S(1)} %get-tuple-element.59), channel_id=1, source_target_pairs={{0,8},{2,10},{4,12},{6,14},{8,0},{10,2},{12,4},{14,6},{1,9},{3,11}... | collective-permute-start | bytes 393224 | tf_op jit(solution)/shard_map/ppermute | solution.py:334
  47.9 5.3 %collective-permute-done.12.refs_2_ = f32[32,1024]{1,0:T(8,128)S(1)} collective-permute-done((f32[32,1024]{1,0:T(8,128)S(1)}, f32[32,1024]{1,0:T(8,128)S(1)}, u32[]{:S(2)}, u32[]{:S(2)}) %collective-permute-start.12) | collective-permute-done | bytes 131104 | tf_op jit(solution)/shard_map/ppermute | solution.py:334
  53.2 2.6 %collective-permute-done.13.refs_3_ = f32[32,1024]{1,0:T(8,128)S(1)} collective-permute-done((f32[32,1024]{1,0:T(8,128)S(1)}, f32[32,1024]{1,0:T(8,128)S(1)}, u32[]{:S(2)}, u32[]{:S(2)}) %collective-permute-start.13) | collective-permute-done | bytes 131104 | tf_op jit(solution)/shard_map/ppermute | solution.py:334
  55.9 3.2 %change.1 = (f32[32,1024]{1,0:T(8,128)S(1)}, f32[32,1024]{1,0:T(8,128)S(1)}, f32[32,1024]{1,0:T(8,128)S(1)}, f32[32,1024]{1,0:T(8,128)S(1)}, f32[32,1024]{1,0:T(...) custom-call(f32[32,1024]{1,0:T(8,128)S(1)} %get-tuple-element.56.ref, ...), custom_call_target="tpu_custom_call" | custom-call | tf_op jit(solution)/shard_map/change/pallas_call | solution.py:76
  59.9 3.3 %collective-permute-start.18 = (f32[32,1024]{1,0:T(8,128)S(1)}, f32[32,1024]{1,0:T(8,128)S(1)}, u32[]{:S(2)}, u32[]{:S(2)}) collective-permute-start(f32[32,1024]{1,0:T(8,128)S(1)} %get-tuple-element.62), channel_id=1, source_target_pairs={{0,14},{2,12},{4,10},{6,8},{8,6},{10,4},{12,2},{14,0},{1,15},{3,13... | collective-permute-start | bytes 393224 | tf_op jit(solution)/shard_map/ppermute | solution.py:334
  64.4 3.0 %collective-permute-done.16.refs_2_.refs_1_.refs_6_ = f32[32,1024]{1,0:T(8,128)S(1)} collective-permute-done((f32[32,1024]{1,0:T(8,128)S(1)}, f32[32,1024]{1,0:T(8,128)S(1)}, u32[]{:S(2)}, u32[]{:S(2)}) %collective-permute-start.16) | collective-permute-done | bytes 131104 | tf_op jit(solution)/shard_map/ppermute | solution.py:334
  67.4 2.6 %frozen_blocks.11.refs_0_.refs_3_ = f32[4,128,256]{2,1,0:T(8,128)} custom-call(f32[256,1024]{1,0:T(8,128)S(1)} %get-tuple-element.49.refs_0_.refs_3_, bf16[1024,8192]{1,0:T(8,128)(2,1)} %refs_1_.12, f32[32,1024]{1,0:T(8,128)S(1)} %collective-permute-done.16.refs_2_.refs_1_.refs_6_), custom_call_target="tpu_custom_call" | custom-call | tf_op jit(solution)/shard_map/frozen_blocks/pallas_call | solution.py:76
  70.0 3.1 %frozen_blocks.9.refs_0_.refs_2_ = f32[4,128,384]{2,1,0:T(8,128)} custom-call(f32[256,1024]{1,0:T(8,128)S(1)} %get-tuple-element.49.refs_0_.refs_3_, bf16[1024,8192]{1,0:T(8,128)(2,1)} %refs_1_.12, f32[32,1024]{1,0:T(8,128)S(1)} %collective-permute-done.16.refs_2_.refs_1_.refs_6_), custom_call_target="tpu_custom_call" | custom-call | tf_op jit(solution)/shard_map/frozen_blocks/pallas_call | solution.py:76
  75.3 2.7 %collective-permute-start.21 = (f32[2,128,384]{2,1,0:T(8,128)}, f32[2,128,384]{2,1,0:T(8,128)S(1)}, u32[]{:S(2)}, u32[]{:S(2)}) collective-permute-start(f32[2,128,384]{2,1,0:T(8,128)} %get-tuple-element.64.refs_2_), channel_id=1, source_target_pairs={{0,4},{2,6},{4,0},{6,2},{8,12},{10,14},{12,8},{14,10},{1,5},{3,7},... | collective-permute-start | bytes 1179656 | tf_op jit(solution)/shard_map/ppermute | solution.py:334
  80.6 2.2 %collective-permute-start.20 = (f32[1,128,384]{2,1,0:T(8,128)}, f32[1,128,384]{2,1,0:T(8,128)S(1)}, u32[]{:S(2)}, u32[]{:S(2)}) collective-permute-start(f32[1,128,384]{2,1,0:T(8,128)} %get-tuple-element.66.refs_3_), channel_id=1, source_target_pairs={{0,8},{2,10},{4,12},{6,14},{8,0},{10,2},{12,4},{14,6},{1,9},{3,11}... | collective-permute-start | bytes 589832 | tf_op jit(solution)/shard_map/ppermute | solution.py:334
  83.6 2.6 %frozen_blocks.10.refs_4_.refs_0_ = f32[4,128,256]{2,1,0:T(8,128)} custom-call(f32[256,1024]{1,0:T(8,128)S(1)} %get-tuple-element.49.refs_0_.refs_3_, bf16[1024,8192]{1,0:T(8,128)(2,1)} %refs_1_.12, f32[2,128,384]{2,1,0:T(8,128)} %get-tuple-element.64.refs_2_, f32[1,128,384]{2,1,0:T(8,128)} %get-tuple-element.66.refs_3_), custom_call_target="tpu_custom_call" | custom-call | tf_op jit(solution)/shard_map/frozen_blocks/pallas_call | solution.py:76
  86.2 9.2 %collective-permute-done.22.refs_2_.refs_6_ = f32[32,1024]{1,0:T(8,128)S(1)} collective-permute-done((f32[32,1024]{1,0:T(8,128)S(1)}, f32[32,1024]{1,0:T(8,128)S(1)}, u32[]{:S(2)}, u32[]{:S(2)}) %collective-permute-start.22) | collective-permute-done | bytes 131104 | tf_op jit(solution)/shard_map/ppermute | solution.py:334
  98.8 3.8 %collective-permute-done.26.refs_5_ = f32[32,1024]{1,0:T(8,128)S(1)} collective-permute-done((f32[32,1024]{1,0:T(8,128)S(1)}, f32[32,1024]{1,0:T(8,128)S(1)}, u32[]{:S(2)}, u32[]{:S(2)}) %collective-permute-start.26) | collective-permute-done | bytes 131104 | tf_op jit(solution)/shard_map/ppermute | solution.py:334
  107.3 4.7 %collective-permute-done.23.refs_2_.refs_6_ = f32[1,128,384]{2,1,0:T(8,128)S(1)} collective-permute-done((f32[1,128,384]{2,1,0:T(8,128)}, f32[1,128,384]{2,1,0:T(8,128)S(1)}, u32[]{:S(2)}, u32[]{:S(2)}) %collective-permute-start.23) | collective-permute-done | bytes 196640 | tf_op jit(solution)/shard_map/ppermute | solution.py:334
  117.9 3.0 %update.1 = (bf16[16,16,1024]{2,1,0:T(8,128)(2,1)}, bf16[16,16,1024]{2,1,0:T(8,128)(2,1)}) custom-call(s32[16]{0:T(128)S(1)} %select_reduce_fusion.refs_0_, bf16[16,16,1024]{2,1,0:T(8,128)(2,1)} %refs_1_.13, bf16[16,16,1024]{2,1,0:T(8,128)(2,1)} %refs_2_.5, f32[8,32,1024]{2,1,0:T(8,128)S(1)} %pack.1.refs_3_, f32[8,32,1024]{2,1,0:T(8,128)S(1)} %collective-permute-done.30.refs_4_), custom_call_target="tpu_custom_call" | custom-call | tf_op jit(solution)/shard_map/update/pallas_call | solution.py:76
  120.9 4.2 %collective-permute-done.29.refs_8_ = f32[1,128,256]{2,1,0:T(8,128)S(1)} collective-permute-done((f32[1,128,256]{2,1,0:T(8,128)}, f32[1,128,256]{2,1,0:T(8,128)S(1)}, u32[]{:S(2)}, u32[]{:S(2)}) %collective-permute-start.29) | collective-permute-done | bytes 131104 | tf_op jit(solution)/shard_map/ppermute | solution.py:334
  (71 shorter events, 43.1 us)
Async XLA Ops:
  2.7 19.1 %collective-permute-start.6 = (f32[256,1024]{1,0:T(8,128)S(1)}, f32[256,1024]{1,0:T(8,128)S(1)}, u32[]{:S(2)}, u32[]{:S(2)}) collective-permute-start(f32[256,1024]{1,0:T(8,128)S(1)} %get-tuple-element.49.refs_0_.refs_3_), channel_id=1, source_target_pairs={{0,1},{1,0},{2,3},{3,2},{4,5},{5,4},{6,7},{7,6},{8,9},{9,8},{10,11... | collective-permute-start | bytes 3145736 | tf_op jit(solution)/shard_map/ppermute | solution.py:334
  12.8 23.2 %collective-permute-start.8 = (f32[4,128,384]{2,1,0:T(8,128)}, f32[4,128,384]{2,1,0:T(8,128)S(1)}, u32[]{:S(2)}, u32[]{:S(2)}) collective-permute-start(f32[4,128,384]{2,1,0:T(8,128)} %frozen_blocks.6.refs_4_), channel_id=1, source_target_pairs={{0,2},{2,0},{4,6},{6,4},{8,10},{10,8},{12,14},{14,12},{1,3},{3,1},... | collective-permute-start | bytes 2359304 | tf_op jit(solution)/shard_map/ppermute | solution.py:334
  22.1 7.5 %collective-permute-start.7 = (f32[32,1024]{1,0:T(8,128)S(1)}, f32[32,1024]{1,0:T(8,128)S(1)}, u32[]{:S(2)}, u32[]{:S(2)}) collective-permute-start(f32[32,1024]{1,0:T(8,128)S(1)} %get-tuple-element.51), channel_id=1, source_target_pairs={{0,12},{2,14},{4,8},{6,10},{8,4},{10,6},{12,0},{14,2},{1,13},{3,15... | collective-permute-start | bytes 393224 | tf_op jit(solution)/shard_map/ppermute | solution.py:334
  23.6 9.0 %collective-permute-start.9 = (f32[32,1024]{1,0:T(8,128)S(1)}, f32[32,1024]{1,0:T(8,128)S(1)}, u32[]{:S(2)}, u32[]{:S(2)}) collective-permute-start(f32[32,1024]{1,0:T(8,128)S(1)} %get-tuple-element.52), channel_id=1, source_target_pairs={{0,14},{2,12},{4,10},{6,8},{8,6},{10,4},{12,2},{14,0},{1,15},{3,13... | collective-permute-start | bytes 393224 | tf_op jit(solution)/shard_map/ppermute | solution.py:334
  27.0 10.5 %collective-permute-start.10 = (f32[32,1024]{1,0:T(8,128)S(1)}, f32[32,1024]{1,0:T(8,128)S(1)}, u32[]{:S(2)}, u32[]{:S(2)}) collective-permute-start(f32[32,1024]{1,0:T(8,128)S(1)} %get-tuple-element.53), channel_id=1, source_target_pairs={{0,2},{2,0},{4,6},{6,4},{8,10},{10,8},{12,14},{14,12},{1,3},{3,1},... | collective-permute-start | bytes 393224 | tf_op jit(solution)/shard_map/ppermute | solution.py:334
  39.5 33.6 %collective-permute-start.17 = (f32[4,128,384]{2,1,0:T(8,128)}, f32[4,128,384]{2,1,0:T(8,128)S(1)}, u32[]{:S(2)}, u32[]{:S(2)}) collective-permute-start(f32[4,128,384]{2,1,0:T(8,128)} %release.11), channel_id=1, source_target_pairs={{0,2},{2,0},{4,6},{6,4},{8,10},{10,8},{12,14},{14,12},{1,3},{3,1},... | collective-permute-start | bytes 2359304 | tf_op jit(solution)/shard_map/ppermute | solution.py:334
  40.1 7.8 %collective-permute-start.14 = (f32[32,1024]{1,0:T(8,128)S(1)}, f32[32,1024]{1,0:T(8,128)S(1)}, u32[]{:S(2)}, u32[]{:S(2)}) collective-permute-start(f32[32,1024]{1,0:T(8,128)S(1)} %get-tuple-element.59), channel_id=1, source_target_pairs={{0,8},{2,10},{4,12},{6,14},{8,0},{10,2},{12,4},{14,6},{1,9},{3,11}... | collective-permute-start | bytes 393224 | tf_op jit(solution)/shard_map/ppermute | solution.py:334
  44.0 9.2 %collective-permute-start.12 = (f32[32,1024]{1,0:T(8,128)S(1)}, f32[32,1024]{1,0:T(8,128)S(1)}, u32[]{:S(2)}, u32[]{:S(2)}) collective-permute-start(f32[32,1024]{1,0:T(8,128)S(1)} %release.8), channel_id=1, source_target_pairs={{0,4},{2,6},{4,0},{6,2},{8,12},{10,14},{12,8},{14,10},{1,5},{3,7},... | collective-permute-start | bytes 393224 | tf_op jit(solution)/shard_map/ppermute | solution.py:334
  44.5 11.4 %collective-permute-start.13 = (f32[32,1024]{1,0:T(8,128)S(1)}, f32[32,1024]{1,0:T(8,128)S(1)}, u32[]{:S(2)}, u32[]{:S(2)}) collective-permute-start(f32[32,1024]{1,0:T(8,128)S(1)} %release.9), channel_id=1, source_target_pairs={{0,6},{2,4},{4,2},{6,0},{8,14},{10,12},{12,10},{14,8},{1,7},{3,5},... | collective-permute-start | bytes 393224 | tf_op jit(solution)/shard_map/ppermute | solution.py:334
  46.5 9.3 %collective-permute-start.15 = (f32[32,1024]{1,0:T(8,128)S(1)}, f32[32,1024]{1,0:T(8,128)S(1)}, u32[]{:S(2)}, u32[]{:S(2)}) collective-permute-start(f32[32,1024]{1,0:T(8,128)S(1)} %release.10), channel_id=1, source_target_pairs={{0,10},{2,8},{4,14},{6,12},{8,2},{10,0},{12,6},{14,4},{1,11},{3,9}... | collective-permute-start | bytes 393224 | tf_op jit(solution)/shard_map/ppermute | solution.py:334
  59.0 8.3 %collective-permute-start.16 = (f32[32,1024]{1,0:T(8,128)S(1)}, f32[32,1024]{1,0:T(8,128)S(1)}, u32[]{:S(2)}, u32[]{:S(2)}) collective-permute-start(f32[32,1024]{1,0:T(8,128)S(1)} %get-tuple-element.61), channel_id=1, source_target_pairs={{0,12},{2,14},{4,8},{6,10},{8,4},{10,6},{12,0},{14,2},{1,13},{3,15... | collective-permute-start | bytes 393224 | tf_op jit(solution)/shard_map/ppermute | solution.py:334
  59.9 13.2 %collective-permute-start.18 = (f32[32,1024]{1,0:T(8,128)S(1)}, f32[32,1024]{1,0:T(8,128)S(1)}, u32[]{:S(2)}, u32[]{:S(2)}) collective-permute-start(f32[32,1024]{1,0:T(8,128)S(1)} %get-tuple-element.62), channel_id=1, source_target_pairs={{0,14},{2,12},{4,10},{6,8},{8,6},{10,4},{12,2},{14,0},{1,15},{3,13... | collective-permute-start | bytes 393224 | tf_op jit(solution)/shard_map/ppermute | solution.py:334
  63.2 10.0 %collective-permute-start.19 = (f32[32,1024]{1,0:T(8,128)S(1)}, f32[32,1024]{1,0:T(8,128)S(1)}, u32[]{:S(2)}, u32[]{:S(2)}) collective-permute-start(f32[32,1024]{1,0:T(8,128)S(1)} %get-tuple-element.63), channel_id=1, source_target_pairs={{0,2},{2,0},{4,6},{6,4},{8,10},{10,8},{12,14},{14,12},{1,3},{3,1},... | collective-permute-start | bytes 393224 | tf_op jit(solution)/shard_map/ppermute | solution.py:334
  64.4 14.4 %collective-permute-start.11 = (f32[2,128,384]{2,1,0:T(8,128)}, f32[2,128,384]{2,1,0:T(8,128)S(1)}, u32[]{:S(2)}, u32[]{:S(2)}) collective-permute-start(f32[2,128,384]{2,1,0:T(8,128)} %get-tuple-element.55.refs_2_.refs_1_), channel_id=1, source_target_pairs={{0,4},{2,6},{4,0},{6,2},{8,12},{10,14},{12,8},{14,10},{1,5},{3,7},... | collective-permute-start | bytes 1179656 | tf_op jit(solution)/shard_map/ppermute | solution.py:334
  75.3 20.1 %collective-permute-start.21 = (f32[2,128,384]{2,1,0:T(8,128)}, f32[2,128,384]{2,1,0:T(8,128)S(1)}, u32[]{:S(2)}, u32[]{:S(2)}) collective-permute-start(f32[2,128,384]{2,1,0:T(8,128)} %get-tuple-element.64.refs_2_), channel_id=1, source_target_pairs={{0,4},{2,6},{4,0},{6,2},{8,12},{10,14},{12,8},{14,10},{1,5},{3,7},... | collective-permute-start | bytes 1179656 | tf_op jit(solution)/shard_map/ppermute | solution.py:334
  78.0 24.7 %collective-permute-start.24 = (f32[4,128,256]{2,1,0:T(8,128)S(1)}, f32[4,128,256]{2,1,0:T(8,128)S(1)}, u32[]{:S(2)}, u32[]{:S(2)}) collective-permute-start(f32[4,128,256]{2,1,0:T(8,128)S(1)} %release.13), channel_id=1, source_target_pairs={{0,2},{2,0},{4,6},{6,4},{8,10},{10,8},{12,14},{14,12},{1,3},{3,1},... | collective-permute-start | bytes 1572872 | tf_op jit(solution)/shard_map/ppermute | solution.py:334
  78.7 16.7 %collective-permute-start.22 = (f32[32,1024]{1,0:T(8,128)S(1)}, f32[32,1024]{1,0:T(8,128)S(1)}, u32[]{:S(2)}, u32[]{:S(2)}) collective-permute-start(f32[32,1024]{1,0:T(8,128)S(1)} %release.12), channel_id=1, source_target_pairs={{0,4},{2,6},{4,0},{6,2},{8,12},{10,14},{12,8},{14,10},{1,5},{3,7},... | collective-permute-start | bytes 393224 | tf_op jit(solution)/shard_map/ppermute | solution.py:334
  80.6 22.1 %collective-permute-start.20 = (f32[1,128,384]{2,1,0:T(8,128)}, f32[1,128,384]{2,1,0:T(8,128)S(1)}, u32[]{:S(2)}, u32[]{:S(2)}) collective-permute-start(f32[1,128,384]{2,1,0:T(8,128)} %get-tuple-element.66.refs_3_), channel_id=1, source_target_pairs={{0,8},{2,10},{4,12},{6,14},{8,0},{10,2},{12,4},{14,6},{1,9},{3,11}... | collective-permute-start | bytes 589832 | tf_op jit(solution)/shard_map/ppermute | solution.py:334
  82.8 16.0 %collective-permute-start.25 = (f32[32,1024]{1,0:T(8,128)S(1)}, f32[32,1024]{1,0:T(8,128)S(1)}, u32[]{:S(2)}, u32[]{:S(2)}) collective-permute-start(f32[32,1024]{1,0:T(8,128)S(1)} %get-tuple-element.71), channel_id=1, source_target_pairs={{0,8},{2,10},{4,12},{6,14},{8,0},{10,2},{12,4},{14,6},{1,9},{3,11}... | collective-permute-start | bytes 393224 | tf_op jit(solution)/shard_map/ppermute | solution.py:334
  95.4 7.3 %collective-permute-start.26 = (f32[32,1024]{1,0:T(8,128)S(1)}, f32[32,1024]{1,0:T(8,128)S(1)}, u32[]{:S(2)}, u32[]{:S(2)}) collective-permute-start(f32[32,1024]{1,0:T(8,128)S(1)} %release.14), channel_id=1, source_target_pairs={{0,10},{2,8},{4,14},{6,12},{8,2},{10,0},{12,6},{14,4},{1,11},{3,9}... | collective-permute-start | bytes 393224 | tf_op jit(solution)/shard_map/ppermute | solution.py:334
  95.4 7.3 %collective-permute-start.27 = (f32[32,1024]{1,0:T(8,128)S(1)}, f32[32,1024]{1,0:T(8,128)S(1)}, u32[]{:S(2)}, u32[]{:S(2)}) collective-permute-start(f32[32,1024]{1,0:T(8,128)S(1)} %release.15), channel_id=1, source_target_pairs={{0,6},{2,4},{4,2},{6,0},{8,14},{10,12},{12,10},{14,8},{1,7},{3,5},... | collective-permute-start | bytes 393224 | tf_op jit(solution)/shard_map/ppermute | solution.py:334
  104.6 8.8 %collective-permute-start.28 = (f32[2,128,256]{2,1,0:T(8,128)}, f32[2,128,256]{2,1,0:T(8,128)S(1)}, u32[]{:S(2)}, u32[]{:S(2)}) collective-permute-start(f32[2,128,256]{2,1,0:T(8,128)} %get-tuple-element.75), channel_id=1, source_target_pairs={{0,4},{2,6},{4,0},{6,2},{8,12},{10,14},{12,8},{14,10},{1,5},{3,7},... | collective-permute-start | bytes 786440 | tf_op jit(solution)/shard_map/ppermute | solution.py:334
  105.1 6.9 %collective-permute-start.23 = (f32[1,128,384]{2,1,0:T(8,128)}, f32[1,128,384]{2,1,0:T(8,128)S(1)}, u32[]{:S(2)}, u32[]{:S(2)}) collective-permute-start(f32[1,128,384]{2,1,0:T(8,128)} %get-tuple-element.70.refs_2_), channel_id=1, source_target_pairs={{0,8},{2,10},{4,12},{6,14},{8,0},{10,2},{12,4},{14,6},{1,9},{3,11}... | collective-permute-start | bytes 589832 | tf_op jit(solution)/shard_map/ppermute | solution.py:334
  115.3 9.8 %collective-permute-start.29 = (f32[1,128,256]{2,1,0:T(8,128)}, f32[1,128,256]{2,1,0:T(8,128)S(1)}, u32[]{:S(2)}, u32[]{:S(2)}) collective-permute-start(f32[1,128,256]{2,1,0:T(8,128)} %get-tuple-element.77.refs_8_), channel_id=1, source_target_pairs={{0,8},{2,10},{4,12},{6,14},{8,0},{10,2},{12,4},{14,6},{1,9},{3,11}... | collective-permute-start | bytes 393224 | tf_op jit(solution)/shard_map/ppermute | solution.py:334
  (9 other events, 79.3 us)
